TPU v7x, 32 devices: a whole 2x2x4 slice. The times are simulated.
32 devices in a mesh: ctx: 8 (over y, x, core), fsdp: 4 (over z).
Axes of the slice: x: 2, y: 2, z: 4, core: 2. Of those that a mesh axis runs over, the one named last changes fastest.
Arguments:
- query_in: bfloat16 [4, 1024, 2048], P('fsdp', 'ctx'), may hold values from -6 to 6
- key_in: bfloat16 [4, 1024, 2048], P('fsdp', 'ctx'), may hold values from -6 to 6
- value_in: bfloat16 [4, 1024, 2048], P('fsdp', 'ctx'), may hold values from -6 to 6
- feature_taps: float32 [3, 3, 2048], replicated, may hold values from -3 to 3
- decay_rate: float32 [128, 16], replicated, as said below
- residues: float32 [128, 16], replicated, may hold values from -3 to 3
- skip_gain: float32 [2048], replicated, may hold values from 0.5 to 1.5
- out_weight: bfloat16 [2048, 2048], P('fsdp'), may hold values from -0.1875 to 0.1875
Outputs:
- block_out: bfloat16 [4, 1024, 2048], P('fsdp', 'ctx')
Inputs may be any that keep to these rules, and one draw needn't show every extreme that they name: `decay_rate`: every rate is positive.
All inputs are finite; a program needn't handle non-finite values.
Results may differ from a plain program's by a relative error of at most 0.0062.
Values may be sent and summed in bfloat16 or wider, within the bound.
No kernel may reach another device: no remote copies, remote signals or barrier semaphores. Data moves between devices by JAX's collectives and lax.ppermute only.
A program may use at most 128 MiB of HBM per device.

v0:
```python
import math

import jax
import jax.numpy as jnp
from jax import lax
from jax.sharding import PartitionSpec as P

GROUP = 16
FEAT = 3


exact_precision = lax.Precision.HIGHEST
split_precision = lax.Precision.HIGH


def shifted(shard, axis, by):
    count = lax.axis_size(axis)
    pairs = [(i, i + by) for i in range(count) if 0 <= i + by < count]
    return lax.ppermute(shard, axis, pairs)


def featurize(rows, tail, taps_one):
    values = jnp.concatenate([tail, rows], axis=0).astype(jnp.float32)
    count = rows.shape[0]
    total = taps_one[0] * values[FEAT - 1 :]
    for offset in range(1, FEAT):
        total = total + taps_one[offset] * values[FEAT - 1 - offset : FEAT - 1 - offset + count]
    return total


def mode_tables(rate_rows, residue_rows, width):
    positions = jnp.arange(width).astype(jnp.float32)
    scale = residue_rows * jnp.sqrt(-jnp.expm1(-2.0 * rate_rows))
    powers = jnp.exp(-rate_rows[:, :, None] * positions)
    kernel = jnp.einsum("gm,gmt->gt", scale, powers, precision=exact_precision)
    lagged = jnp.exp(-rate_rows[:, :, None] * (positions + 1.0)) * scale[:, :, None]
    closing = jnp.exp(-rate_rows[:, :, None] * (width - 1.0 - positions))
    return (kernel, lagged, closing)


def lower_toeplitz(kernel):
    groups_here, width = kernel.shape
    extended = jnp.concatenate([jnp.zeros((groups_here, width), jnp.float32), kernel], axis=1)
    reversed_ext = extended[:, ::-1]
    tiled = jnp.tile(reversed_ext, (1, width))[:, : width * (2 * width - 1)]
    framed = tiled.reshape(groups_here, width, 2 * width - 1)
    return framed[:, :, width - 1 : 2 * width - 1]


def block_terms(operands):
    signal, kernel, closing = operands
    toeplitz = lower_toeplitz(kernel)
    inner = jnp.einsum("gij,gcbj->gcbi", toeplitz, signal, precision=split_precision)
    ending = jnp.einsum("gcbj,gmj->gcbm", signal, closing, precision=split_precision)
    return (inner, ending)


def spanned_terms(signal, kernel, closing):
    groups_here = signal.shape[0]
    width = signal.shape[-1]
    per_span = math.gcd(groups_here, max(1, (1 << 20) // (width * width)))
    outer = groups_here // per_span

    def reshape_front(array):
        return array.reshape((outer, per_span) + array.shape[1:])

    inner, ending = lax.map(
        block_terms, (reshape_front(signal), reshape_front(kernel), reshape_front(closing))
    )
    return (inner.reshape(signal.shape), ending.reshape((groups_here,) + ending.shape[2:]))


def channel_conv(signal, rate_rows, residue_rows):
    chans_here, length = signal.shape
    width = min(128, length)
    blocks = length // width
    groups_here = chans_here // GROUP
    values = signal.astype(jnp.float32).reshape(groups_here, GROUP, blocks, width)
    kernel, lagged, closing = mode_tables(rate_rows, residue_rows, width)
    inner, ending = spanned_terms(values, kernel, closing)
    factor = jnp.broadcast_to(jnp.exp(-rate_rows * width)[:, None, None, :], ending.shape)

    def combine(earlier, later):
        return (earlier[0] * later[0], earlier[1] * later[0] + later[1])

    through = lax.associative_scan(combine, (factor, ending), axis=2)[1]
    entering = jnp.concatenate([jnp.zeros_like(through[:, :, :1]), through[:, :, :-1]], axis=2)
    crossing = jnp.einsum("gcbm,gmi->gcbi", entering, lagged, precision=split_precision)
    return (inner + crossing).reshape(chans_here, length)


def local(query_in, key_in, value_in, feature_taps, decay_rate, residues, skip_gain, out_weight):
    query_rows = query_in[0]
    key_rows = key_in[0]
    value_rows = value_in[0]
    rows_here = query_rows.shape[0]
    keep = FEAT - 1
    tails = shifted(
        (
            query_rows[rows_here - keep :],
            key_rows[rows_here - keep :],
            value_rows[rows_here - keep :],
        ),
        "ctx",
        1,
    )
    featured_q = featurize(query_rows, tails[0], feature_taps[0])
    featured_k = featurize(key_rows, tails[1], feature_taps[1])
    featured_v = featurize(value_rows, tails[2], feature_taps[2])
    kv_round = lax.optimization_barrier((featured_k * featured_v).astype(jnp.bfloat16))
    spread = lax.all_to_all(jnp.transpose(kv_round), "ctx", split_axis=0, concat_axis=1, tiled=True)
    groups_here = spread.shape[0] // GROUP
    first_group = lax.axis_index("ctx") * groups_here
    rate_rows = lax.dynamic_slice_in_dim(decay_rate, first_group, groups_here, 0)
    residue_rows = lax.dynamic_slice_in_dim(residues, first_group, groups_here, 0)
    filtered = channel_conv(spread, rate_rows, residue_rows).astype(jnp.bfloat16)
    convolved = jnp.transpose(
        lax.all_to_all(filtered, "ctx", split_axis=1, concat_axis=0, tiled=True)
    )
    convolved = lax.optimization_barrier(convolved)
    gated = (
        featured_q * (convolved.astype(jnp.float32) + skip_gain * kv_round.astype(jnp.float32))
    ).astype(jnp.bfloat16)
    block_out = jnp.dot(
        gated,
        lax.all_gather(out_weight, "fsdp", axis=0, tiled=True),
        preferred_element_type=jnp.float32,
    ).astype(jnp.bfloat16)
    return block_out[None]


def solution(mesh):
    return jax.shard_map(
        local,
        mesh=mesh,
        in_specs=(
            P("fsdp", "ctx", None),
            P("fsdp", "ctx", None),
            P("fsdp", "ctx", None),
            P(),
            P(),
            P(),
            P(),
            P("fsdp", None),
        ),
        out_specs=P("fsdp", "ctx", None),
        check_vma=False,
    )
```

profile of v0, /device:TPU:0, one launch (start us, length us, event | category | flops | bytes accessed | tf_op | source)
XLA Modules:
  0.0 173.9 jit_solution(10942134035882569238)
XLA Ops:
  6.5 0.0 all-gather.2.cloned.1.call-start
  6.6 0.7 all-gather.2.cloned.1.call-update
  7.3 0.3 copy-done.3
  7.6 2.4 %collective-permute-start.1 = (bf16[2,2048]{1,0:T(2,128)(2,1)S(1)}, bf16[2,2048]{1,0:T(2,128)(2,1)S(1)}, u32[]{:S(2)}, u32[]{:S(2)}) collective-permute-start(bf16[2,2048]{1,0:T(2,128)(2,1)S(1)} %slice_bitcast_fusion.3), channel_id=1, source_target_pairs={{0,4},{4,8},{8,12},{12,16},{16,20},{20,24},{24,28},{1,5},{5,9},{9,... | collective-permute-start | bytes 24584 | tf_op jit(solution)/shard_map/ppermute | solution.py:19
  10.0 4.5 %collective-permute-start.2 = (bf16[2,2048]{1,0:T(2,128)(2,1)S(1)}, bf16[2,2048]{1,0:T(2,128)(2,1)S(1)}, u32[]{:S(2)}, u32[]{:S(2)}) collective-permute-start(bf16[2,2048]{1,0:T(2,128)(2,1)S(1)} %slice_bitcast_fusion.2), channel_id=1, source_target_pairs={{0,4},{4,8},{8,12},{12,16},{16,20},{20,24},{24,28},{1,5},{5,9},{9,... | collective-permute-start | bytes 24584 | tf_op jit(solution)/shard_map/ppermute | solution.py:19
  14.5 0.0 copy-done.7
  14.5 0.0 copy-done.8
  14.5 0.1 multiply_multiply_fusion
  14.6 0.1 fusion.42
  14.7 0.0 collective-permute-done.1
  14.7 0.1 maximum_convert_fusion.1
  14.9 0.4 collective-permute-done.2
  15.3 0.1 maximum_convert_fusion.2
  15.5 0.7 fusion.5
  16.1 0.0 copy-start.1
  16.2 1.0 copy.27
  17.2 4.4 %all-to-all-start = ((bf16[8,256,128]{2,1,0:T(8,128)(2,1)}), bf16[8,256,128]{2,1,0:T(8,128)(2,1)S(1)}, u32[]{:S(2)}, u32[]{:S(2)}) async-start(bf16[8,256,128]{2,1,0:T(8,128)(2,1)} %bitcast.16), calls=%async_computation | async-start | bytes 1048576 | tf_op jit(solution)/shard_map/all_to_all | solution.py:111
  21.6 0.1 copy.29
  21.6 0.1 copy.30
  21.7 0.1 copy.31
  21.8 0.1 copy.32
  21.8 0.1 copy.35
  21.9 0.1 copy.38
  22.0 0.3 fusion.29
  22.3 0.2 rev.4
  22.5 0.2 tile.14
  22.7 1.2 copy.43
  23.9 0.1 slice.214
  24.1 4.6 %reshape.65 = f32[16,128,255]{2,1,0:T(8,128)} reshape(f32[16,32640]{1,0:T(8,128)S(1)} %slice.214) | data formatting | bytes 4177920 | tf_op jit(solution)/shard_map/while/body/eval_jaxpr/reshape | solution.py:46
  28.7 2.6 %all-to-all-done = bf16[8,256,128]{2,1,0:T(8,128)(2,1)S(1)} async-done(((bf16[8,256,128]{2,1,0:T(8,128)(2,1)}), bf16[8,256,128]{2,1,0:T(8,128)(2,1)S(1)}, u32[]{:S(2)}, u32[]{:S(2)}) %all-to-all-start) | async-done | bytes 524320 | tf_op jit(solution)/shard_map/all_to_all | solution.py:111
  31.3 0.3 copy.28
  31.7 0.5 fusion.22
  32.2 0.5 slice.188
  32.7 0.6 slice.190
  33.3 0.2 multiply_add_fusion
  33.5 0.6 slice.192
  34.2 0.6 slice.194
  34.8 5.1 %slice.203 = f32[16,16,3,16]{3,2,1,0:T(4,128)} slice(f32[16,16,8,16]{3,2,1,0:T(8,128)S(1)} %fusion.22), slice={[0:16:1], [0:16:1], [2:8:2], [0:16:1]} | slice | bytes 98304 | tf_op jit(solution)/shard_map/slice | solution.py:86
  39.9 0.2 multiply_add_fusion.1
  40.1 0.2 slice_add_fusion.1
  40.3 0.4 fusion.41
  40.8 0.3 pad_maximum_fusion.1
  41.1 3.4 %pad.23 = f32[16,16,4,16]{3,2,1,0:T(4,128)S(1)} pad(f32[16,16,2,16]{3,2,1,0:T(2,128)S(1)} %pad_maximum_fusion.1, f32[]{:T(128)} %constant.17.clone.1), padding=0_0_0x0_0_0x0_1_1x0_0_0 | pad | bytes 98308 | tf_op jit(solution)/shard_map/pad | solution.py:86
  44.5 0.3 pad_add_fusion
  44.7 3.4 %pad.24 = f32[16,16,4,16]{3,2,1,0:T(4,128)S(1)} pad(f32[16,16,2,16]{3,2,1,0:T(2,128)S(1)} %pad_add_fusion, f32[]{:T(128)} %constant.17.clone.1), padding=0_0_0x0_0_0x1_0_1x0_0_0 | pad | bytes 98308 | tf_op jit(solution)/shard_map/pad | solution.py:86
  48.1 0.2 add.92
  48.3 2.2 %pad.62 = f32[16,16,8,16]{3,2,1,0:T(8,128)S(1)} pad(f32[16,16,4,16]{3,2,1,0:T(4,128)S(1)} %add.92, f32[]{:T(128)} %constant.17.clone.1), padding=0_0_0x0_0_0x1_0_1x0_0_0 | pad | bytes 196612
  50.5 0.0 slice-start
  50.5 1.3 fusion.15
  51.9 0.3 pad_maximum_fusion
  52.2 2.2 %pad.38 = f32[16,16,7,16]{3,2,1,0:T(8,128)S(1)} pad(f32[16,16,4,16]{3,2,1,0:T(4,128)S(1)} %pad_maximum_fusion, f32[]{:T(128)} %constant.17.clone.1), padding=0_0_0x0_0_0x0_0_1x0_0_0 | pad | bytes 180228 | tf_op jit(solution)/shard_map/slice | solution.py:87
  54.4 2.5 %fusion.2 = f32[16,16,8,128]{3,2,1,0:T(8,128)S(1)} fusion(bf16[16,16,8,128]{3,2,1,0:T(8,128)(2,1)S(1)} %bitcast.56, f32[16,128,255]{2,1,0:T(8,128)} %reshape.65), kind=kOutput, calls=%fused_computation.5 | convolution fusion | flops 201326592 | bytes 2621440 | tf_op jit(solution)/shard_map/while/body/eval_jaxpr/gij,gcbj->gcbi/dot_general | solution.py:53
  56.9 0.1 slice_add_fusion.2
  57.1 0.7 fusion.1
  57.8 0.0 copy-start.5
  57.8 0.9 copy.36
  58.8 3.5 %all-to-all-start.1 = ((bf16[256,8,128]{2,0,1:T(8,128)(2,1)}), bf16[256,8,128]{2,0,1:T(8,128)(2,1)S(1)}, u32[]{:S(2)}, u32[]{:S(2)}) async-start(bf16[256,8,128]{2,0,1:T(8,128)(2,1)} %copy.36), calls=%async_computation.1 | async-start | bytes 1048576 | tf_op jit(solution)/shard_map/all_to_all | solution.py:118
  62.3 2.3 %collective-permute-start = (bf16[2,2048]{1,0:T(2,128)(2,1)S(1)}, bf16[2,2048]{1,0:T(2,128)(2,1)S(1)}, u32[]{:S(2)}, u32[]{:S(2)}) collective-permute-start(bf16[2,2048]{1,0:T(2,128)(2,1)S(1)} %slice_bitcast_fusion.4), channel_id=1, source_target_pairs={{0,4},{4,8},{8,12},{12,16},{16,20},{20,24},{24,28},{1,5},{5,9},{9,... | collective-permute-start | bytes 24584 | tf_op jit(solution)/shard_map/ppermute | solution.py:19
  64.6 0.8 collective-permute-done
  65.4 0.1 maximum_convert_fusion
  65.6 6.4 %all-to-all-done.1 = bf16[256,8,128]{2,0,1:T(8,128)(2,1)S(1)} async-done(((bf16[256,8,128]{2,0,1:T(8,128)(2,1)}), bf16[256,8,128]{2,0,1:T(8,128)(2,1)S(1)}, u32[]{:S(2)}, u32[]{:S(2)}) %all-to-all-start.1) | async-done | bytes 524320 | tf_op jit(solution)/shard_map/all_to_all | solution.py:118
  71.9 0.2 copy.37
  72.2 89.2 %all-gather.2.cloned.1.call-done = bf16[2048,2048]{1,0:T(8,128)(2,1)} async-done(((bf16[512,2048]{1,0:T(8,128)(2,1)}), bf16[2048,2048]{1,0:T(8,128)(2,1)}) %all-gather.2.cloned.1.call-update) | async-done | bytes 8388624 | tf_op jit(solution)/shard_map/all_gather | solution.py:126
  161.3 5.7 %fusion = bf16[1,128,2048]{2,1,0:T(8,128)(2,1)} fusion(bf16[2048,2048]{1,0:T(8,128)(2,1)} %all-gather.2.cloned.1.call-done, f32[130,2048]{1,0:T(8,128)S(1)} %maximum_convert_fusion, bf16[128,2048]{1,0:T(8,128)(2,1)S(1)} %copy-done.2, bf16[128,2048]{1,0:T(8,128)(2,1)S(1)} %bitcast.64, f32[2048]{0:T(1024)S(1)} %copy-done.9, f32[2048]{0:T(1024)S(1)} %bitcast.73, ...), kind=kOutput, calls=%fused_computation.1 | convolution fusion | flops 1076887552 | bytes 13139968 | tf_op jit(solution)/shard_map/dot_general | solution.py:124
  (24 shorter events, 0.1 us)
Async XLA Ops:
  6.5 1.0 copy-start.3
  6.5 3.4 %copy-start.4 = (bf16[1,128,2048]{2,1,0:T(8,128)(2,1)S(1)}, bf16[1,128,2048]{2,1,0:T(8,128)(2,1)}, u32[]{:S(2)}) copy-start(bf16[1,128,2048]{2,1,0:T(8,128)(2,1)} %param.10) | copy-start | bytes 1572868
  6.5 8.0 %copy-start.7 = (f32[128,16]{0,1:T(8,128)S(1)}, f32[128,16]{0,1:T(8,128)}, u32[]{:S(2)}) copy-start(f32[128,16]{0,1:T(8,128)} %param.12) | copy-start | bytes 24580
  6.5 8.0 %copy-start.8 = (f32[128,16]{0,1:T(8,128)S(1)}, f32[128,16]{0,1:T(8,128)}, u32[]{:S(2)}) copy-start(f32[128,16]{0,1:T(8,128)} %param.13) | copy-start | bytes 24580
  6.5 8.1 %copy-start.6 = (f32[3,3,2048]{2,1,0:T(4,128)S(1)}, f32[3,3,2048]{2,1,0:T(4,128)}, u32[]{:S(2)}) copy-start(f32[3,3,2048]{2,1,0:T(4,128)} %param.11) | copy-start | bytes 221188
  6.5 154.8 %all-gather.2.cloned.1.call-start = ((), (), s32[]{:S(2)}) async-start(), calls=%async_computation.2 | async-start | bytes 10485760 | tf_op jit(solution)/shard_map/all_gather | solution.py:126
  7.6 7.1 %collective-permute-start.1 = (bf16[2,2048]{1,0:T(2,128)(2,1)S(1)}, bf16[2,2048]{1,0:T(2,128)(2,1)S(1)}, u32[]{:S(2)}, u32[]{:S(2)}) collective-permute-start(bf16[2,2048]{1,0:T(2,128)(2,1)S(1)} %slice_bitcast_fusion.3), channel_id=1, source_target_pairs={{0,4},{4,8},{8,12},{12,16},{16,20},{20,24},{24,28},{1,5},{5,9},{9,... | collective-permute-start | bytes 24584 | tf_op jit(solution)/shard_map/ppermute | solution.py:19
  10.0 5.3 %collective-permute-start.2 = (bf16[2,2048]{1,0:T(2,128)(2,1)S(1)}, bf16[2,2048]{1,0:T(2,128)(2,1)S(1)}, u32[]{:S(2)}, u32[]{:S(2)}) collective-permute-start(bf16[2,2048]{1,0:T(2,128)(2,1)S(1)} %slice_bitcast_fusion.2), channel_id=1, source_target_pairs={{0,4},{4,8},{8,12},{12,16},{16,20},{20,24},{24,28},{1,5},{5,9},{9,... | collective-permute-start | bytes 24584 | tf_op jit(solution)/shard_map/ppermute | solution.py:19
  16.1 6.2 %copy-start.1 = (bf16[128,2048]{1,0:T(8,128)(2,1)}, bf16[128,2048]{1,0:T(8,128)(2,1)S(1)}, u32[]{:S(2)}) copy-start(bf16[128,2048]{1,0:T(8,128)(2,1)S(1)} %fusion.5) | copy-start | bytes 1572868
  17.2 14.1 %all-to-all-start = ((bf16[8,256,128]{2,1,0:T(8,128)(2,1)}), bf16[8,256,128]{2,1,0:T(8,128)(2,1)S(1)}, u32[]{:S(2)}, u32[]{:S(2)}) async-start(bf16[8,256,128]{2,1,0:T(8,128)(2,1)} %bitcast.16), calls=%async_computation | async-start | bytes 1048576 | tf_op jit(solution)/shard_map/all_to_all | solution.py:111
  32.2 7.8 %copy-start = (f32[16,16,8,16]{3,2,1,0:T(8,128)}, f32[16,16,8,16]{3,2,1,0:T(8,128)S(1)}, u32[]{:S(2)}) copy-start(f32[16,16,8,16]{3,2,1,0:T(8,128)S(1)} %fusion.22) | copy-start | bytes 393220
  50.5 1.3 slice-start
  57.8 4.5 %copy-start.5 = (bf16[1,128,2048]{2,1,0:T(8,128)(2,1)S(1)}, bf16[1,128,2048]{2,1,0:T(8,128)(2,1)}, u32[]{:S(2)}) copy-start(bf16[1,128,2048]{2,1,0:T(8,128)(2,1)} %param.8) | copy-start | bytes 1572868
  58.8 13.2 %all-to-all-start.1 = ((bf16[256,8,128]{2,0,1:T(8,128)(2,1)}), bf16[256,8,128]{2,0,1:T(8,128)(2,1)S(1)}, u32[]{:S(2)}, u32[]{:S(2)}) async-start(bf16[256,8,128]{2,0,1:T(8,128)(2,1)} %copy.36), calls=%async_computation.1 | async-start | bytes 1048576 | tf_op jit(solution)/shard_map/all_to_all | solution.py:118
  62.3 3.1 %collective-permute-start = (bf16[2,2048]{1,0:T(2,128)(2,1)S(1)}, bf16[2,2048]{1,0:T(2,128)(2,1)S(1)}, u32[]{:S(2)}, u32[]{:S(2)}) collective-permute-start(bf16[2,2048]{1,0:T(2,128)(2,1)S(1)} %slice_bitcast_fusion.4), channel_id=1, source_target_pairs={{0,4},{4,8},{8,12},{12,16},{16,20},{20,24},{24,28},{1,5},{5,9},{9,... | collective-permute-start | bytes 24584 | tf_op jit(solution)/shard_map/ppermute | solution.py:19
  65.4 95.9 %copy-start.2 = (bf16[128,2048]{1,0:T(8,128)(2,1)S(1)}, bf16[128,2048]{1,0:T(8,128)(2,1)}, u32[]{:S(2)}) copy-start(bf16[128,2048]{1,0:T(8,128)(2,1)} %copy-done.1) | copy-start | bytes 1572868
  65.4 95.9 %copy-start.9 = (f32[2048]{0:T(1024)S(1)}, f32[2048]{0:T(1024)}, u32[]{:S(2)}) copy-start(f32[2048]{0:T(1024)} %param.14) | copy-start | bytes 24580
Sparse Core Ops, SparseCore 0:
  9.0 152.3 all-gather.1
where the time goes:
time: 174 us
  waiting for transfers between devices  100 us (57%)
  local copies, waits for them, and re-layouts  28.5 us (16%)
  starting transfers between devices  17.1 us (10%)
  between operations  13.8 us (8%)
  matrix products  9.79 us (6%)
  other arithmetic  4.65 us (3%)
    all_gather x1, waiting for transfers between devices, local(): lax.all_gather(out_weight, 'fsdp', axis=0, tiled=True)  89.2 us
    ppermute x3, starting transfers between devices, shifted(): return lax.ppermute(shard, axis, pairs)  9.16 us
    slice x7, local copies, waits for them, and re-layouts, channel_conv(): through = lax.associative_scan(combine, (factor, ending), axis=2)[1]  7.56 us
    pad x2, local copies, waits for them, and re-layouts, channel_conv(): through = lax.associative_scan(combine, (factor, ending), axis=2)[1]  6.82 us
    all_to_all x1, waiting for transfers between devices, local(): lax.all_to_all(filtered, 'ctx', split_axis=1, concat_axis=0, tiled=True)  6.37 us
    dot_general x1, matrix products, local(): jnp.dot(gated, lax.all_gather(out_weight, 'fsdp', axis=0, tiled=True), pr...  5.73 us
    reshape x1, local copies, waits for them, and re-layouts, lower_toeplitz(): framed = tiled.reshape(groups_here, width, 2 * width - 1)  4.65 us
    all_to_all x1, starting transfers between devices, local(): lax.all_to_all(jnp.transpose(kv_round), 'ctx', split_axis=0, concat_axis=...  4.38 us
  transfers between devices with their start and end apart: 6, of which 5 were waited for; matrix products, arithmetic and copies ran while one was open for 21% of the time, Pallas kernels for 0%

commit v1 on v0

v1 whole, which is shorter than its diff:
```python
import functools

import jax
import jax.numpy as jnp
from jax import lax
from jax.experimental import pallas as pl
from jax.experimental.pallas import tpu as pltpu
from jax.sharding import PartitionSpec as P

GROUP = 16
FEAT = 3
WIDE = 256
VMEM_LIMIT = 48 << 20

bf16 = jnp.bfloat16
f32 = jnp.float32


def after(x, *deps):
    return lax.optimization_barrier((x,) + deps)[0]


def params():
    return pltpu.CompilerParams(vmem_limit_bytes=VMEM_LIMIT)


def split(x):
    high = x.astype(bf16)
    return high, (x - high.astype(f32)).astype(bf16)


def iota(shape, dim):
    return lax.broadcasted_iota(jnp.int32, shape, dim)


def dot(a, b):
    return jnp.dot(a, b, preferred_element_type=f32)


def featurize(rows, tail, taps):
    values = rows.astype(f32)
    at = iota(values.shape, 0)
    one = jnp.where(at == 0, tail[1:2], pltpu.roll(values, 1, 0))
    two = jnp.where(at == 0, tail[0:1], jnp.where(at == 1, tail[1:2], pltpu.roll(values, 2, 0)))
    return taps[0:1] * values + taps[1:2] * one + taps[2:3] * two


def closing_kernel(rate_ref, scale_ref, out_ref):
    rows = out_ref.shape[1] // 2
    back = (rows - 1 - iota((rows, WIDE), 0)).astype(f32)
    table = jnp.exp(-rate_ref[0] * back) * scale_ref[0]
    high, low = split(table.T)
    out_ref[:, :rows] = high
    out_ref[:, rows:] = low


def product_kernel(key_ref, value_ref, halo_ref, taps_ref, closing_ref, kv_ref, state_ref):
    halo = halo_ref[...]
    key = featurize(key_ref[...], halo[2:4], taps_ref[1])
    value = featurize(value_ref[...], halo[4:6], taps_ref[2])
    kv = (key * value).astype(bf16)
    kv_ref[...] = kv
    ends = dot(closing_ref[...], jnp.concatenate([kv, kv], axis=0))
    modes = state_ref.shape[0]
    owner = iota((modes, WIDE), 1) // GROUP
    total = jnp.zeros((modes, WIDE), f32)
    for g in range(WIDE // GROUP):
        total = jnp.where(owner == g, ends[g * modes : (g + 1) * modes], total)
    state_ref[...] = total


def inner_kernel(rate_ref, scale_ref, kv_ref, out_ref):
    rows = kv_ref.shape[0]
    groups, modes = rate_ref.shape
    at = iota((groups, rows), 1)
    lag = jnp.where(at == 0, 0, rows - at).astype(f32)
    taps = jnp.zeros((groups, rows), f32)
    for n in range(modes):
        taps = taps + scale_ref[:, n : n + 1] * jnp.exp(-rate_ref[:, n : n + 1] * lag)
    kv = kv_ref[...]
    twice = jnp.concatenate([kv, kv], axis=0)
    causal = iota((rows, rows), 0) >= iota((rows, rows), 1)
    owner = iota((rows, WIDE), 1) // GROUP
    total = jnp.zeros((rows, WIDE), f32)
    for g in range(groups):
        band = jnp.broadcast_to(taps[g : g + 1], (rows, rows))
        band = pltpu.roll(band, 0, 1, stride=1, stride_axis=0)
        high, low = split(jnp.where(causal, band, 0.0))
        part = dot(jnp.concatenate([high, low], axis=1), twice)
        total = jnp.where(owner == g, part, total)
    out_ref[...] = total


def gate_kernel(query_ref, halo_ref, taps_ref, kv_ref, inner_ref, enter_ref, rate_ref, skip_ref, out_ref):
    rows = query_ref.shape[0]
    query = featurize(query_ref[...], halo_ref[0:2], taps_ref[0])
    ahead = (iota((rows, WIDE), 0) + 1).astype(f32)
    lag_high, lag_low = split(jnp.exp(-rate_ref[0] * ahead))
    enter = enter_ref[...]
    modes = enter.shape[0]
    spread = jnp.concatenate([enter] * (WIDE // modes), axis=0)
    same = iota((WIDE, WIDE), 0) // modes == iota((WIDE, WIDE), 1) // GROUP
    in_high, in_low = split(jnp.where(same, spread, 0.0))
    cross = dot(lag_high, in_high) + dot(lag_low, in_high) + dot(lag_high, in_low)
    convolved = (inner_ref[...] + cross).astype(bf16).astype(f32)
    kv = kv_ref[...].astype(f32)
    out_ref[...] = (query * (convolved + skip_ref[...] * kv)).astype(bf16)


def wide(rows):
    return pl.BlockSpec((rows, WIDE), lambda b: (0, b))


def conv_path(query, key, value, taps, rate, residues, skip):
    rows, chans = query.shape
    modes = rate.shape[1]
    blocks = chans // WIDE
    count = lax.axis_size("ctx")
    index = lax.axis_index("ctx")
    scale = residues * jnp.sqrt(-jnp.expm1(-2.0 * rate))
    rate_row = rate.reshape(blocks, 1, WIDE)
    scale_row = scale.reshape(blocks, 1, WIDE)
    keep = FEAT - 1
    tails = jnp.concatenate(
        [query[rows - keep :], key[rows - keep :], value[rows - keep :], query[rows - keep :]]
    ).astype(f32)
    halo = lax.ppermute(tails, "ctx", [(i, i + 1) for i in range(count - 1)])
    row_spec = pl.BlockSpec((1, 1, WIDE), lambda b: (b, 0, 0))
    taps_spec = pl.BlockSpec((3, FEAT, WIDE), lambda b: (0, 0, b))
    mode_spec = pl.BlockSpec((WIDE // GROUP, modes), lambda b: (b, 0))
    closing = pl.pallas_call(
        closing_kernel,
        grid=(blocks,),
        in_specs=[row_spec, row_spec],
        out_specs=pl.BlockSpec((WIDE, 2 * rows), lambda b: (b, 0)),
        out_shape=jax.ShapeDtypeStruct((blocks * WIDE, 2 * rows), bf16),
        compiler_params=params(),
        name="closing_table",
    )(rate_row, scale_row)
    kv, state = pl.pallas_call(
        product_kernel,
        grid=(blocks,),
        in_specs=[
            wide(rows),
            wide(rows),
            wide(8),
            taps_spec,
            pl.BlockSpec((WIDE, 2 * rows), lambda b: (b, 0)),
        ],
        out_specs=[wide(rows), wide(modes)],
        out_shape=[
            jax.ShapeDtypeStruct((rows, chans), bf16),
            jax.ShapeDtypeStruct((modes, chans), f32),
        ],
        compiler_params=params(),
        name="kv_and_state",
    )(key, value, halo, taps, closing)
    inner = pl.pallas_call(
        inner_kernel,
        grid=(blocks,),
        in_specs=[mode_spec, mode_spec, wide(rows)],
        out_specs=wide(rows),
        out_shape=jax.ShapeDtypeStruct((rows, chans), f32),
        compiler_params=params(),
        name="inner_conv",
    )(rate, scale, kv)
    rate_chan = jnp.repeat(rate.T, GROUP, axis=1)
    enter = jnp.zeros_like(state)
    step = 1
    while step < count:
        other = lax.ppermute(state, "ctx", [(i, i ^ step) for i in range(count)])
        upper = (index // step) % 2 == 1
        within = (index % step * rows).astype(f32)
        enter = jnp.where(upper, enter + jnp.exp(-rate_chan * within) * other, enter)
        fade = jnp.exp(-rate_chan * float(step * rows))
        state = jnp.where(upper, other * fade + state, state * fade + other)
        step *= 2
    return pl.pallas_call(
        gate_kernel,
        grid=(blocks,),
        in_specs=[
            wide(rows),
            wide(8),
            taps_spec,
            wide(rows),
            wide(rows),
            wide(modes),
            row_spec,
            wide(1),
        ],
        out_specs=wide(rows),
        out_shape=jax.ShapeDtypeStruct((rows, chans), bf16),
        compiler_params=params(),
        name="gate",
    )(query, halo, taps, kv, inner, enter, rate_row, skip[None])


def hop(x, first):
    count = lax.axis_size("ctx")
    even, odd = (2, 4) if first else (4, 2)
    return lax.ppermute(x, "ctx", [(i, i ^ (odd if i % 2 else even)) for i in range(count)])


def gather_weight(weight):
    index = lax.axis_index("ctx")
    place = lax.axis_index("fsdp")
    depth, cols = weight.shape
    block = cols // 8
    inward = [(1, 2), (2, 1)]
    outward = [(1, 0), (2, 3)]
    middle = (place == 1) | (place == 2)
    mine = lax.dynamic_slice(weight, (0, (index % 8) * block), (depth, block))
    near = lax.ppermute(mine, "fsdp", [(i, i ^ 1) for i in range(4)])
    across = lax.ppermute(mine, "fsdp", inward)
    far = lax.ppermute(mine, "fsdp", [(0, 2), (3, 1)])
    slots = []
    one_a, one_b = hop(near, True), hop(near, False)
    out_two = lax.ppermute(across, "fsdp", outward)
    one_c = hop(one_a, False)
    slots.append((near, one_a, one_b, one_c))
    two = jnp.where(middle, across, after(out_two, one_a))
    two_a, two_b = hop(two, True), hop(two, False)
    out_three = lax.ppermute(after(far, out_two), "fsdp", outward)
    two_c = hop(two_a, False)
    slots.append((two, two_a, two_b, two_c))
    three = jnp.where(middle, far, after(out_three, two_a, one_c))
    three_a, three_b = hop(three, True), hop(three, False)
    three_c = hop(after(three_a, two_c, two_b), False)
    slots.append((three, three_a, three_b, three_c))
    return slots


def matmul_kernel(slot_count, has_own, has_acc, last, nums_ref, *refs):
    refs = list(refs)
    mine_ref, other_ref = refs[0], refs[1]
    refs = refs[2:]
    if has_own:
        weight_ref = refs.pop(0)
    slots = [refs[4 * s : 4 * s + 4] for s in range(slot_count)]
    refs = refs[4 * slot_count :]
    if has_acc:
        acc_ref = refs.pop(0)
    rows = mine_ref.shape[0]
    depth, block = slots[0][0].shape

    def rows_of(part):
        at = pl.multiple_of(nums_ref[part] * depth, depth)
        return jnp.concatenate(
            [mine_ref[:, pl.ds(at, depth)], other_ref[:, pl.ds(at, depth)]], axis=0
        )

    lhs = [rows_of(1 + s) for s in range(slot_count)]
    if has_own:
        own = rows_of(0)
    for r in range(4):
        total = acc_ref[:, r * block : (r + 1) * block] if has_acc else None
        if has_own:
            at = pl.multiple_of(nums_ref[4 + r] * block, block)
            total = dot(own, weight_ref[:, pl.ds(at, block)])
        for s in range(slot_count):
            part = dot(lhs[s], slots[s][r][...])
            total = part if total is None else total + part
        if last:
            at = pl.multiple_of(nums_ref[8 + r] * block, block)
            done = total.astype(bf16)
            refs[0][:, pl.ds(at, block)] = done[:rows]
            refs[1][:, pl.ds(at, block)] = done[rows:]
        else:
            refs[0][:, r * block : (r + 1) * block] = total


def join_kernel(nums_ref, mine_ref, other_ref, out_ref):
    block = mine_ref.shape[1] // 4
    core = nums_ref[0]
    for h in range(4):
        at = pl.multiple_of((2 * h + core) * block, block)
        out_ref[:, pl.ds(at, block)] = mine_ref[:, h * block : (h + 1) * block]
        at = pl.multiple_of((2 * h + 1 - core) * block, block)
        out_ref[:, pl.ds(at, block)] = other_ref[:, h * block : (h + 1) * block]


def project(gated, weight, slots):
    count = lax.axis_size("ctx")
    index = lax.axis_index("ctx")
    place = lax.axis_index("fsdp")
    rows = gated.shape[0]
    depth, cols = weight.shape
    half = cols // 2
    swap = [(i, i ^ 1) for i in range(count)]
    other = lax.ppermute(gated, "ctx", swap)
    core = index % 2
    first, second = jnp.where(core == 0, 2, 4), jnp.where(core == 0, 4, 2)
    rel = index % 8
    order = [rel, rel ^ first, rel ^ second, rel ^ 6]
    parts = [
        place,
        place ^ 1,
        jnp.where(place <= 1, 2, 1),
        jnp.where(place <= 1, 3, 0),
    ]
    nums = jnp.stack(parts + order + [n // 2 for n in order]).astype(jnp.int32)
    vmem = pl.BlockSpec(memory_space=pltpu.VMEM)
    smem = pl.BlockSpec(memory_space=pltpu.SMEM)
    acc = pl.pallas_call(
        functools.partial(matmul_kernel, 2, True, False, False),
        in_specs=[smem] + [vmem] * 11,
        out_specs=vmem,
        out_shape=jax.ShapeDtypeStruct((2 * rows, half), f32),
        compiler_params=params(),
        name="project_near",
    )(nums, gated, other, weight, *slots[0], *slots[1])
    late = nums.at[1].set(nums[3])
    mine, theirs = pl.pallas_call(
        functools.partial(matmul_kernel, 1, False, True, True),
        in_specs=[smem] + [vmem] * 7,
        out_specs=[vmem, vmem],
        out_shape=[jax.ShapeDtypeStruct((rows, half), bf16)] * 2,
        compiler_params=params(),
        name="project_far",
    )(late, gated, other, *slots[2], acc)
    back = lax.ppermute(theirs, "ctx", swap)
    return pl.pallas_call(
        join_kernel,
        in_specs=[smem, vmem, vmem],
        out_specs=vmem,
        out_shape=jax.ShapeDtypeStruct((rows, cols), bf16),
        compiler_params=params(),
        name="join_columns",
    )(core[None].astype(jnp.int32), mine, back)


def local(query_in, key_in, value_in, feature_taps, decay_rate, residues, skip_gain, out_weight):
    gated = conv_path(
        query_in[0], key_in[0], value_in[0], feature_taps, decay_rate, residues, skip_gain
    )
    return project(gated, out_weight, gather_weight(out_weight))[None]


def solution(mesh):
    return jax.shard_map(
        local,
        mesh=mesh,
        in_specs=(
            P("fsdp", "ctx", None),
            P("fsdp", "ctx", None),
            P("fsdp", "ctx", None),
            P(),
            P(),
            P(),
            P(),
            P("fsdp", None),
        ),
        out_specs=P("fsdp", "ctx", None),
        check_vma=False,
    )
```

time: 174 us -> 78.4 us (0.45)
  waiting for transfers between devices: 100 us -> 18.5 us
  local copies, waits for them, and re-layouts: 28.5 us -> 10.9 us
  Pallas kernels: 0 us -> 17.3 us
  between operations: 13.8 us -> 0.35 us
  starting transfers between devices: 17.1 us -> 29.6 us
  matrix products: 9.79 us -> 0 us
  other arithmetic: 4.65 us -> 0.98 us
    all_gather x1 -> x0, waiting for transfers between devices: 89.2 us -> none  [local(): lax.all_gather(out_weight, 'fsdp', axis=0, tiled=True)]
    ppermute x3 -> x20, starting transfers between devices: 9.16 us -> 29.6 us  [the longest x9 9.96 us: hop(): lax.ppermute(x, 'ctx', [(i, i ^ (odd if i % 2 else even)) for i in range(...]
    pallas_call x0 -> x7, Pallas kernels: none -> 17.3 us  [the longest x1 6.17 us: conv_path(): pl.pallas_call(inner_kernel, grid=(blocks,), in_specs=[mode_spec, mode_sp...]
    ppermute x3 -> x20, waiting for transfers between devices: 1.25 us -> 18.5 us  [the longest x9 12.9 us: hop(): lax.ppermute(x, 'ctx', [(i, i ^ (odd if i % 2 else even)) for i in range(...]
    dot_general x5 -> x0, matrix products: 9.79 us -> none  [the longest x1 5.73 us: local(): jnp.dot(gated, lax.all_gather(out_weight, 'fsdp', axis=0, tiled=True), pr...]
    all_to_all x2 -> x0, waiting for transfers between devices: 8.97 us -> none  [the longest x1 6.37 us: local(): lax.all_to_all(filtered, 'ctx', split_axis=1, concat_axis=0, tiled=True)]
    slice x13 -> x2, local copies, waits for them, and re-layouts: 10 us -> 1.66 us  [the longest x1 0.86 us: conv_path(): query[rows - keep:]]
    all_to_all x2 -> x0, starting transfers between devices: 7.87 us -> none  [the longest x1 4.38 us: local(): lax.all_to_all(jnp.transpose(kv_round), 'ctx', split_axis=0, concat_axis=...]
  transfers between devices with their start and end apart: 6 -> 20, of which waited for: 5 -> 10; matrix products, arithmetic and copies ran while one was open for 21% -> 12% of each run, Pallas kernels for 0% -> 16%
where the time goes in v1:
time: 78.4 us; the launch traced here: 77.6 us
  starting transfers between devices  29.6 us (38%)
  waiting for transfers between devices  18.5 us (24%)
  Pallas kernels  17.3 us (22%)
  local copies, waits for them, and re-layouts  10.9 us (14%)
  other arithmetic  0.98 us (1%)
    ppermute x9, waiting for transfers between devices, hop(): lax.ppermute(x, 'ctx', [(i, i ^ (odd if i % 2 else even)) for i in range(...  12.9 us
    ppermute x9, starting transfers between devices, hop(): lax.ppermute(x, 'ctx', [(i, i ^ (odd if i % 2 else even)) for i in range(...  9.96 us
    pallas_call x1, Pallas kernels, conv_path(): pl.pallas_call(inner_kernel, grid=(blocks,), in_specs=[mode_spec, mode_sp...  6.17 us
    ppermute x3, starting transfers between devices, conv_path(): other = lax.ppermute(state, 'ctx', [(i, i ^ step) for i in range(count)])  5.8 us
    ppermute x1, starting transfers between devices, gather_weight(): far = lax.ppermute(mine, 'fsdp', [(0, 2), (3, 1)])  5.74 us
    ppermute x1, waiting for transfers between devices, gather_weight(): out_two = lax.ppermute(across, 'fsdp', outward)  3.25 us
    pallas_call x1, Pallas kernels, project(): pl.pallas_call(functools.partial(matmul_kernel, 2, True, False, False), i...  2.59 us
    pallas_call x1, Pallas kernels, conv_path(): pl.pallas_call(gate_kernel, grid=(blocks,), in_specs=[wide(rows), wide(8)...  2.57 us
  transfers between devices with their start and end apart: 20, of which 10 were waited for; matrix products, arithmetic and copies ran while one was open for 12% of the time, Pallas kernels for 16%

profile of v1, /device:TPU:0, one launch (start us, length us, event | category | flops | bytes accessed | tf_op | source)
XLA Modules:
  0.0 77.6 jit_solution(16575895807024629016)
XLA Ops:
  0.0 0.9 %slice_bitcast_fusion.2 = bf16[2,2048]{1,0:T(2,128)(2,1)S(1)} fusion(bf16[1,128,2048]{2,1,0:T(8,128)(2,1)} %param.10), kind=kLoop, calls=%fused_computation.16 | loop fusion | bytes 16384 | tf_op jit(solution)/shard_map/slice | solution.py:125
  0.9 0.8 %slice_bitcast_fusion = (bf16[2,2048]{1,0:T(2,128)(2,1)S(1)}, bf16[2,2048]{1,0:T(2,128)(2,1)S(1)}) fusion(bf16[1,128,2048]{2,1,0:T(8,128)(2,1)} %param.12, bf16[1,128,2048]{2,1,0:T(8,128)(2,1)} %param.11), kind=kLoop, calls=%fused_computation.14 | loop fusion | bytes 32768 | tf_op jit(solution)/shard_map/slice | solution.py:125
  1.7 2.4 %collective-permute-start = (f32[8,2048]{1,0:T(8,128)S(1)}, f32[8,2048]{1,0:T(8,128)S(1)}, u32[]{:S(2)}, u32[]{:S(2)}) collective-permute-start(f32[8,2048]{1,0:T(8,128)S(1)} %maximum_convert_fusion), channel_id=1, source_target_pairs={{0,4},{4,8},{8,12},{12,16},{16,20},{20,24},{24,28},{1,5},{5,9},{9,... | collective-permute-start | bytes 196616 | tf_op jit(solution)/shard_map/ppermute | solution.py:127
  4.1 0.7 exponential_bitcast_fusion.4
  4.8 0.1 copy.24
  4.9 0.8 %copy.25 = f32[128,16]{1,0:T(8,128)S(1)} copy(f32[128,16]{0,1:T(8,128)} %param.15) | data formatting | bytes 16384 | tf_op args[5]
  5.8 0.8 %copy.23.rate_ref = f32[128,16]{1,0:T(8,128)S(1)} copy(f32[128,16]{0,1:T(8,128)} %param.14) | data formatting | bytes 16384 | tf_op args[4]
  6.6 0.1 reshape.52.scale_ref
  6.6 0.1 reshape.51.rate_ref
  6.7 1.0 %closing_table.1.closing_ref = bf16[2048,256]{1,0:T(8,128)(2,1)S(1)} custom-call(f32[8,1,256]{2,1,0:T(1,128)S(1)} %reshape.51.rate_ref, f32[8,1,256]{2,1,0:T(1,128)S(1)} %reshape.52.scale_ref), custom_call_target="tpu_custom_call" | custom-call | tf_op jit(solution)/shard_map/closing_table/pallas_call | solution.py:131
  7.8 0.0 collective-permute-done.halo_ref
  7.8 0.0 copy-start.3
  7.8 0.9 %copy-done.3 = f32[3,3,2048]{2,1,0:T(4,128)S(1)} copy-done((f32[3,3,2048]{2,1,0:T(4,128)S(1)}, f32[3,3,2048]{2,1,0:T(4,128)}, u32[]{:S(2)}) %copy-start.3) | copy-done | bytes 73752
  8.7 2.5 %kv_and_state.1 = (bf16[128,2048]{1,0:T(8,128)(2,1)S(1)}, f32[16,2048]{1,0:T(8,128)S(1)}) custom-call(bf16[128,2048]{1,0:T(8,128)(2,1)S(1)} %bitcast.35, bf16[128,2048]{1,0:T(8,128)(2,1)S(1)} %bitcast.34, f32[8,2048]{1,0:T(8,128)S(1)} %collective-permute-done.halo_ref, f32[3,3,2048]{2,1,0:T(4,128)S(1)} %copy-done.3, ...), custom_call_target="tpu_custom_call" | custom-call | tf_op jit(solution)/shard_map/kv_and_state/pallas_call | solution.py:140
  11.3 2.7 %collective-permute-start.1 = (f32[16,2048]{1,0:T(8,128)S(1)}, f32[16,2048]{1,0:T(8,128)S(1)}, u32[]{:S(2)}, u32[]{:S(2)}) collective-permute-start(f32[16,2048]{1,0:T(8,128)S(1)} %get-tuple-element.26), channel_id=1, source_target_pairs={{0,4},{4,0},{8,12},{12,8},{16,20},{20,16},{24,28},{28,24},{1,5},{5... | collective-permute-start | bytes 393224 | tf_op jit(solution)/shard_map/ppermute | solution.py:171
  13.9 1.0 %constant_dynamic-slice_fusion = bf16[512,256]{1,0:T(8,128)(2,1)S(1)} fusion(bf16[512,2048]{1,0:T(8,128)(2,1)} %refs_2_.1, s32[]{:T(128)S(6)} %select_n.131), kind=kLoop, calls=%fused_computation.18 | loop fusion | bytes 524292 | tf_op jit(solution)/shard_map/dynamic_slice | solution.py:212
  14.9 1.6 %collective-permute-start.9 = (bf16[512,256]{1,0:T(8,128)(2,1)S(1)}, bf16[512,256]{1,0:T(8,128)(2,1)S(1)}, u32[]{:S(2)}, u32[]{:S(2)}) collective-permute-start(bf16[512,256]{1,0:T(8,128)(2,1)S(1)} %constant_dynamic-slice_fusion), channel_id=1, source_target_pairs={{0,1},{1,0},{2,3},{3,2},{4,5},{5,4},{6,7},{7,6},{8,9},{9,8},{10,11... | collective-permute-start | bytes 786440 | tf_op jit(solution)/shard_map/ppermute | solution.py:213
  16.5 1.4 %collective-permute-start.6 = (bf16[512,256]{1,0:T(8,128)(2,1)S(1)}, bf16[512,256]{1,0:T(8,128)(2,1)}, u32[]{:S(2)}, u32[]{:S(2)}) collective-permute-start(bf16[512,256]{1,0:T(8,128)(2,1)S(1)} %constant_dynamic-slice_fusion), channel_id=1, source_target_pairs={{1,2},{2,1},{5,6},{6,5},{9,10},{10,9},{13,14},{14,13},{17,18},{18,... | collective-permute-start | bytes 786440 | tf_op jit(solution)/shard_map/ppermute | solution.py:214
  17.9 0.3 broadcast_in_dim.24
  18.2 0.6 exp.58
  18.9 0.0 collective-permute-done.1
  18.9 1.6 %collective-permute-start.2 = (f32[16,2048]{1,0:T(8,128)S(1)}, f32[16,2048]{1,0:T(8,128)S(1)}, u32[]{:S(2)}, u32[]{:S(2)}) collective-permute-start(f32[16,2048]{1,0:T(8,128)S(1)} %add_select_fusion.3), channel_id=1, source_target_pairs={{0,8},{4,12},{8,0},{12,4},{16,24},{20,28},{24,16},{28,20},{1,9},{5... | collective-permute-start | bytes 393224 | tf_op jit(solution)/shard_map/ppermute | solution.py:171
  20.5 5.7 %collective-permute-start.5 = (bf16[512,256]{1,0:T(8,128)(2,1)S(1)}, bf16[512,256]{1,0:T(8,128)(2,1)}, u32[]{:S(2)}, u32[]{:S(2)}) collective-permute-start(bf16[512,256]{1,0:T(8,128)(2,1)S(1)} %constant_dynamic-slice_fusion), channel_id=1, source_target_pairs={{0,2},{3,1},{4,6},{7,5},{8,10},{11,9},{12,14},{15,13},{16,18},{19,... | collective-permute-start | bytes 786440 | tf_op jit(solution)/shard_map/ppermute | solution.py:215
  26.2 0.3 broadcast_in_dim.26
  26.5 0.6 exp.64
  27.2 0.3 broadcast_in_dim.22
  27.5 0.6 exp.52
  28.1 0.3 broadcast_in_dim.23
  28.5 0.6 exp.55
  29.1 0.3 broadcast_in_dim.25
  29.4 1.3 %exp.61 = f32[16,2048]{1,0:T(8,128)} reshape(f32[16,128,16]{2,1,0:T(8,128)S(1)} %broadcast_in_dim.25) | data formatting | bytes 262144 | tf_op jit(solution)/shard_map/exp | solution.py:174
  30.7 6.2 %inner_conv.1.inner_ref = f32[128,2048]{1,0:T(8,128)S(1)} custom-call(f32[128,16]{1,0:T(8,128)S(1)} %copy.23.rate_ref, f32[128,16]{1,0:T(8,128)S(1)} %sqrt_multiply_fusion.scale_ref, bf16[128,2048]{1,0:T(8,128)(2,1)S(1)} %get-tuple-element.25.kv_ref), custom_call_target="tpu_custom_call" | custom-call | tf_op jit(solution)/shard_map/inner_conv/pallas_call | solution.py:158
  36.9 0.0 collective-permute-done.9.refs_3_
  36.9 0.6 collective-permute-start.10
  37.5 1.3 %collective-permute-start.7 = (bf16[512,256]{1,0:T(8,128)(2,1)}, bf16[512,256]{1,0:T(8,128)(2,1)S(1)}, u32[]{:S(2)}, u32[]{:S(2)}) collective-permute-start(bf16[512,256]{1,0:T(8,128)(2,1)} %collective-permute-done.6), channel_id=1, source_target_pairs={{1,0},{2,3},{5,4},{6,7},{9,8},{10,11},{13,12},{14,15},{17,16},{18,... | collective-permute-start | bytes 786440 | tf_op jit(solution)/shard_map/ppermute | solution.py:218
  38.9 1.6 %collective-permute-start.3 = (f32[16,2048]{1,0:T(8,128)S(1)}, f32[16,2048]{1,0:T(8,128)S(1)}, u32[]{:S(2)}, u32[]{:S(2)}) collective-permute-start(f32[16,2048]{1,0:T(8,128)S(1)} %add_select_fusion.2), channel_id=1, source_target_pairs={{0,16},{4,20},{8,24},{12,28},{16,0},{20,4},{24,8},{28,12},{1,17},{... | collective-permute-start | bytes 393224 | tf_op jit(solution)/shard_map/ppermute | solution.py:171
  40.5 2.9 %collective-permute-done.10.refs_4_ = bf16[512,256]{1,0:T(8,128)(2,1)S(1)} collective-permute-done((bf16[512,256]{1,0:T(8,128)(2,1)S(1)}, bf16[512,256]{1,0:T(8,128)(2,1)S(1)}, u32[]{:S(2)}, u32[]{:S(2)}) %collective-permute-start.10) | collective-permute-done | bytes 262176 | tf_op jit(solution)/shard_map/ppermute | solution.py:201
  43.4 3.3 %collective-permute-done.7 = bf16[512,256]{1,0:T(8,128)(2,1)S(1)} collective-permute-done((bf16[512,256]{1,0:T(8,128)(2,1)}, bf16[512,256]{1,0:T(8,128)(2,1)S(1)}, u32[]{:S(2)}, u32[]{:S(2)}) %collective-permute-start.7) | collective-permute-done | bytes 262176 | tf_op jit(solution)/shard_map/ppermute | solution.py:218
  46.7 1.7 %collective-permute-start.11 = (bf16[512,256]{1,0:T(8,128)(2,1)S(1)}, bf16[512,256]{1,0:T(8,128)(2,1)S(1)}, u32[]{:S(2)}, u32[]{:S(2)}) collective-permute-start(bf16[512,256]{1,0:T(8,128)(2,1)S(1)} %broadcast_select_fusion.1.refs_7_), channel_id=1, source_target_pairs={{0,8},{4,20},{8,0},{12,28},{16,24},{20,4},{24,16},{28,12},{1,9},{5... | collective-permute-start | bytes 786440 | tf_op jit(solution)/shard_map/ppermute | solution.py:201
  48.4 0.0 collective-permute-done.5
  48.4 1.3 %collective-permute-start.8 = (bf16[512,256]{1,0:T(8,128)(2,1)}, bf16[512,256]{1,0:T(8,128)(2,1)S(1)}, u32[]{:S(2)}, u32[]{:S(2)}) collective-permute-start(bf16[512,256]{1,0:T(8,128)(2,1)} %collective-permute-done.5), channel_id=1, source_target_pairs={{1,0},{2,3},{5,4},{6,7},{9,8},{10,11},{13,12},{14,15},{17,16},{18,... | collective-permute-start | bytes 786440 | tf_op jit(solution)/shard_map/ppermute | solution.py:223
  49.7 0.6 collective-permute-start.12
  50.2 0.1 add_select_fusion.enter_ref
  50.3 2.6 %gate.1.refs_0_ = bf16[128,2048]{1,0:T(8,128)(2,1)S(1)} custom-call(bf16[128,2048]{1,0:T(8,128)(2,1)S(1)} %bitcast.36, f32[8,2048]{1,0:T(8,128)S(1)} %collective-permute-done.halo_ref, f32[3,3,2048]{2,1,0:T(4,128)S(1)} %copy-done.4, bf16[128,2048]{1,0:T(8,128)(2,1)S(1)} %get-tuple-element.25.kv_ref, f32[128,2048]{1,0:T(8,128)S(1)} %inner_conv.1.inner_ref, ...), custom_call_target="tpu_custom_call" | custom-call | tf_op jit(solution)/shard_map/gate/pallas_call | solution.py:178
  52.9 0.1 collective-permute-start.4
  53.0 1.6 %collective-permute-start.16 = (bf16[512,256]{1,0:T(8,128)(2,1)S(1)}, bf16[512,256]{1,0:T(8,128)(2,1)S(1)}, u32[]{:S(2)}, u32[]{:S(2)}) collective-permute-start(bf16[512,256]{1,0:T(8,128)(2,1)S(1)} %broadcast_select_fusion.1.refs_7_), channel_id=1, source_target_pairs={{0,16},{4,12},{8,24},{12,4},{16,0},{20,28},{24,8},{28,20},{1,17},{... | collective-permute-start | bytes 786440 | tf_op jit(solution)/shard_map/ppermute | solution.py:201
  54.6 1.0 %collective-permute-done.11.refs_8_ = bf16[512,256]{1,0:T(8,128)(2,1)S(1)} collective-permute-done((bf16[512,256]{1,0:T(8,128)(2,1)S(1)}, bf16[512,256]{1,0:T(8,128)(2,1)S(1)}, u32[]{:S(2)}, u32[]{:S(2)}) %collective-permute-start.11) | collective-permute-done | bytes 262176 | tf_op jit(solution)/shard_map/ppermute | solution.py:201
  55.6 0.5 collective-permute-done.12.refs_6_
  56.1 0.7 collective-permute-done.8
  56.8 0.5 collective-permute-start.15
  57.4 1.6 %collective-permute-start.13 = (bf16[512,256]{1,0:T(8,128)(2,1)S(1)}, bf16[512,256]{1,0:T(8,128)(2,1)}, u32[]{:S(2)}, u32[]{:S(2)}) collective-permute-start(bf16[512,256]{1,0:T(8,128)(2,1)S(1)} %broadcast_select_fusion.refs_2_), channel_id=1, source_target_pairs={{0,8},{4,20},{8,0},{12,28},{16,24},{20,4},{24,16},{28,12},{1,9},{5... | collective-permute-start | bytes 786440 | tf_op jit(solution)/shard_map/ppermute | solution.py:201
  58.9 0.6 collective-permute-start.18
  59.5 1.0 %collective-permute-done.16.refs_9_ = bf16[512,256]{1,0:T(8,128)(2,1)S(1)} collective-permute-done((bf16[512,256]{1,0:T(8,128)(2,1)S(1)}, bf16[512,256]{1,0:T(8,128)(2,1)S(1)}, u32[]{:S(2)}, u32[]{:S(2)}) %collective-permute-start.16) | collective-permute-done | bytes 262176 | tf_op jit(solution)/shard_map/ppermute | solution.py:201
  60.5 1.3 %collective-permute-start.14 = (bf16[512,256]{1,0:T(8,128)(2,1)S(1)}, bf16[512,256]{1,0:T(8,128)(2,1)}, u32[]{:S(2)}, u32[]{:S(2)}) collective-permute-start(bf16[512,256]{1,0:T(8,128)(2,1)S(1)} %broadcast_select_fusion.refs_2_), channel_id=1, source_target_pairs={{0,16},{4,12},{8,24},{12,4},{16,0},{20,28},{24,8},{28,20},{1,17},{... | collective-permute-start | bytes 786440 | tf_op jit(solution)/shard_map/ppermute | solution.py:201
  61.8 3.2 %collective-permute-done.15.refs_10_ = bf16[512,256]{1,0:T(8,128)(2,1)S(1)} collective-permute-done((bf16[512,256]{1,0:T(8,128)(2,1)S(1)}, bf16[512,256]{1,0:T(8,128)(2,1)S(1)}, u32[]{:S(2)}, u32[]{:S(2)}) %collective-permute-start.15) | collective-permute-done | bytes 262176 | tf_op jit(solution)/shard_map/ppermute | solution.py:201
  65.0 1.8 %collective-permute-done.13.refs_3_ = bf16[512,256]{1,0:T(8,128)(2,1)} collective-permute-done((bf16[512,256]{1,0:T(8,128)(2,1)S(1)}, bf16[512,256]{1,0:T(8,128)(2,1)}, u32[]{:S(2)}, u32[]{:S(2)}) %collective-permute-start.13) | collective-permute-done | bytes 262176 | tf_op jit(solution)/shard_map/ppermute | solution.py:201
  66.8 1.5 %collective-permute-start.17 = (bf16[512,256]{1,0:T(8,128)(2,1)}, bf16[512,256]{1,0:T(8,128)(2,1)}, u32[]{:S(2)}, u32[]{:S(2)}) collective-permute-start(bf16[512,256]{1,0:T(8,128)(2,1)} %collective-permute-done.13.refs_3_), channel_id=1, source_target_pairs={{0,16},{4,12},{8,24},{12,4},{16,0},{20,28},{24,8},{28,20},{1,17},{... | collective-permute-start | bytes 786440 | tf_op jit(solution)/shard_map/ppermute | solution.py:201
  68.3 0.1 stack.51.nums_ref
  68.4 2.6 %project_near.1.refs_6_ = f32[256,1024]{1,0:T(8,128)S(1)} custom-call(s32[12]{0:T(128)S(1)} %stack.51.nums_ref, bf16[128,2048]{1,0:T(8,128)(2,1)S(1)} %gate.1.refs_0_, bf16[128,2048]{1,0:T(8,128)(2,1)S(1)} %collective-permute-done.4.refs_1_, bf16[512,2048]{1,0:T(8,128)(2,1)} %refs_2_.1, bf16[512,256]{1,0:T(8,128)(2,1)S(1)} %collective-permute-done.9.refs_3_, ...), custom_call_target="tpu_custom_call" | custom-call | tf_op jit(solution)/shard_map/project_near/pallas_call | solution.py:304
  71.1 2.5 %collective-permute-done.17.refs_5_ = bf16[512,256]{1,0:T(8,128)(2,1)} collective-permute-done((bf16[512,256]{1,0:T(8,128)(2,1)}, bf16[512,256]{1,0:T(8,128)(2,1)}, u32[]{:S(2)}, u32[]{:S(2)}) %collective-permute-start.17) | collective-permute-done | bytes 262176 | tf_op jit(solution)/shard_map/ppermute | solution.py:201
  73.6 1.6 %project_far.1 = (bf16[128,1024]{1,0:T(8,128)(2,1)S(1)}, bf16[128,1024]{1,0:T(8,128)(2,1)S(1)}) custom-call(s32[12]{0:T(128)S(1)} %constant_dynamic-update-slice_fusion.nums_ref, bf16[128,2048]{1,0:T(8,128)(2,1)S(1)} %gate.1.refs_0_, bf16[128,2048]{1,0:T(8,128)(2,1)S(1)} %collective-permute-done.4.refs_1_, ...), custom_call_target="tpu_custom_call" | custom-call | tf_op jit(solution)/shard_map/project_far/pallas_call | solution.py:313
  75.2 0.1 collective-permute-start.19
  75.2 1.5 %collective-permute-done.19.other_ref = bf16[128,1024]{1,0:T(8,128)(2,1)S(1)} collective-permute-done((bf16[128,1024]{1,0:T(8,128)(2,1)S(1)}, bf16[128,1024]{1,0:T(8,128)(2,1)S(1)}, u32[]{:S(2)}, u32[]{:S(2)}) %collective-permute-start.19) | collective-permute-done | bytes 262176 | tf_op jit(solution)/shard_map/ppermute | solution.py:321
  76.8 0.9 %join_columns.1 = bf16[128,2048]{1,0:T(8,128)(2,1)} custom-call(s32[1]{0:T(128)} %bitcast.nums_ref, bf16[128,1024]{1,0:T(8,128)(2,1)S(1)} %get-tuple-element.31.mine_ref, bf16[128,1024]{1,0:T(8,128)(2,1)S(1)} %collective-permute-done.19.other_ref), custom_call_target="tpu_custom_call" | custom-call | tf_op jit(solution)/shard_map/join_columns/pallas_call | solution.py:322
  (25 shorter events, 0.3 us)
Async XLA Ops:
  0.0 7.8 %copy-start.1 = (bf16[1,128,2048]{2,1,0:T(8,128)(2,1)S(1)}, bf16[1,128,2048]{2,1,0:T(8,128)(2,1)}, u32[]{:S(2)}) copy-start(bf16[1,128,2048]{2,1,0:T(8,128)(2,1)} %param.11) | copy-start | bytes 1572868
  0.0 7.8 %copy-start = (bf16[1,128,2048]{2,1,0:T(8,128)(2,1)S(1)}, bf16[1,128,2048]{2,1,0:T(8,128)(2,1)}, u32[]{:S(2)}) copy-start(bf16[1,128,2048]{2,1,0:T(8,128)(2,1)} %param.12) | copy-start | bytes 1572868
  1.7 6.1 %collective-permute-start = (f32[8,2048]{1,0:T(8,128)S(1)}, f32[8,2048]{1,0:T(8,128)S(1)}, u32[]{:S(2)}, u32[]{:S(2)}) collective-permute-start(f32[8,2048]{1,0:T(8,128)S(1)} %maximum_convert_fusion), channel_id=1, source_target_pairs={{0,4},{4,8},{8,12},{12,16},{16,20},{20,24},{24,28},{1,5},{5,9},{9,... | collective-permute-start | bytes 196616 | tf_op jit(solution)/shard_map/ppermute | solution.py:127
  7.8 0.9 %copy-start.3 = (f32[3,3,2048]{2,1,0:T(4,128)S(1)}, f32[3,3,2048]{2,1,0:T(4,128)}, u32[]{:S(2)}) copy-start(f32[3,3,2048]{2,1,0:T(4,128)} %taps_ref.3) | copy-start | bytes 221188
  11.3 7.6 %collective-permute-start.1 = (f32[16,2048]{1,0:T(8,128)S(1)}, f32[16,2048]{1,0:T(8,128)S(1)}, u32[]{:S(2)}, u32[]{:S(2)}) collective-permute-start(f32[16,2048]{1,0:T(8,128)S(1)} %get-tuple-element.26), channel_id=1, source_target_pairs={{0,4},{4,0},{8,12},{12,8},{16,20},{20,16},{24,28},{28,24},{1,5},{5... | collective-permute-start | bytes 393224 | tf_op jit(solution)/shard_map/ppermute | solution.py:171
  14.9 22.0 %collective-permute-start.9 = (bf16[512,256]{1,0:T(8,128)(2,1)S(1)}, bf16[512,256]{1,0:T(8,128)(2,1)S(1)}, u32[]{:S(2)}, u32[]{:S(2)}) collective-permute-start(bf16[512,256]{1,0:T(8,128)(2,1)S(1)} %constant_dynamic-slice_fusion), channel_id=1, source_target_pairs={{0,1},{1,0},{2,3},{3,2},{4,5},{5,4},{6,7},{7,6},{8,9},{9,8},{10,11... | collective-permute-start | bytes 786440 | tf_op jit(solution)/shard_map/ppermute | solution.py:213
  16.5 21.0 %collective-permute-start.6 = (bf16[512,256]{1,0:T(8,128)(2,1)S(1)}, bf16[512,256]{1,0:T(8,128)(2,1)}, u32[]{:S(2)}, u32[]{:S(2)}) collective-permute-start(bf16[512,256]{1,0:T(8,128)(2,1)S(1)} %constant_dynamic-slice_fusion), channel_id=1, source_target_pairs={{1,2},{2,1},{5,6},{6,5},{9,10},{10,9},{13,14},{14,13},{17,18},{18,... | collective-permute-start | bytes 786440 | tf_op jit(solution)/shard_map/ppermute | solution.py:214
  18.9 19.9 %collective-permute-start.2 = (f32[16,2048]{1,0:T(8,128)S(1)}, f32[16,2048]{1,0:T(8,128)S(1)}, u32[]{:S(2)}, u32[]{:S(2)}) collective-permute-start(f32[16,2048]{1,0:T(8,128)S(1)} %add_select_fusion.3), channel_id=1, source_target_pairs={{0,8},{4,12},{8,0},{12,4},{16,24},{20,28},{24,16},{28,20},{1,9},{5... | collective-permute-start | bytes 393224 | tf_op jit(solution)/shard_map/ppermute | solution.py:171
  20.5 27.9 %collective-permute-start.5 = (bf16[512,256]{1,0:T(8,128)(2,1)S(1)}, bf16[512,256]{1,0:T(8,128)(2,1)}, u32[]{:S(2)}, u32[]{:S(2)}) collective-permute-start(bf16[512,256]{1,0:T(8,128)(2,1)S(1)} %constant_dynamic-slice_fusion), channel_id=1, source_target_pairs={{0,2},{3,1},{4,6},{7,5},{8,10},{11,9},{12,14},{15,13},{16,18},{19,... | collective-permute-start | bytes 786440 | tf_op jit(solution)/shard_map/ppermute | solution.py:215
  30.7 19.5 %copy-start.6 = (f32[16,2048]{1,0:T(8,128)S(1)}, f32[16,2048]{1,0:T(8,128)}, u32[]{:S(2)}) copy-start(f32[16,2048]{1,0:T(8,128)} %exp.61) | copy-start | bytes 393220
  30.7 19.6 %copy-start.2 = (bf16[1,128,2048]{2,1,0:T(8,128)(2,1)S(1)}, bf16[1,128,2048]{2,1,0:T(8,128)(2,1)}, u32[]{:S(2)}) copy-start(bf16[1,128,2048]{2,1,0:T(8,128)(2,1)} %param.10) | copy-start | bytes 1572868
  30.7 19.6 %copy-start.4 = (f32[3,3,2048]{2,1,0:T(4,128)S(1)}, f32[3,3,2048]{2,1,0:T(4,128)}, u32[]{:S(2)}) copy-start(f32[3,3,2048]{2,1,0:T(4,128)} %taps_ref.3) | copy-start | bytes 221188
  30.7 19.6 %copy-start.5 = (f32[2048]{0:T(1024)S(1)}, f32[2048]{0:T(1024)}, u32[]{:S(2)}) copy-start(f32[2048]{0:T(1024)} %param.16) | copy-start | bytes 24580
  36.9 6.4 %collective-permute-start.10 = (bf16[512,256]{1,0:T(8,128)(2,1)S(1)}, bf16[512,256]{1,0:T(8,128)(2,1)S(1)}, u32[]{:S(2)}, u32[]{:S(2)}) collective-permute-start(bf16[512,256]{1,0:T(8,128)(2,1)S(1)} %collective-permute-done.9.refs_3_), channel_id=1, source_target_pairs={{0,8},{4,20},{8,0},{12,28},{16,24},{20,4},{24,16},{28,12},{1,9},{5... | collective-permute-start | bytes 786440 | tf_op jit(solution)/shard_map/ppermute | solution.py:201
  37.5 9.1 %collective-permute-start.7 = (bf16[512,256]{1,0:T(8,128)(2,1)}, bf16[512,256]{1,0:T(8,128)(2,1)S(1)}, u32[]{:S(2)}, u32[]{:S(2)}) collective-permute-start(bf16[512,256]{1,0:T(8,128)(2,1)} %collective-permute-done.6), channel_id=1, source_target_pairs={{1,0},{2,3},{5,4},{6,7},{9,8},{10,11},{13,12},{14,15},{17,16},{18,... | collective-permute-start | bytes 786440 | tf_op jit(solution)/shard_map/ppermute | solution.py:218
  38.9 11.4 %collective-permute-start.3 = (f32[16,2048]{1,0:T(8,128)S(1)}, f32[16,2048]{1,0:T(8,128)S(1)}, u32[]{:S(2)}, u32[]{:S(2)}) collective-permute-start(f32[16,2048]{1,0:T(8,128)S(1)} %add_select_fusion.2), channel_id=1, source_target_pairs={{0,16},{4,20},{8,24},{12,28},{16,0},{20,4},{24,8},{28,12},{1,17},{... | collective-permute-start | bytes 393224 | tf_op jit(solution)/shard_map/ppermute | solution.py:171
  46.7 8.9 %collective-permute-start.11 = (bf16[512,256]{1,0:T(8,128)(2,1)S(1)}, bf16[512,256]{1,0:T(8,128)(2,1)S(1)}, u32[]{:S(2)}, u32[]{:S(2)}) collective-permute-start(bf16[512,256]{1,0:T(8,128)(2,1)S(1)} %broadcast_select_fusion.1.refs_7_), channel_id=1, source_target_pairs={{0,8},{4,20},{8,0},{12,28},{16,24},{20,4},{24,16},{28,12},{1,9},{5... | collective-permute-start | bytes 786440 | tf_op jit(solution)/shard_map/ppermute | solution.py:201
  48.4 8.5 %collective-permute-start.8 = (bf16[512,256]{1,0:T(8,128)(2,1)}, bf16[512,256]{1,0:T(8,128)(2,1)S(1)}, u32[]{:S(2)}, u32[]{:S(2)}) collective-permute-start(bf16[512,256]{1,0:T(8,128)(2,1)} %collective-permute-done.5), channel_id=1, source_target_pairs={{1,0},{2,3},{5,4},{6,7},{9,8},{10,11},{13,12},{14,15},{17,16},{18,... | collective-permute-start | bytes 786440 | tf_op jit(solution)/shard_map/ppermute | solution.py:223
  49.7 6.4 %collective-permute-start.12 = (bf16[512,256]{1,0:T(8,128)(2,1)S(1)}, bf16[512,256]{1,0:T(8,128)(2,1)S(1)}, u32[]{:S(2)}, u32[]{:S(2)}) collective-permute-start(bf16[512,256]{1,0:T(8,128)(2,1)S(1)} %collective-permute-done.10.refs_4_), channel_id=1, source_target_pairs={{0,16},{4,12},{8,24},{12,4},{16,0},{20,28},{24,8},{28,20},{1,17},{... | collective-permute-start | bytes 786440 | tf_op jit(solution)/shard_map/ppermute | solution.py:201
  52.9 15.5 %collective-permute-start.4 = (bf16[128,2048]{1,0:T(8,128)(2,1)S(1)}, bf16[128,2048]{1,0:T(8,128)(2,1)S(1)}, u32[]{:S(2)}, u32[]{:S(2)}) collective-permute-start(bf16[128,2048]{1,0:T(8,128)(2,1)S(1)} %gate.1.refs_0_), channel_id=1, source_target_pairs={{0,4},{4,0},{8,12},{12,8},{16,20},{20,16},{24,28},{28,24},{1,5},{5... | collective-permute-start | bytes 1572872 | tf_op jit(solution)/shard_map/ppermute | solution.py:290
  53.0 7.5 %collective-permute-start.16 = (bf16[512,256]{1,0:T(8,128)(2,1)S(1)}, bf16[512,256]{1,0:T(8,128)(2,1)S(1)}, u32[]{:S(2)}, u32[]{:S(2)}) collective-permute-start(bf16[512,256]{1,0:T(8,128)(2,1)S(1)} %broadcast_select_fusion.1.refs_7_), channel_id=1, source_target_pairs={{0,16},{4,12},{8,24},{12,4},{16,0},{20,28},{24,8},{28,20},{1,17},{... | collective-permute-start | bytes 786440 | tf_op jit(solution)/shard_map/ppermute | solution.py:201
  56.8 8.2 %collective-permute-start.15 = (bf16[512,256]{1,0:T(8,128)(2,1)S(1)}, bf16[512,256]{1,0:T(8,128)(2,1)S(1)}, u32[]{:S(2)}, u32[]{:S(2)}) collective-permute-start(bf16[512,256]{1,0:T(8,128)(2,1)S(1)} %collective-permute-done.11.refs_8_), channel_id=1, source_target_pairs={{0,16},{4,12},{8,24},{12,4},{16,0},{20,28},{24,8},{28,20},{1,17},{... | collective-permute-start | bytes 786440 | tf_op jit(solution)/shard_map/ppermute | solution.py:201
  57.4 9.4 %collective-permute-start.13 = (bf16[512,256]{1,0:T(8,128)(2,1)S(1)}, bf16[512,256]{1,0:T(8,128)(2,1)}, u32[]{:S(2)}, u32[]{:S(2)}) collective-permute-start(bf16[512,256]{1,0:T(8,128)(2,1)S(1)} %broadcast_select_fusion.refs_2_), channel_id=1, source_target_pairs={{0,8},{4,20},{8,0},{12,28},{16,24},{20,4},{24,16},{28,12},{1,9},{5... | collective-permute-start | bytes 786440 | tf_op jit(solution)/shard_map/ppermute | solution.py:201
  58.9 9.5 %collective-permute-start.18 = (bf16[512,256]{1,0:T(8,128)(2,1)S(1)}, bf16[512,256]{1,0:T(8,128)(2,1)S(1)}, u32[]{:S(2)}, u32[]{:S(2)}) collective-permute-start(bf16[512,256]{1,0:T(8,128)(2,1)S(1)} %collective-permute-done.9.refs_3_), channel_id=1, source_target_pairs={{0,16},{4,12},{8,24},{12,4},{16,0},{20,28},{24,8},{28,20},{1,17},{... | collective-permute-start | bytes 786440 | tf_op jit(solution)/shard_map/ppermute | solution.py:201
  60.5 10.5 %collective-permute-start.14 = (bf16[512,256]{1,0:T(8,128)(2,1)S(1)}, bf16[512,256]{1,0:T(8,128)(2,1)}, u32[]{:S(2)}, u32[]{:S(2)}) collective-permute-start(bf16[512,256]{1,0:T(8,128)(2,1)S(1)} %broadcast_select_fusion.refs_2_), channel_id=1, source_target_pairs={{0,16},{4,12},{8,24},{12,4},{16,0},{20,28},{24,8},{28,20},{1,17},{... | collective-permute-start | bytes 786440 | tf_op jit(solution)/shard_map/ppermute | solution.py:201
  66.8 6.8 %collective-permute-start.17 = (bf16[512,256]{1,0:T(8,128)(2,1)}, bf16[512,256]{1,0:T(8,128)(2,1)}, u32[]{:S(2)}, u32[]{:S(2)}) collective-permute-start(bf16[512,256]{1,0:T(8,128)(2,1)} %collective-permute-done.13.refs_3_), channel_id=1, source_target_pairs={{0,16},{4,12},{8,24},{12,4},{16,0},{20,28},{24,8},{28,20},{1,17},{... | collective-permute-start | bytes 786440 | tf_op jit(solution)/shard_map/ppermute | solution.py:201
  75.2 1.6 %collective-permute-start.19 = (bf16[128,1024]{1,0:T(8,128)(2,1)S(1)}, bf16[128,1024]{1,0:T(8,128)(2,1)S(1)}, u32[]{:S(2)}, u32[]{:S(2)}) collective-permute-start(bf16[128,1024]{1,0:T(8,128)(2,1)S(1)} %get-tuple-element.32), channel_id=1, source_target_pairs={{0,4},{4,0},{8,12},{12,8},{16,20},{20,16},{24,28},{28,24},{1,5},{5... | collective-permute-start | bytes 786440 | tf_op jit(solution)/shard_map/ppermute | solution.py:321

commit v2 on v1

v2 whole, which is shorter than its diff:
```python
import functools

import jax
import jax.numpy as jnp
from jax import lax
from jax.experimental import pallas as pl
from jax.experimental.pallas import tpu as pltpu
from jax.sharding import PartitionSpec as P

GROUP = 16
FEAT = 3
WIDE = 512
LANES = 128
SUB = 32
VMEM_LIMIT = 48 << 20

bf16 = jnp.bfloat16
f32 = jnp.float32


def after(x, *deps):
    return lax.optimization_barrier((x,) + deps)[0]


def params():
    return pltpu.CompilerParams(vmem_limit_bytes=VMEM_LIMIT)


def split(x):
    high = x.astype(bf16)
    return high, (x - high.astype(f32)).astype(bf16)


def iota(shape, dim):
    return lax.broadcasted_iota(jnp.int32, shape, dim)


def one_less_exp(x):
    small = jnp.minimum(x, 0.5)
    series = jnp.ones_like(x)
    for n in range(9, 1, -1):
        series = 1.0 - small * (1.0 / n) * series
    return jnp.where(x < 0.5, small * series, 1.0 - jnp.exp(-x))


def dot(a, b):
    return jnp.dot(a, b, preferred_element_type=f32)


def featurize(rows, tail, taps):
    values = rows.astype(f32)
    at = iota(values.shape, 0)
    one = jnp.where(at == 0, tail[1:2], pltpu.roll(values, 1, 0))
    two = jnp.where(at == 0, tail[0:1], jnp.where(at == 1, tail[1:2], pltpu.roll(values, 2, 0)))
    return taps[0:1] * values + taps[1:2] * one + taps[2:3] * two


def table_kernel(rate_ref, residue_ref, left_ref, lag_ref, rate_chan_ref):
    rate = rate_ref[...]
    groups, modes = rate.shape
    scale = residue_ref[...] * jnp.sqrt(one_less_exp(2.0 * rate))
    blocks, _, depth = left_ref.shape
    sub = left_ref.shape[1] // 2 - modes
    each = groups // blocks

    def expand(table, width, count, first):
        pick = iota((groups, count), 0) == first + iota((groups, count), 1) // width
        return lax.dot_general(
            table,
            pick.astype(f32),
            (((0,), (0,)), ((), ())),
            precision=lax.Precision.HIGHEST,
            preferred_element_type=f32,
        )

    rate_chan_ref[...] = expand(rate, GROUP, groups * GROUP, 0)
    rate_wide = expand(rate, sub, groups * sub, 0)
    scale_wide = expand(scale, sub, groups * sub, 0)
    place = iota((modes, groups * sub), 1) % sub
    back = jnp.where(place == 0, 0, sub - place).astype(f32)
    taps = jnp.sum(scale_wide * jnp.exp(-rate_wide * back), axis=0, keepdims=True)
    ends = scale_wide * jnp.exp(-rate_wide * (sub - 1 - place).astype(f32))
    end_high, end_low = split(ends)
    causal = iota((sub, LANES), 0) >= iota((sub, LANES), 1) % sub
    start = iota((1, LANES), 1) % sub == 0
    mode_pick = iota((modes, each * modes), 0) == iota((modes, each * modes), 1) % modes
    group_at = iota((groups, each * modes), 1) // modes
    ahead = (iota((sub, each * modes), 0) + 1).astype(f32)
    for b in range(blocks):
        for part in range(depth // LANES):
            at = b * depth + part * LANES
            row = taps[:, at : at + LANES]
            row = jnp.where(start, row, pltpu.roll(row, LANES - sub, 1))
            band = pltpu.roll(jnp.broadcast_to(row, (sub, LANES)), 0, 1, stride=1, stride_axis=0)
            high, low = split(jnp.where(causal, band, 0.0))
            to = slice(part * LANES, (part + 1) * LANES)
            left_ref[b, :sub, to] = high
            left_ref[b, sub : 2 * sub, to] = low
        cols = slice(b * depth, (b + 1) * depth)
        left_ref[b, 2 * sub : 2 * sub + modes] = end_high[:, cols]
        left_ref[b, 2 * sub + modes :] = end_low[:, cols]
        spread = jnp.dot(
            (iota((groups, each * modes), 0) == b * each + group_at).astype(f32).T,
            rate,
            precision=lax.Precision.HIGHEST,
            preferred_element_type=f32,
        )
        rate_lane = jnp.sum(jnp.where(mode_pick, spread.T, 0.0), axis=0, keepdims=True)
        high, low = split(jnp.exp(-rate_lane * ahead))
        lag_ref[b, :sub] = jnp.concatenate([high, high], axis=1)
        lag_ref[b, sub:] = jnp.concatenate([low, jnp.zeros_like(low)], axis=1)


def own_groups(rows_each):
    rows = LANES // GROUP * rows_each
    return iota((rows, LANES), 0) // rows_each == iota((rows, LANES), 1) // GROUP


def product_kernel(
    key_ref, value_ref, halo_ref, taps_ref, left_ref, rate_ref, kv_ref, inner_ref, before_ref, state_ref
):
    rows, width = key_ref.shape
    modes = rate_ref.shape[0]
    sub = left_ref.shape[1] // 2 - modes
    count = rows // sub
    halo = halo_ref[...]
    key = featurize(key_ref[...], halo[2:4], taps_ref[1])
    value = featurize(value_ref[...], halo[4:6], taps_ref[2])
    kv = (key * value).astype(bf16)
    kv_ref[...] = kv
    same = own_groups(sub)
    fade = jnp.exp(-rate_ref[...] * float(sub))
    for b in range(width // LANES):
        cols = slice(b * LANES, (b + 1) * LANES)
        total = jnp.zeros((modes, LANES), f32)
        for first in range(0, count, 2):
            right = []
            for s in (first, first + 1):
                piece = kv[s * sub : (s + 1) * sub, cols]
                spread = jnp.concatenate([piece] * (LANES // GROUP), axis=0)
                right.append(jnp.where(same, spread, jnp.zeros_like(spread)))
            out = dot(left_ref[b], jnp.concatenate(right, axis=1))
            for s in (first, first + 1):
                part = out[:, (s - first) * LANES : (s - first + 1) * LANES]
                inner_ref[s * sub : (s + 1) * sub, cols] = part[:sub] + part[sub : 2 * sub]
                before_ref[s * modes : (s + 1) * modes, cols] = total
                total = total * fade[:, cols] + (
                    part[2 * sub : 2 * sub + modes] + part[2 * sub + modes :]
                )
        state_ref[:, cols] = total


def blend_kernel(rows, step, where_ref, state_ref, other_ref, enter_ref, rate_ref, new_ref, into_ref):
    index = where_ref[0]
    upper = (index // step) % 2 == 1
    within = ((index % step) * rows).astype(f32)
    rate = rate_ref[...]
    state, other, enter = state_ref[...], other_ref[...], enter_ref[...]
    into_ref[...] = jnp.where(upper, enter + jnp.exp(-rate * within) * other, enter)
    fade = jnp.exp(-rate * float(step * rows))
    new_ref[...] = jnp.where(upper, other * fade + state, state * fade + other)


def gate_kernel(
    step, where_ref, query_ref, halo_ref, taps_ref, kv_ref, inner_ref, before_ref, enter_ref, other_ref,
    rate_ref, lag_ref, skip_ref, out_ref,
):
    rows, width = query_ref.shape
    modes = rate_ref.shape[0]
    sub = lag_ref.shape[1] // 2
    index = where_ref[0]
    upper = (index // step) % 2 == 1
    within = ((index % step) * rows).astype(f32)
    query = featurize(query_ref[...], halo_ref[0:2], taps_ref[0])
    rate = rate_ref[...]
    enter = enter_ref[...]
    enter = jnp.where(upper, enter + jnp.exp(-rate * within) * other_ref[...], enter)
    fade = jnp.exp(-rate * float(sub))
    same = own_groups(modes)
    for b in range(width // LANES):
        cols = slice(b * LANES, (b + 1) * LANES)
        far = enter[:, cols]
        for first in range(0, rows // sub, 2):
            right = []
            for s in (first, first + 1):
                total = far + before_ref[s * modes : (s + 1) * modes, cols]
                spread = jnp.concatenate([total] * (LANES // GROUP), axis=0)
                right.append(jnp.concatenate(split(jnp.where(same, spread, 0.0)), axis=0))
                far = far * fade[:, cols]
            cross = dot(lag_ref[b], jnp.concatenate(right, axis=1))
            for s in (first, first + 1):
                part = cross[:, (s - first) * LANES : (s - first + 1) * LANES]
                at = slice(s * sub, (s + 1) * sub)
                convolved = inner_ref[at, cols] + (part[:sub] + part[sub:])
                convolved = convolved.astype(bf16).astype(f32)
                kv = kv_ref[at, cols].astype(f32)
                out_ref[at, cols] = (query[at, cols] * (convolved + skip_ref[:, cols] * kv)).astype(bf16)


def tail_kernel(query_ref, key_ref, value_ref, out_ref):
    keep = FEAT - 1
    for i, ref in enumerate((query_ref, key_ref, value_ref)):
        rows = ref[...].astype(f32)
        out_ref[i * keep : (i + 1) * keep] = rows[rows.shape[0] - keep :]
    out_ref[3 * keep :] = jnp.zeros((out_ref.shape[0] - 3 * keep, out_ref.shape[1]), f32)


def send_tails(query, key, value):
    rows, chans = query.shape
    count = lax.axis_size("ctx")
    last = pl.BlockSpec((16, chans), lambda i: (rows // 16 - 1, 0))
    tails = pl.pallas_call(
        tail_kernel,
        grid=(1,),
        in_specs=[last] * 3,
        out_specs=pl.BlockSpec((8, chans), lambda i: (0, 0)),
        out_shape=jax.ShapeDtypeStruct((8, chans), f32),
        compiler_params=params(),
        name="last_rows",
    )(query, key, value)
    return lax.ppermute(tails, "ctx", [(i, i + 1) for i in range(count - 1)])


def conv_path(query, key, value, halo, taps, rate, residues, skip):
    rows, chans = query.shape
    groups, modes = rate.shape
    count = lax.axis_size("ctx")
    here = lax.axis_index("ctx")[None].astype(jnp.int32)
    blocks = chans // LANES
    depth = LANES // GROUP * SUB
    steps = chans // WIDE
    per = WIDE // LANES
    vmem = pl.BlockSpec(memory_space=pltpu.VMEM)
    smem = pl.BlockSpec(memory_space=pltpu.SMEM)
    state_shape = jax.ShapeDtypeStruct((modes, chans), f32)
    left, lag, rate_chan = pl.pallas_call(
        table_kernel,
        in_specs=[vmem, vmem],
        out_specs=[vmem] * 3,
        out_shape=[
            jax.ShapeDtypeStruct((blocks, 2 * (SUB + modes), depth), bf16),
            jax.ShapeDtypeStruct((blocks, 2 * SUB, 2 * (LANES // GROUP) * modes), bf16),
            state_shape,
        ],
        compiler_params=params(),
        name="tables",
    )(rate, residues)

    def wide(height):
        return pl.BlockSpec((height, WIDE), lambda b: (0, b))

    def stack(array):
        return pl.BlockSpec((per,) + array.shape[1:], lambda b: (b, 0, 0))

    taps_spec = pl.BlockSpec((3, FEAT, WIDE), lambda b: (0, 0, b))
    subs = rows // SUB
    kv, inner, before, state = pl.pallas_call(
        product_kernel,
        grid=(steps,),
        in_specs=[wide(rows), wide(rows), wide(8), taps_spec, stack(left), wide(modes)],
        out_specs=[wide(rows), wide(rows), wide(subs * modes), wide(modes)],
        out_shape=[
            jax.ShapeDtypeStruct((rows, chans), bf16),
            jax.ShapeDtypeStruct((rows, chans), f32),
            jax.ShapeDtypeStruct((subs * modes, chans), f32),
            state_shape,
        ],
        compiler_params=params(),
        name="kv_and_state",
    )(key, value, halo, taps, left, rate_chan)
    enter = jnp.zeros_like(state)
    step = 1
    while True:
        other = lax.ppermute(state, "ctx", [(i, i ^ step) for i in range(count)])
        if 2 * step >= count:
            break
        state, enter = pl.pallas_call(
            functools.partial(blend_kernel, rows, step),
            in_specs=[smem] + [vmem] * 4,
            out_specs=[vmem] * 2,
            out_shape=[state_shape] * 2,
            compiler_params=params(),
            name="blend_states",
        )(here, state, other, enter, rate_chan)
        step *= 2
    return pl.pallas_call(
        functools.partial(gate_kernel, step),
        grid=(steps,),
        in_specs=[
            smem,
            wide(rows),
            wide(8),
            taps_spec,
            wide(rows),
            wide(rows),
            wide(subs * modes),
            wide(modes),
            wide(modes),
            wide(modes),
            stack(lag),
            wide(1),
        ],
        out_specs=wide(rows),
        out_shape=jax.ShapeDtypeStruct((rows, chans), bf16),
        compiler_params=params(),
        name="gate",
    )(here, query, halo, taps, kv, inner, before, enter, other, rate_chan, lag, skip[None])


def hop(x, first):
    count = lax.axis_size("ctx")
    even, odd = (2, 4) if first else (4, 2)
    return lax.ppermute(x, "ctx", [(i, i ^ (odd if i % 2 else even)) for i in range(count)])


def spread_slot(piece, *first):
    one, two = hop(piece, True), hop(piece, False)
    return piece, one, two, hop(after(one, *first), False)


def send_weight(weight):
    index = lax.axis_index("ctx")
    depth, cols = weight.shape
    block = cols // 8
    mine = lax.dynamic_slice(weight, (0, (index % 8) * block), (depth, block))
    near = lax.ppermute(mine, "fsdp", [(i, i ^ 1) for i in range(4)])
    return mine, near


def gather_weight(mine, near):
    two = lax.ppermute(mine, "fsdp", [(i, i ^ 2) for i in range(4)])
    three = lax.ppermute(mine, "fsdp", [(i, i ^ 3) for i in range(4)])
    slot_one = spread_slot(near)
    slot_two = spread_slot(after(two, slot_one[1]))
    slot_three = spread_slot(after(three, slot_two[1], *slot_one), *slot_two)
    return slot_one, slot_two, slot_three


def matmul_kernel(slot_count, has_own, has_acc, last, nums_ref, *refs):
    refs = list(refs)
    mine_ref, other_ref = refs[0], refs[1]
    refs = refs[2:]
    if has_own:
        weight_ref = refs.pop(0)
    slots = [refs[4 * s : 4 * s + 4] for s in range(slot_count)]
    refs = refs[4 * slot_count :]
    if has_acc:
        acc_ref = refs.pop(0)
    rows = mine_ref.shape[0]
    depth, block = slots[0][0].shape

    def rows_of(part):
        at = pl.multiple_of(nums_ref[part] * depth, depth)
        return jnp.concatenate(
            [mine_ref[:, pl.ds(at, depth)], other_ref[:, pl.ds(at, depth)]], axis=0
        )

    lhs = [rows_of(1 + s) for s in range(slot_count)]
    if has_own:
        own = rows_of(0)
    for r in range(4):
        total = acc_ref[:, r * block : (r + 1) * block] if has_acc else None
        if has_own:
            at = pl.multiple_of(nums_ref[4 + r] * block, block)
            total = dot(own, weight_ref[:, pl.ds(at, block)])
        for s in range(slot_count):
            part = dot(lhs[s], slots[s][r][...])
            total = part if total is None else total + part
        if last:
            at = pl.multiple_of(nums_ref[8 + r] * block, block)
            done = total.astype(bf16)
            refs[0][:, pl.ds(at, block)] = done[:rows]
            refs[1][:, pl.ds(at, block)] = done[rows:]
        else:
            refs[0][:, r * block : (r + 1) * block] = total


def join_kernel(nums_ref, mine_ref, other_ref, out_ref):
    block = mine_ref.shape[1] // 4
    core = nums_ref[0]
    for h in range(4):
        at = pl.multiple_of((2 * h + core) * block, block)
        out_ref[:, pl.ds(at, block)] = mine_ref[:, h * block : (h + 1) * block]
        at = pl.multiple_of((2 * h + 1 - core) * block, block)
        out_ref[:, pl.ds(at, block)] = other_ref[:, h * block : (h + 1) * block]


def project(gated, weight, slots):
    count = lax.axis_size("ctx")
    index = lax.axis_index("ctx")
    place = lax.axis_index("fsdp")
    rows = gated.shape[0]
    depth, cols = weight.shape
    half = cols // 2
    swap = [(i, i ^ 1) for i in range(count)]
    other = lax.ppermute(gated, "ctx", swap)
    core = index % 2
    first, second = jnp.where(core == 0, 2, 4), jnp.where(core == 0, 4, 2)
    rel = index % 8
    order = [rel, rel ^ first, rel ^ second, rel ^ 6]
    parts = [place, place ^ 1, place ^ 2, place ^ 3]
    nums = jnp.stack(parts + order + [n // 2 for n in order]).astype(jnp.int32)
    vmem = pl.BlockSpec(memory_space=pltpu.VMEM)
    smem = pl.BlockSpec(memory_space=pltpu.SMEM)
    acc = pl.pallas_call(
        functools.partial(matmul_kernel, 2, True, False, False),
        in_specs=[smem] + [vmem] * 11,
        out_specs=vmem,
        out_shape=jax.ShapeDtypeStruct((2 * rows, half), f32),
        compiler_params=params(),
        name="project_near",
    )(nums, gated, other, weight, *slots[0], *slots[1])
    late = nums.at[1].set(nums[3])
    mine, theirs = pl.pallas_call(
        functools.partial(matmul_kernel, 1, False, True, True),
        in_specs=[smem] + [vmem] * 7,
        out_specs=[vmem, vmem],
        out_shape=[jax.ShapeDtypeStruct((rows, half), bf16)] * 2,
        compiler_params=params(),
        name="project_far",
    )(late, gated, other, *slots[2], acc)
    back = lax.ppermute(theirs, "ctx", swap)
    return pl.pallas_call(
        join_kernel,
        in_specs=[smem, vmem, vmem],
        out_specs=vmem,
        out_shape=jax.ShapeDtypeStruct((rows, cols), bf16),
        compiler_params=params(),
        name="join_columns",
    )(core[None].astype(jnp.int32), mine, back)


def local(query_in, key_in, value_in, feature_taps, decay_rate, residues, skip_gain, out_weight):
    query, key, value = query_in[0], key_in[0], value_in[0]
    mine, near = send_weight(out_weight)
    halo = send_tails(query, key, value)
    gated = conv_path(query, key, value, halo, feature_taps, decay_rate, residues, skip_gain)
    return project(gated, out_weight, gather_weight(mine, near))[None]


def solution(mesh):
    return jax.shard_map(
        local,
        mesh=mesh,
        in_specs=(
            P("fsdp", "ctx", None),
            P("fsdp", "ctx", None),
            P("fsdp", "ctx", None),
            P(),
            P(),
            P(),
            P(),
            P("fsdp", None),
        ),
        out_specs=P("fsdp", "ctx", None),
        check_vma=False,
    )
```

time: 78.4 us -> 74.1 us (0.945)
  waiting for transfers between devices: 18.5 us -> 29.9 us
  Pallas kernels: 17.3 us -> 11.9 us
  local copies, waits for them, and re-layouts: 10.9 us -> 6.08 us
  starting transfers between devices: 29.6 us -> 25.7 us
  other arithmetic: 0.98 us -> 0 us
    ppermute x3, waiting for transfers between devices: 0.01 us -> 8.78 us  [conv_path(): other = lax.ppermute(state, 'ctx', [(i, i ^ step) for i in range(count)])]
    ppermute x6 -> x4, waiting for transfers between devices: 4 us -> 9.42 us  [the longest x1 9.41 us: send_weight(): near = lax.ppermute(mine, 'fsdp', [(i, i ^ 1) for i in range(4)])]
    pallas_call x4 -> x6, Pallas kernels: 12.3 us -> 6.89 us  [the longest x1 2.57 us: conv_path(): pl.pallas_call(table_kernel, in_specs=[vmem, vmem], out_specs=[vmem] * 3,...]
    ppermute x6 -> x4, starting transfers between devices: 13.7 us -> 9.55 us  [the longest x1 3.05 us: send_weight(): near = lax.ppermute(mine, 'fsdp', [(i, i ^ 1) for i in range(4)])]
    exp x5 -> x0, local copies, waits for them, and re-layouts: 3.8 us -> none  [the longest x3 2.54 us: conv_path(): jnp.exp(-rate_chan * within) * other]
    ppermute x9, waiting for transfers between devices: 12.9 us -> 10.2 us  [hop(): lax.ppermute(x, 'ctx', [(i, i ^ (odd if i % 2 else even)) for i in range(...]
    unnamed x16 -> x22, local copies, waits for them, and re-layouts: 2.5 us -> 4.24 us
    slice x2 -> x0, local copies, waits for them, and re-layouts: 1.66 us -> none  [the longest x1 0.86 us: conv_path(): query[rows - keep:]]
  transfers between devices with their start and end apart: 20 -> 18, of which waited for: 10 -> 7; matrix products, arithmetic and copies ran while one was open for 12% -> 0% of each run, Pallas kernels for 16% -> 13%
where the time goes in v2:
time: 74.1 us; the launch traced here: 73.8 us
  waiting for transfers between devices  29.9 us (40%)
  starting transfers between devices  25.7 us (35%)
  Pallas kernels  11.9 us (16%)
  local copies, waits for them, and re-layouts  6.08 us (8%)
    ppermute x9, waiting for transfers between devices, hop(): lax.ppermute(x, 'ctx', [(i, i ^ (odd if i % 2 else even)) for i in range(...  10.2 us
    ppermute x9, starting transfers between devices, hop(): lax.ppermute(x, 'ctx', [(i, i ^ (odd if i % 2 else even)) for i in range(...  10.1 us
    ppermute x1, waiting for transfers between devices, send_weight(): near = lax.ppermute(mine, 'fsdp', [(i, i ^ 1) for i in range(4)])  9.41 us
    ppermute x3, waiting for transfers between devices, conv_path(): other = lax.ppermute(state, 'ctx', [(i, i ^ step) for i in range(count)])  8.78 us
    ppermute x3, starting transfers between devices, conv_path(): other = lax.ppermute(state, 'ctx', [(i, i ^ step) for i in range(count)])  5.92 us
    unnamed x22, local copies, waits for them, and re-layouts  4.24 us
    ppermute x1, starting transfers between devices, send_weight(): near = lax.ppermute(mine, 'fsdp', [(i, i ^ 1) for i in range(4)])  3.05 us
    ppermute x1, starting transfers between devices, gather_weight(): two = lax.ppermute(mine, 'fsdp', [(i, i ^ 2) for i in range(4)])  2.59 us
  transfers between devices with their start and end apart: 18, of which 7 were waited for; matrix products, arithmetic and copies ran while one was open for 0% of the time, Pallas kernels for 13%

profile of v2, /device:TPU:0, one launch (start us, length us, event | category | flops | bytes accessed | tf_op | source)
XLA Modules:
  0.0 73.8 jit_solution(7570222974903886392)
XLA Ops:
  0.0 0.0 copy-start.3
  0.0 0.0 copy-start.8
  0.0 0.0 copy-start.9
  0.0 1.7 %constant_dynamic-slice_fusion = bf16[512,256]{1,0:T(8,128)(2,1)} fusion(bf16[512,2048]{1,0:T(8,128)(2,1)} %refs_2_.1, s32[]{:T(128)S(6)} %select_n.44), kind=kLoop, calls=%fused_computation.1 | loop fusion | bytes 524292 | tf_op jit(solution)/shard_map/dynamic_slice | solution.py:325
  1.7 3.0 %collective-permute-start.7 = (bf16[512,256]{1,0:T(8,128)(2,1)}, bf16[512,256]{1,0:T(8,128)(2,1)S(1)}, u32[]{:S(2)}, u32[]{:S(2)}) collective-permute-start(bf16[512,256]{1,0:T(8,128)(2,1)} %constant_dynamic-slice_fusion), channel_id=1, source_target_pairs={{0,1},{1,0},{2,3},{3,2},{4,5},{5,4},{6,7},{7,6},{8,9},{9,8},{10,11... | collective-permute-start | bytes 786440 | tf_op jit(solution)/shard_map/ppermute | solution.py:326
  4.8 2.6 %collective-permute-start.6 = (bf16[512,256]{1,0:T(8,128)(2,1)}, bf16[512,256]{1,0:T(8,128)(2,1)S(1)}, u32[]{:S(2)}, u32[]{:S(2)}) collective-permute-start(bf16[512,256]{1,0:T(8,128)(2,1)} %constant_dynamic-slice_fusion), channel_id=1, source_target_pairs={{0,2},{1,3},{2,0},{3,1},{4,6},{5,7},{6,4},{7,5},{8,10},{9,11},{10,... | collective-permute-start | bytes 786440 | tf_op jit(solution)/shard_map/ppermute | solution.py:331
  7.4 9.4 %collective-permute-done.7.refs_3_ = bf16[512,256]{1,0:T(8,128)(2,1)S(1)} collective-permute-done((bf16[512,256]{1,0:T(8,128)(2,1)}, bf16[512,256]{1,0:T(8,128)(2,1)S(1)}, u32[]{:S(2)}, u32[]{:S(2)}) %collective-permute-start.7) | collective-permute-done | bytes 262176 | tf_op jit(solution)/shard_map/ppermute | solution.py:326
  16.8 1.7 %collective-permute-start.8 = (bf16[512,256]{1,0:T(8,128)(2,1)S(1)}, bf16[512,256]{1,0:T(8,128)(2,1)S(1)}, u32[]{:S(2)}, u32[]{:S(2)}) collective-permute-start(bf16[512,256]{1,0:T(8,128)(2,1)S(1)} %collective-permute-done.7.refs_3_), channel_id=1, source_target_pairs={{0,8},{4,20},{8,0},{12,28},{16,24},{20,4},{24,16},{28,12},{1,9},{5... | collective-permute-start | bytes 786440 | tf_op jit(solution)/shard_map/ppermute | solution.py:313
  18.4 0.0 copy-start
  18.4 1.0 %copy-done = bf16[1,128,2048]{2,1,0:T(8,128)(2,1)S(1)} copy-done((bf16[1,128,2048]{2,1,0:T(8,128)(2,1)S(1)}, bf16[1,128,2048]{2,1,0:T(8,128)(2,1)}, u32[]{:S(2)}) %copy-start) | copy-done | bytes 524312
  19.5 1.0 %copy-done.2 = bf16[1,128,2048]{2,1,0:T(8,128)(2,1)S(1)} copy-done((bf16[1,128,2048]{2,1,0:T(8,128)(2,1)S(1)}, bf16[1,128,2048]{2,1,0:T(8,128)(2,1)}, u32[]{:S(2)}) %copy-start.2) | copy-done | bytes 524312
  20.5 1.0 %copy-done.4 = bf16[1,128,2048]{2,1,0:T(8,128)(2,1)S(1)} copy-done((bf16[1,128,2048]{2,1,0:T(8,128)(2,1)S(1)}, bf16[1,128,2048]{2,1,0:T(8,128)(2,1)}, u32[]{:S(2)}) %copy-start.4) | copy-done | bytes 524312
  21.6 0.0 copy-start.1
  21.6 1.4 %collective-permute-start = (f32[8,2048]{1,0:T(8,128)S(1)}, f32[8,2048]{1,0:T(8,128)S(1)}, u32[]{:S(2)}, u32[]{:S(2)}) collective-permute-start(f32[8,2048]{1,0:T(8,128)S(1)} %last_rows.1), channel_id=1, source_target_pairs={{0,4},{4,8},{8,12},{12,16},{16,20},{20,24},{24,28},{1,5},{5,9},{9,... | collective-permute-start | bytes 196616 | tf_op jit(solution)/shard_map/ppermute | solution.py:221
  23.0 0.0 copy-done.8
  23.0 0.1 copy.9.rate_ref
  23.1 0.0 copy-done.9
  23.2 0.1 copy.10.residue_ref
  23.3 2.6 %tables.1 = (bf16[16,96,256]{2,1,0:T(8,128)(2,1)S(1)}, bf16[16,64,256]{2,1,0:T(8,128)(2,1)S(1)}, f32[16,2048]{1,0:T(8,128)S(1)}) custom-call(f32[128,16]{1,0:T(8,128)S(1)} %copy.9.rate_ref, f32[128,16]{1,0:T(8,128)S(1)} %copy.10.residue_ref), custom_call_target="tpu_custom_call" | custom-call | tf_op jit(solution)/shard_map/tables/pallas_call | solution.py:236
  25.8 0.0 collective-permute-done.halo_ref
  25.8 0.0 copy-done.3
  25.8 0.0 copy-done.5
  25.8 0.0 copy-start.6
  25.9 0.9 %copy-done.6 = f32[3,3,2048]{2,1,0:T(4,128)S(1)} copy-done((f32[3,3,2048]{2,1,0:T(4,128)S(1)}, f32[3,3,2048]{2,1,0:T(4,128)}, u32[]{:S(2)}) %copy-start.6) | copy-done | bytes 73752
  26.7 2.3 %kv_and_state.1 = (bf16[128,2048]{1,0:T(8,128)(2,1)S(1)}, f32[128,2048]{1,0:T(8,128)S(1)}, f32[64,2048]{1,0:T(8,128)S(1)}, f32[16,2048]{1,0:T(8,128)S(1)}) custom-call(bf16[128,2048]{1,0:T(8,128)(2,1)S(1)} %bitcast.22, bf16[128,2048]{1,0:T(8,128)(2,1)S(1)} %bitcast.24, f32[8,2048]{1,0:T(8,128)S(1)} %collective-permute-done.halo_ref, ...), custom_call_target="tpu_custom_call" | custom-call | tf_op jit(solution)/shard_map/kv_and_state/pallas_call | solution.py:257
  29.0 1.2 %collective-permute-start.1 = (f32[16,2048]{1,0:T(8,128)S(1)}, f32[16,2048]{1,0:T(8,128)S(1)}, u32[]{:S(2)}, u32[]{:S(2)}) collective-permute-start(f32[16,2048]{1,0:T(8,128)S(1)} %get-tuple-element.38.state_ref), channel_id=1, source_target_pairs={{0,4},{4,0},{8,12},{12,8},{16,20},{20,16},{24,28},{28,24},{1,5},{5... | collective-permute-start | bytes 393224 | tf_op jit(solution)/shard_map/ppermute | solution.py:274
  30.2 1.0 %collective-permute-done.1.other_ref = f32[16,2048]{1,0:T(8,128)S(1)} collective-permute-done((f32[16,2048]{1,0:T(8,128)S(1)}, f32[16,2048]{1,0:T(8,128)S(1)}, u32[]{:S(2)}, u32[]{:S(2)}) %collective-permute-start.1) | collective-permute-done | bytes 131104 | tf_op jit(solution)/shard_map/ppermute | solution.py:274
  31.2 0.1 blend_states.2
  31.3 2.7 %collective-permute-start.2 = (f32[16,2048]{1,0:T(8,128)S(1)}, f32[16,2048]{1,0:T(8,128)S(1)}, u32[]{:S(2)}, u32[]{:S(2)}) collective-permute-start(f32[16,2048]{1,0:T(8,128)S(1)} %get-tuple-element.39.state_ref), channel_id=1, source_target_pairs={{0,8},{4,12},{8,0},{12,4},{16,24},{20,28},{24,16},{28,20},{1,9},{5... | collective-permute-start | bytes 393224 | tf_op jit(solution)/shard_map/ppermute | solution.py:274
  34.0 0.0 collective-permute-done.6.refs_7_
  34.0 0.0 collective-permute-done.8.refs_4_
  34.0 0.1 collective-permute-start.9
  34.0 2.5 %collective-permute-start.5 = (bf16[512,256]{1,0:T(8,128)(2,1)}, bf16[512,256]{1,0:T(8,128)(2,1)S(1)}, u32[]{:S(2)}, u32[]{:S(2)}) collective-permute-start(bf16[512,256]{1,0:T(8,128)(2,1)} %constant_dynamic-slice_fusion), channel_id=1, source_target_pairs={{0,3},{1,2},{2,1},{3,0},{4,7},{5,6},{6,5},{7,4},{8,11},{9,10},{10,... | collective-permute-start | bytes 786440 | tf_op jit(solution)/shard_map/ppermute | solution.py:332
  36.5 2.5 %collective-permute-start.10 = (bf16[512,256]{1,0:T(8,128)(2,1)S(1)}, bf16[512,256]{1,0:T(8,128)(2,1)S(1)}, u32[]{:S(2)}, u32[]{:S(2)}) collective-permute-start(bf16[512,256]{1,0:T(8,128)(2,1)S(1)} %collective-permute-done.7.refs_3_), channel_id=1, source_target_pairs={{0,16},{4,12},{8,24},{12,4},{16,0},{20,28},{24,8},{28,20},{1,17},{... | collective-permute-start | bytes 786440 | tf_op jit(solution)/shard_map/ppermute | solution.py:313
  39.0 0.0 collective-permute-start.11
  39.1 0.0 collective-permute-done.2.other_ref
  39.1 0.1 blend_states.3
  39.1 2.1 %collective-permute-start.3 = (f32[16,2048]{1,0:T(8,128)S(1)}, f32[16,2048]{1,0:T(8,128)S(1)}, u32[]{:S(2)}, u32[]{:S(2)}) collective-permute-start(f32[16,2048]{1,0:T(8,128)S(1)} %get-tuple-element.42), channel_id=1, source_target_pairs={{0,16},{4,20},{8,24},{12,28},{16,0},{20,4},{24,8},{28,12},{1,17},{... | collective-permute-start | bytes 393224 | tf_op jit(solution)/shard_map/ppermute | solution.py:274
  41.2 7.8 %collective-permute-done.3.other_ref = f32[16,2048]{1,0:T(8,128)S(1)} collective-permute-done((f32[16,2048]{1,0:T(8,128)S(1)}, f32[16,2048]{1,0:T(8,128)S(1)}, u32[]{:S(2)}, u32[]{:S(2)}) %collective-permute-start.3) | collective-permute-done | bytes 131104 | tf_op jit(solution)/shard_map/ppermute | solution.py:274
  49.0 0.0 copy-done.7
  49.0 0.0 copy-done.1
  49.0 1.9 %gate.1.refs_0_ = bf16[128,2048]{1,0:T(8,128)(2,1)S(1)} custom-call(s32[1]{0:T(128)} %bitcast.13.where_ref, bf16[128,2048]{1,0:T(8,128)(2,1)S(1)} %bitcast.20, f32[8,2048]{1,0:T(8,128)S(1)} %collective-permute-done.halo_ref, f32[3,3,2048]{2,1,0:T(4,128)S(1)} %copy-done.6, bf16[128,2048]{1,0:T(8,128)(2,1)S(1)} %get-tuple-element.35.kv_ref, ...), custom_call_target="tpu_custom_call" | custom-call | tf_op jit(solution)/shard_map/gate/pallas_call | solution.py:286
  50.9 0.1 collective-permute-start.4
  51.0 0.0 collective-permute-done.9.refs_8_
  51.0 1.7 %collective-permute-start.14 = (bf16[512,256]{1,0:T(8,128)(2,1)S(1)}, bf16[512,256]{1,0:T(8,128)(2,1)S(1)}, u32[]{:S(2)}, u32[]{:S(2)}) collective-permute-start(bf16[512,256]{1,0:T(8,128)(2,1)S(1)} %collective-permute-done.6.refs_7_), channel_id=1, source_target_pairs={{0,16},{4,12},{8,24},{12,4},{16,0},{20,28},{24,8},{28,20},{1,17},{... | collective-permute-start | bytes 786440 | tf_op jit(solution)/shard_map/ppermute | solution.py:313
  52.7 0.0 collective-permute-done.5.refs_2_
  52.7 0.4 collective-permute-start.15
  53.1 0.0 collective-permute-done.10.refs_5_
  53.1 0.0 collective-permute-done.11.refs_6_
  53.1 1.5 %collective-permute-start.12 = (bf16[512,256]{1,0:T(8,128)(2,1)S(1)}, bf16[512,256]{1,0:T(8,128)(2,1)}, u32[]{:S(2)}, u32[]{:S(2)}) collective-permute-start(bf16[512,256]{1,0:T(8,128)(2,1)S(1)} %collective-permute-done.5.refs_2_), channel_id=1, source_target_pairs={{0,8},{4,20},{8,0},{12,28},{16,24},{20,4},{24,16},{28,12},{1,9},{5... | collective-permute-start | bytes 786440 | tf_op jit(solution)/shard_map/ppermute | solution.py:313
  54.6 0.6 collective-permute-start.13
  55.2 4.1 %collective-permute-done.14.refs_9_ = bf16[512,256]{1,0:T(8,128)(2,1)S(1)} collective-permute-done((bf16[512,256]{1,0:T(8,128)(2,1)S(1)}, bf16[512,256]{1,0:T(8,128)(2,1)S(1)}, u32[]{:S(2)}, u32[]{:S(2)}) %collective-permute-start.14) | collective-permute-done | bytes 262176 | tf_op jit(solution)/shard_map/ppermute | solution.py:313
  59.3 3.7 %collective-permute-done.15.refs_10_ = bf16[512,256]{1,0:T(8,128)(2,1)S(1)} collective-permute-done((bf16[512,256]{1,0:T(8,128)(2,1)S(1)}, bf16[512,256]{1,0:T(8,128)(2,1)S(1)}, u32[]{:S(2)}, u32[]{:S(2)}) %collective-permute-start.15) | collective-permute-done | bytes 262176 | tf_op jit(solution)/shard_map/ppermute | solution.py:313
  63.0 0.0 collective-permute-done.12.refs_3_
  63.0 1.6 %collective-permute-start.16 = (bf16[512,256]{1,0:T(8,128)(2,1)}, bf16[512,256]{1,0:T(8,128)(2,1)}, u32[]{:S(2)}, u32[]{:S(2)}) collective-permute-start(bf16[512,256]{1,0:T(8,128)(2,1)} %collective-permute-done.12.refs_3_), channel_id=1, source_target_pairs={{0,16},{4,12},{8,24},{12,4},{16,0},{20,28},{24,8},{28,20},{1,17},{... | collective-permute-start | bytes 786440 | tf_op jit(solution)/shard_map/ppermute | solution.py:313
  64.7 0.1 stack.51.nums_ref
  64.8 0.0 collective-permute-done.4.refs_1_
  64.8 2.6 %project_near.1.refs_6_ = f32[256,1024]{1,0:T(8,128)S(1)} custom-call(s32[12]{0:T(128)S(1)} %stack.51.nums_ref, bf16[128,2048]{1,0:T(8,128)(2,1)S(1)} %gate.1.refs_0_, bf16[128,2048]{1,0:T(8,128)(2,1)S(1)} %collective-permute-done.4.refs_1_, bf16[512,2048]{1,0:T(8,128)(2,1)} %refs_2_.1, bf16[512,256]{1,0:T(8,128)(2,1)S(1)} %collective-permute-done.7.refs_3_, ...), custom_call_target="tpu_custom_call" | custom-call | tf_op jit(solution)/shard_map/project_near/pallas_call | solution.py:405
  67.4 0.0 collective-permute-done.13.refs_4_
  67.4 2.3 %collective-permute-done.16.refs_5_ = bf16[512,256]{1,0:T(8,128)(2,1)} collective-permute-done((bf16[512,256]{1,0:T(8,128)(2,1)}, bf16[512,256]{1,0:T(8,128)(2,1)}, u32[]{:S(2)}, u32[]{:S(2)}) %collective-permute-start.16) | collective-permute-done | bytes 262176 | tf_op jit(solution)/shard_map/ppermute | solution.py:313
  69.7 1.6 %project_far.1 = (bf16[128,1024]{1,0:T(8,128)(2,1)S(1)}, bf16[128,1024]{1,0:T(8,128)(2,1)S(1)}) custom-call(s32[12]{0:T(128)S(1)} %constant_dynamic-update-slice_fusion.nums_ref, bf16[128,2048]{1,0:T(8,128)(2,1)S(1)} %gate.1.refs_0_, bf16[128,2048]{1,0:T(8,128)(2,1)S(1)} %collective-permute-done.4.refs_1_, ...), custom_call_target="tpu_custom_call" | custom-call | tf_op jit(solution)/shard_map/project_far/pallas_call | solution.py:414
  71.3 0.1 collective-permute-start.17
  71.4 1.5 %collective-permute-done.17.other_ref = bf16[128,1024]{1,0:T(8,128)(2,1)S(1)} collective-permute-done((bf16[128,1024]{1,0:T(8,128)(2,1)S(1)}, bf16[128,1024]{1,0:T(8,128)(2,1)S(1)}, u32[]{:S(2)}, u32[]{:S(2)}) %collective-permute-start.17) | collective-permute-done | bytes 262176 | tf_op jit(solution)/shard_map/ppermute | solution.py:422
  72.9 0.9 %join_columns.1 = bf16[128,2048]{1,0:T(8,128)(2,1)} custom-call(s32[1]{0:T(128)} %bitcast.nums_ref, bf16[128,1024]{1,0:T(8,128)(2,1)S(1)} %get-tuple-element.47.mine_ref, bf16[128,1024]{1,0:T(8,128)(2,1)S(1)} %collective-permute-done.17.other_ref), custom_call_target="tpu_custom_call" | custom-call | tf_op jit(solution)/shard_map/join_columns/pallas_call | solution.py:423
  (7 shorter events, 0.1 us)
Async XLA Ops:
  0.0 25.8 %copy-start.3 = (bf16[1,128,2048]{2,1,0:T(8,128)(2,1)S(1)}, bf16[1,128,2048]{2,1,0:T(8,128)(2,1)}, u32[]{:S(2)}) copy-start(bf16[1,128,2048]{2,1,0:T(8,128)(2,1)} %param.11) | copy-start | bytes 1572868
  0.0 23.0 %copy-start.8 = (f32[128,16]{0,1:T(8,128)S(1)}, f32[128,16]{0,1:T(8,128)}, u32[]{:S(2)}) copy-start(f32[128,16]{0,1:T(8,128)} %param.14) | copy-start | bytes 24580
  0.0 23.1 %copy-start.9 = (f32[128,16]{0,1:T(8,128)S(1)}, f32[128,16]{0,1:T(8,128)}, u32[]{:S(2)}) copy-start(f32[128,16]{0,1:T(8,128)} %param.15) | copy-start | bytes 24580
  1.7 15.0 %collective-permute-start.7 = (bf16[512,256]{1,0:T(8,128)(2,1)}, bf16[512,256]{1,0:T(8,128)(2,1)S(1)}, u32[]{:S(2)}, u32[]{:S(2)}) collective-permute-start(bf16[512,256]{1,0:T(8,128)(2,1)} %constant_dynamic-slice_fusion), channel_id=1, source_target_pairs={{0,1},{1,0},{2,3},{3,2},{4,5},{5,4},{6,7},{7,6},{8,9},{9,8},{10,11... | collective-permute-start | bytes 786440 | tf_op jit(solution)/shard_map/ppermute | solution.py:326
  4.8 29.2 %collective-permute-start.6 = (bf16[512,256]{1,0:T(8,128)(2,1)}, bf16[512,256]{1,0:T(8,128)(2,1)S(1)}, u32[]{:S(2)}, u32[]{:S(2)}) collective-permute-start(bf16[512,256]{1,0:T(8,128)(2,1)} %constant_dynamic-slice_fusion), channel_id=1, source_target_pairs={{0,2},{1,3},{2,0},{3,1},{4,6},{5,7},{6,4},{7,5},{8,10},{9,11},{10,... | collective-permute-start | bytes 786440 | tf_op jit(solution)/shard_map/ppermute | solution.py:331
  16.8 17.2 %collective-permute-start.8 = (bf16[512,256]{1,0:T(8,128)(2,1)S(1)}, bf16[512,256]{1,0:T(8,128)(2,1)S(1)}, u32[]{:S(2)}, u32[]{:S(2)}) collective-permute-start(bf16[512,256]{1,0:T(8,128)(2,1)S(1)} %collective-permute-done.7.refs_3_), channel_id=1, source_target_pairs={{0,8},{4,20},{8,0},{12,28},{16,24},{20,4},{24,16},{28,12},{1,9},{5... | collective-permute-start | bytes 786440 | tf_op jit(solution)/shard_map/ppermute | solution.py:313
  18.4 1.0 %copy-start = (bf16[1,128,2048]{2,1,0:T(8,128)(2,1)S(1)}, bf16[1,128,2048]{2,1,0:T(8,128)(2,1)}, u32[]{:S(2)}) copy-start(bf16[1,128,2048]{2,1,0:T(8,128)(2,1)} %param.10) | copy-start | bytes 1572868
  19.5 1.0 %copy-start.2 = (bf16[1,128,2048]{2,1,0:T(8,128)(2,1)S(1)}, bf16[1,128,2048]{2,1,0:T(8,128)(2,1)}, u32[]{:S(2)}) copy-start(bf16[1,128,2048]{2,1,0:T(8,128)(2,1)} %param.11) | copy-start | bytes 1572868
  20.5 1.0 %copy-start.4 = (bf16[1,128,2048]{2,1,0:T(8,128)(2,1)S(1)}, bf16[1,128,2048]{2,1,0:T(8,128)(2,1)}, u32[]{:S(2)}) copy-start(bf16[1,128,2048]{2,1,0:T(8,128)(2,1)} %param.12) | copy-start | bytes 1572868
  21.6 4.3 %copy-start.5 = (bf16[1,128,2048]{2,1,0:T(8,128)(2,1)S(1)}, bf16[1,128,2048]{2,1,0:T(8,128)(2,1)}, u32[]{:S(2)}) copy-start(bf16[1,128,2048]{2,1,0:T(8,128)(2,1)} %param.12) | copy-start | bytes 1572868
  21.6 27.4 %copy-start.7 = (f32[2048]{0:T(1024)S(1)}, f32[2048]{0:T(1024)}, u32[]{:S(2)}) copy-start(f32[2048]{0:T(1024)} %param.16) | copy-start | bytes 24580
  21.6 27.4 %copy-start.1 = (bf16[1,128,2048]{2,1,0:T(8,128)(2,1)S(1)}, bf16[1,128,2048]{2,1,0:T(8,128)(2,1)}, u32[]{:S(2)}) copy-start(bf16[1,128,2048]{2,1,0:T(8,128)(2,1)} %param.10) | copy-start | bytes 1572868
  21.6 4.2 %collective-permute-start = (f32[8,2048]{1,0:T(8,128)S(1)}, f32[8,2048]{1,0:T(8,128)S(1)}, u32[]{:S(2)}, u32[]{:S(2)}) collective-permute-start(f32[8,2048]{1,0:T(8,128)S(1)} %last_rows.1), channel_id=1, source_target_pairs={{0,4},{4,8},{8,12},{12,16},{16,20},{20,24},{24,28},{1,5},{5,9},{9,... | collective-permute-start | bytes 196616 | tf_op jit(solution)/shard_map/ppermute | solution.py:221
  25.8 0.9 %copy-start.6 = (f32[3,3,2048]{2,1,0:T(4,128)S(1)}, f32[3,3,2048]{2,1,0:T(4,128)}, u32[]{:S(2)}) copy-start(f32[3,3,2048]{2,1,0:T(4,128)} %taps_ref.3) | copy-start | bytes 221188
  29.0 2.2 %collective-permute-start.1 = (f32[16,2048]{1,0:T(8,128)S(1)}, f32[16,2048]{1,0:T(8,128)S(1)}, u32[]{:S(2)}, u32[]{:S(2)}) collective-permute-start(f32[16,2048]{1,0:T(8,128)S(1)} %get-tuple-element.38.state_ref), channel_id=1, source_target_pairs={{0,4},{4,0},{8,12},{12,8},{16,20},{20,16},{24,28},{28,24},{1,5},{5... | collective-permute-start | bytes 393224 | tf_op jit(solution)/shard_map/ppermute | solution.py:274
  31.3 7.8 %collective-permute-start.2 = (f32[16,2048]{1,0:T(8,128)S(1)}, f32[16,2048]{1,0:T(8,128)S(1)}, u32[]{:S(2)}, u32[]{:S(2)}) collective-permute-start(f32[16,2048]{1,0:T(8,128)S(1)} %get-tuple-element.39.state_ref), channel_id=1, source_target_pairs={{0,8},{4,12},{8,0},{12,4},{16,24},{20,28},{24,16},{28,20},{1,9},{5... | collective-permute-start | bytes 393224 | tf_op jit(solution)/shard_map/ppermute | solution.py:274
  34.0 17.0 %collective-permute-start.9 = (bf16[512,256]{1,0:T(8,128)(2,1)S(1)}, bf16[512,256]{1,0:T(8,128)(2,1)S(1)}, u32[]{:S(2)}, u32[]{:S(2)}) collective-permute-start(bf16[512,256]{1,0:T(8,128)(2,1)S(1)} %collective-permute-done.6.refs_7_), channel_id=1, source_target_pairs={{0,8},{4,20},{8,0},{12,28},{16,24},{20,4},{24,16},{28,12},{1,9},{5... | collective-permute-start | bytes 786440 | tf_op jit(solution)/shard_map/ppermute | solution.py:313
  34.0 18.6 %collective-permute-start.5 = (bf16[512,256]{1,0:T(8,128)(2,1)}, bf16[512,256]{1,0:T(8,128)(2,1)S(1)}, u32[]{:S(2)}, u32[]{:S(2)}) collective-permute-start(bf16[512,256]{1,0:T(8,128)(2,1)} %constant_dynamic-slice_fusion), channel_id=1, source_target_pairs={{0,3},{1,2},{2,1},{3,0},{4,7},{5,6},{6,5},{7,4},{8,11},{9,10},{10,... | collective-permute-start | bytes 786440 | tf_op jit(solution)/shard_map/ppermute | solution.py:332
  36.5 16.5 %collective-permute-start.10 = (bf16[512,256]{1,0:T(8,128)(2,1)S(1)}, bf16[512,256]{1,0:T(8,128)(2,1)S(1)}, u32[]{:S(2)}, u32[]{:S(2)}) collective-permute-start(bf16[512,256]{1,0:T(8,128)(2,1)S(1)} %collective-permute-done.7.refs_3_), channel_id=1, source_target_pairs={{0,16},{4,12},{8,24},{12,4},{16,0},{20,28},{24,8},{28,20},{1,17},{... | collective-permute-start | bytes 786440 | tf_op jit(solution)/shard_map/ppermute | solution.py:313
  39.0 14.1 %collective-permute-start.11 = (bf16[512,256]{1,0:T(8,128)(2,1)S(1)}, bf16[512,256]{1,0:T(8,128)(2,1)S(1)}, u32[]{:S(2)}, u32[]{:S(2)}) collective-permute-start(bf16[512,256]{1,0:T(8,128)(2,1)S(1)} %collective-permute-done.8.refs_4_), channel_id=1, source_target_pairs={{0,16},{4,12},{8,24},{12,4},{16,0},{20,28},{24,8},{28,20},{1,17},{... | collective-permute-start | bytes 786440 | tf_op jit(solution)/shard_map/ppermute | solution.py:313
  39.1 9.9 %collective-permute-start.3 = (f32[16,2048]{1,0:T(8,128)S(1)}, f32[16,2048]{1,0:T(8,128)S(1)}, u32[]{:S(2)}, u32[]{:S(2)}) collective-permute-start(f32[16,2048]{1,0:T(8,128)S(1)} %get-tuple-element.42), channel_id=1, source_target_pairs={{0,16},{4,20},{8,24},{12,28},{16,0},{20,4},{24,8},{28,12},{1,17},{... | collective-permute-start | bytes 393224 | tf_op jit(solution)/shard_map/ppermute | solution.py:274
  50.9 13.9 %collective-permute-start.4 = (bf16[128,2048]{1,0:T(8,128)(2,1)S(1)}, bf16[128,2048]{1,0:T(8,128)(2,1)S(1)}, u32[]{:S(2)}, u32[]{:S(2)}) collective-permute-start(bf16[128,2048]{1,0:T(8,128)(2,1)S(1)} %gate.1.refs_0_), channel_id=1, source_target_pairs={{0,4},{4,0},{8,12},{12,8},{16,20},{20,16},{24,28},{28,24},{1,5},{5... | collective-permute-start | bytes 1572872 | tf_op jit(solution)/shard_map/ppermute | solution.py:396
  51.0 8.3 %collective-permute-start.14 = (bf16[512,256]{1,0:T(8,128)(2,1)S(1)}, bf16[512,256]{1,0:T(8,128)(2,1)S(1)}, u32[]{:S(2)}, u32[]{:S(2)}) collective-permute-start(bf16[512,256]{1,0:T(8,128)(2,1)S(1)} %collective-permute-done.6.refs_7_), channel_id=1, source_target_pairs={{0,16},{4,12},{8,24},{12,4},{16,0},{20,28},{24,8},{28,20},{1,17},{... | collective-permute-start | bytes 786440 | tf_op jit(solution)/shard_map/ppermute | solution.py:313
  52.7 10.3 %collective-permute-start.15 = (bf16[512,256]{1,0:T(8,128)(2,1)S(1)}, bf16[512,256]{1,0:T(8,128)(2,1)S(1)}, u32[]{:S(2)}, u32[]{:S(2)}) collective-permute-start(bf16[512,256]{1,0:T(8,128)(2,1)S(1)} %collective-permute-done.9.refs_8_), channel_id=1, source_target_pairs={{0,16},{4,12},{8,24},{12,4},{16,0},{20,28},{24,8},{28,20},{1,17},{... | collective-permute-start | bytes 786440 | tf_op jit(solution)/shard_map/ppermute | solution.py:313
  53.1 10.0 %collective-permute-start.12 = (bf16[512,256]{1,0:T(8,128)(2,1)S(1)}, bf16[512,256]{1,0:T(8,128)(2,1)}, u32[]{:S(2)}, u32[]{:S(2)}) collective-permute-start(bf16[512,256]{1,0:T(8,128)(2,1)S(1)} %collective-permute-done.5.refs_2_), channel_id=1, source_target_pairs={{0,8},{4,20},{8,0},{12,28},{16,24},{20,4},{24,16},{28,12},{1,9},{5... | collective-permute-start | bytes 786440 | tf_op jit(solution)/shard_map/ppermute | solution.py:313
  54.6 12.8 %collective-permute-start.13 = (bf16[512,256]{1,0:T(8,128)(2,1)S(1)}, bf16[512,256]{1,0:T(8,128)(2,1)}, u32[]{:S(2)}, u32[]{:S(2)}) collective-permute-start(bf16[512,256]{1,0:T(8,128)(2,1)S(1)} %collective-permute-done.5.refs_2_), channel_id=1, source_target_pairs={{0,16},{4,12},{8,24},{12,4},{16,0},{20,28},{24,8},{28,20},{1,17},{... | collective-permute-start | bytes 786440 | tf_op jit(solution)/shard_map/ppermute | solution.py:313
  63.0 6.7 %collective-permute-start.16 = (bf16[512,256]{1,0:T(8,128)(2,1)}, bf16[512,256]{1,0:T(8,128)(2,1)}, u32[]{:S(2)}, u32[]{:S(2)}) collective-permute-start(bf16[512,256]{1,0:T(8,128)(2,1)} %collective-permute-done.12.refs_3_), channel_id=1, source_target_pairs={{0,16},{4,12},{8,24},{12,4},{16,0},{20,28},{24,8},{28,20},{1,17},{... | collective-permute-start | bytes 786440 | tf_op jit(solution)/shard_map/ppermute | solution.py:313
  71.3 1.6 %collective-permute-start.17 = (bf16[128,1024]{1,0:T(8,128)(2,1)S(1)}, bf16[128,1024]{1,0:T(8,128)(2,1)S(1)}, u32[]{:S(2)}, u32[]{:S(2)}) collective-permute-start(bf16[128,1024]{1,0:T(8,128)(2,1)S(1)} %get-tuple-element.48), channel_id=1, source_target_pairs={{0,4},{4,0},{8,12},{12,8},{16,20},{20,16},{24,28},{28,24},{1,5},{5... | collective-permute-start | bytes 786440 | tf_op jit(solution)/shard_map/ppermute | solution.py:422

commit v3 on v2

--- a/solution.py
+++ b/solution.py
@@ -22,8 +22,8 @@
     return lax.optimization_barrier((x,) + deps)[0]
 
 
-def params():
-    return pltpu.CompilerParams(vmem_limit_bytes=VMEM_LIMIT)
+def params(limit=VMEM_LIMIT):
+    return pltpu.CompilerParams(vmem_limit_bytes=limit)
 
 
 def split(x):
@@ -63,19 +63,18 @@
     sub = left_ref.shape[1] // 2 - modes
     each = groups // blocks
 
-    def expand(table, width, count, first):
-        pick = iota((groups, count), 0) == first + iota((groups, count), 1) // width
-        return lax.dot_general(
-            table,
-            pick.astype(f32),
-            (((0,), (0,)), ((), ())),
-            precision=lax.Precision.HIGHEST,
-            preferred_element_type=f32,
-        )
-
-    rate_chan_ref[...] = expand(rate, GROUP, groups * GROUP, 0)
-    rate_wide = expand(rate, sub, groups * sub, 0)
-    scale_wide = expand(scale, sub, groups * sub, 0)
+    def expand(table, width, count):
+        pick = iota((groups, count), 0) == iota((groups, count), 1) // width
+        pick = pick.astype(bf16)
+        high = table.astype(bf16)
+        rest = table - high.astype(f32)
+        middle, low = split(rest)
+        return dot(high, pick) + (dot(middle, pick) + dot(low, pick))
+
+    rate_turned, scale_turned = rate.T, scale.T
+    rate_chan_ref[...] = expand(rate_turned, GROUP, groups * GROUP)
+    rate_wide = expand(rate_turned, sub, groups * sub)
+    scale_wide = expand(scale_turned, sub, groups * sub)
     place = iota((modes, groups * sub), 1) % sub
     back = jnp.where(place == 0, 0, sub - place).astype(f32)
     taps = jnp.sum(scale_wide * jnp.exp(-rate_wide * back), axis=0, keepdims=True)
@@ -197,31 +196,48 @@
                 out_ref[at, cols] = (query[at, cols] * (convolved + skip_ref[:, cols] * kv)).astype(bf16)
 
 
-def tail_kernel(query_ref, key_ref, value_ref, out_ref):
+def prepare_kernel(which_ref, query_ref, key_ref, value_ref, weight_ref, tail_ref, piece_ref, rows_ref, sems):
     keep = FEAT - 1
+    height = rows_ref.shape[1]
+    width = piece_ref.shape[1]
+    at = pl.multiple_of(which_ref[0] * width, width)
+    copies = [pltpu.make_async_copy(weight_ref.at[:, pl.ds(at, width)], piece_ref, sems.at[3])]
     for i, ref in enumerate((query_ref, key_ref, value_ref)):
-        rows = ref[...].astype(f32)
-        out_ref[i * keep : (i + 1) * keep] = rows[rows.shape[0] - keep :]
-    out_ref[3 * keep :] = jnp.zeros((out_ref.shape[0] - 3 * keep, out_ref.shape[1]), f32)
-
-
-def send_tails(query, key, value):
-    rows, chans = query.shape
-    count = lax.axis_size("ctx")
-    last = pl.BlockSpec((16, chans), lambda i: (rows // 16 - 1, 0))
-    tails = pl.pallas_call(
-        tail_kernel,
-        grid=(1,),
-        in_specs=[last] * 3,
-        out_specs=pl.BlockSpec((8, chans), lambda i: (0, 0)),
-        out_shape=jax.ShapeDtypeStruct((8, chans), f32),
-        compiler_params=params(),
-        name="last_rows",
-    )(query, key, value)
-    return lax.ppermute(tails, "ctx", [(i, i + 1) for i in range(count - 1)])
-
-
-def conv_path(query, key, value, halo, taps, rate, residues, skip):
+        first = ref.shape[0] - height
+        copies.append(
+            pltpu.make_async_copy(ref.at[pl.ds(first, height)], rows_ref.at[i], sems.at[i])
+        )
+    for copy in copies:
+        copy.start()
+    for copy in copies[1:]:
+        copy.wait()
+    for i in range(3):
+        tail_ref[i * keep : (i + 1) * keep] = rows_ref[i].astype(f32)[height - keep :]
+    tail_ref[3 * keep :] = jnp.zeros((tail_ref.shape[0] - 3 * keep, tail_ref.shape[1]), f32)
+    copies[0].wait()
+
+
+def prepare(query, key, value, weight):
+    chans = query.shape[1]
+    depth, cols = weight.shape
+    which = (lax.axis_index("ctx") % 8)[None].astype(jnp.int32)
+    hbm = pl.BlockSpec(memory_space=pltpu.HBM)
+    vmem = pl.BlockSpec(memory_space=pltpu.VMEM)
+    return pl.pallas_call(
+        prepare_kernel,
+        in_specs=[pl.BlockSpec(memory_space=pltpu.SMEM)] + [hbm] * 4,
+        out_specs=[vmem, vmem],
+        out_shape=[
+            jax.ShapeDtypeStruct((8, chans), f32),
+            jax.ShapeDtypeStruct((depth, cols // 8), bf16),
+        ],
+        scratch_shapes=[pltpu.VMEM((3, 16, chans), bf16), pltpu.SemaphoreType.DMA((4,))],
+        compiler_params=params(63 << 20),
+        name="prepare",
+    )(which, query, key, value, weight)
+
+
+def conv_path(query, key, value, halo, near, taps, rate, residues, skip):
     rows, chans = query.shape
     groups, modes = rate.shape
     count = lax.axis_size("ctx")
@@ -245,6 +261,8 @@
         compiler_params=params(),
         name="tables",
     )(rate, residues)
+    near = after(near, halo, left)
+    near_one, near_two = hop(near, True), hop(near, False)
 
     def wide(height):
         return pl.BlockSpec((height, WIDE), lambda b: (0, b))
@@ -270,6 +288,7 @@
     )(key, value, halo, taps, left, rate_chan)
     enter = jnp.zeros_like(state)
     step = 1
+    states = [state]
     while True:
         other = lax.ppermute(state, "ctx", [(i, i ^ step) for i in range(count)])
         if 2 * step >= count:
@@ -283,7 +302,8 @@
             name="blend_states",
         )(here, state, other, enter, rate_chan)
         step *= 2
-    return pl.pallas_call(
+        states.append(state)
+    gated = pl.pallas_call(
         functools.partial(gate_kernel, step),
         grid=(steps,),
         in_specs=[
@@ -305,6 +325,7 @@
         compiler_params=params(),
         name="gate",
     )(here, query, halo, taps, kv, inner, before, enter, other, rate_chan, lag, skip[None])
+    return gated, states, (near, near_one, near_two)
 
 
 def hop(x, first):
@@ -313,27 +334,25 @@
     return lax.ppermute(x, "ctx", [(i, i ^ (odd if i % 2 else even)) for i in range(count)])
 
 
-def spread_slot(piece, *first):
-    one, two = hop(piece, True), hop(piece, False)
-    return piece, one, two, hop(after(one, *first), False)
-
-
-def send_weight(weight):
-    index = lax.axis_index("ctx")
-    depth, cols = weight.shape
-    block = cols // 8
-    mine = lax.dynamic_slice(weight, (0, (index % 8) * block), (depth, block))
+def send_weight(mine):
     near = lax.ppermute(mine, "fsdp", [(i, i ^ 1) for i in range(4)])
-    return mine, near
-
-
-def gather_weight(mine, near):
     two = lax.ppermute(mine, "fsdp", [(i, i ^ 2) for i in range(4)])
-    three = lax.ppermute(mine, "fsdp", [(i, i ^ 3) for i in range(4)])
-    slot_one = spread_slot(near)
-    slot_two = spread_slot(after(two, slot_one[1]))
-    slot_three = spread_slot(after(three, slot_two[1], *slot_one), *slot_two)
-    return slot_one, slot_two, slot_three
+    three = lax.ppermute(after(mine, near), "fsdp", [(i, i ^ 3) for i in range(4)])
+    return near, two, three
+
+
+def spread_weight(near, two, three, states):
+    near, one, side = near
+    corner = hop(after(one, states[1]), False)
+    slot_one = (near, one, side, corner)
+    two = after(two, states[1])
+    one, side = hop(two, True), hop(two, False)
+    corner = hop(after(one, states[-1]), False)
+    slot_two = (two, one, side, corner)
+    three = after(three, states[-1])
+    one, side = hop(three, True), hop(three, False)
+    corner = hop(after(one, *slot_two), False)
+    return slot_one, slot_two, (three, one, side, corner)
 
 
 def matmul_kernel(slot_count, has_own, has_acc, last, nums_ref, *refs):
@@ -432,10 +451,14 @@
 
 def local(query_in, key_in, value_in, feature_taps, decay_rate, residues, skip_gain, out_weight):
     query, key, value = query_in[0], key_in[0], value_in[0]
-    mine, near = send_weight(out_weight)
-    halo = send_tails(query, key, value)
-    gated = conv_path(query, key, value, halo, feature_taps, decay_rate, residues, skip_gain)
-    return project(gated, out_weight, gather_weight(mine, near))[None]
+    tails, mine = prepare(query, key, value, out_weight)
+    count = lax.axis_size("ctx")
+    halo = lax.ppermute(tails, "ctx", [(i, i + 1) for i in range(count - 1)])
+    near, two, three = send_weight(mine)
+    gated, states, near = conv_path(
+        query, key, value, halo, near, feature_taps, decay_rate, residues, skip_gain
+    )
+    return project(gated, out_weight, spread_weight(near, two, three, states))[None]
 
 
 def solution(mesh):

time: 74.1 us -> 57.6 us (0.78)
  waiting for transfers between devices: 29.9 us -> 16.9 us
  local copies, waits for them, and re-layouts: 6.08 us -> 1.38 us
  Pallas kernels: 11.9 us -> 13.1 us
    ppermute x1, waiting for transfers between devices: 9.41 us -> 0.01 us  [send_weight(): near = lax.ppermute(mine, 'fsdp', [(i, i ^ 1) for i in range(4)])]
    ppermute x3, waiting for transfers between devices: 8.78 us -> 4.42 us  [conv_path(): other = lax.ppermute(state, 'ctx', [(i, i ^ step) for i in range(count)])]
    unnamed x22 -> x18, local copies, waits for them, and re-layouts: 4.24 us -> 1.27 us
    ppermute x3, starting transfers between devices: 6.51 us -> 8.69 us  [the longest x1 4.13 us: send_weight(): two = lax.ppermute(mine, 'fsdp', [(i, i ^ 2) for i in range(4)])]
    pallas_call x1, Pallas kernels: 0.02 us -> 1.83 us  [prepare(): pl.pallas_call(prepare_kernel, in_specs=[pl.BlockSpec(memory_space=pltpu....]
    dynamic_slice x1 -> x0, local copies, waits for them, and re-layouts: 1.73 us -> none  [send_weight(): mine = lax.dynamic_slice(weight, (0, index % 8 * block), (depth, block))]
    ppermute x9, starting transfers between devices: 10.1 us -> 8.51 us  [hop(): lax.ppermute(x, 'ctx', [(i, i ^ (odd if i % 2 else even)) for i in range(...]
    ppermute x1, starting transfers between devices: 3.05 us -> 1.58 us  [send_weight(): near = lax.ppermute(mine, 'fsdp', [(i, i ^ 1) for i in range(4)])]
  transfers between devices with their start and end apart: 18 -> 18, of which waited for: 7 -> 9; matrix products, arithmetic and copies ran while one was open for 0% -> 1% of each run, Pallas kernels for 13% -> 15%
where the time goes in v3:
time: 57.6 us; the launch traced here: 57.4 us
  starting transfers between devices  25.9 us (45%)
  waiting for transfers between devices  16.9 us (29%)
  Pallas kernels  13.1 us (23%)
  local copies, waits for them, and re-layouts  1.38 us (2%)
    ppermute x9, waiting for transfers between devices, hop(): lax.ppermute(x, 'ctx', [(i, i ^ (odd if i % 2 else even)) for i in range(...  10.9 us
    ppermute x9, starting transfers between devices, hop(): lax.ppermute(x, 'ctx', [(i, i ^ (odd if i % 2 else even)) for i in range(...  8.51 us
    ppermute x3, starting transfers between devices, conv_path(): other = lax.ppermute(state, 'ctx', [(i, i ^ step) for i in range(count)])  6.96 us
    ppermute x3, waiting for transfers between devices, conv_path(): other = lax.ppermute(state, 'ctx', [(i, i ^ step) for i in range(count)])  4.42 us
    ppermute x1, starting transfers between devices, send_weight(): two = lax.ppermute(mine, 'fsdp', [(i, i ^ 2) for i in range(4)])  4.13 us
    ppermute x1, starting transfers between devices, send_weight(): lax.ppermute(after(mine, near), 'fsdp', [(i, i ^ 3) for i in range(4)])  3.28 us
    pallas_call x1, Pallas kernels, project(): pl.pallas_call(functools.partial(matmul_kernel, 2, True, False, False), i...  2.58 us
    pallas_call x1, Pallas kernels, conv_path(): pl.pallas_call(product_kernel, grid=(steps,), in_specs=[wide(rows), wide(...  2.26 us
  transfers between devices with their start and end apart: 18, of which 9 were waited for; matrix products, arithmetic and copies ran while one was open for 1% of the time, Pallas kernels for 15%

profile of v3, /device:TPU:0, one launch (start us, length us, event | category | flops | bytes accessed | tf_op | source)
XLA Modules:
  0.0 57.4 jit_solution(6222306527195220718)
XLA Ops:
  0.0 0.0 copy-start.1
  0.0 0.0 copy-start.5
  0.0 0.0 copy-start.6
  0.0 0.0 copy-start.3
  0.0 0.0 copy-start.4
  0.0 1.8 %prepare.1 = (f32[8,2048]{1,0:T(8,128)}, bf16[512,256]{1,0:T(8,128)(2,1)}) custom-call(s32[1]{0:T(128)} %bitcast.5.which_ref, bf16[128,2048]{1,0:T(8,128)(2,1)} %bitcast.19, bf16[128,2048]{1,0:T(8,128)(2,1)} %bitcast.21, bf16[128,2048]{1,0:T(8,128)(2,1)} %bitcast.23, bf16[512,2048]{1,0:T(8,128)(2,1)} %refs_2_.1), custom_call_target="tpu_custom_call" | custom-call | tf_op jit(solution)/shard_map/prepare/pallas_call | solution.py:226
  1.8 0.0 copy-start
  1.9 4.1 %collective-permute-start.9 = (bf16[512,256]{1,0:T(8,128)(2,1)}, bf16[512,256]{1,0:T(8,128)(2,1)S(1)}, u32[]{:S(2)}, u32[]{:S(2)}) collective-permute-start(bf16[512,256]{1,0:T(8,128)(2,1)} %get-tuple-element.52), channel_id=1, source_target_pairs={{0,2},{1,3},{2,0},{3,1},{4,6},{5,7},{6,4},{7,5},{8,10},{9,11},{10,... | collective-permute-start | bytes 786440 | tf_op jit(solution)/shard_map/ppermute | solution.py:339
  6.0 1.6 %collective-permute-start.5 = (bf16[512,256]{1,0:T(8,128)(2,1)}, bf16[512,256]{1,0:T(8,128)(2,1)S(1)}, u32[]{:S(2)}, u32[]{:S(2)}) collective-permute-start(bf16[512,256]{1,0:T(8,128)(2,1)} %get-tuple-element.52), channel_id=1, source_target_pairs={{0,1},{1,0},{2,3},{3,2},{4,5},{5,4},{6,7},{7,6},{8,9},{9,8},{10,11... | collective-permute-start | bytes 786440 | tf_op jit(solution)/shard_map/ppermute | solution.py:338
  7.6 1.3 %collective-permute-start = (f32[8,2048]{1,0:T(8,128)}, f32[8,2048]{1,0:T(8,128)S(1)}, u32[]{:S(2)}, u32[]{:S(2)}) collective-permute-start(f32[8,2048]{1,0:T(8,128)} %get-tuple-element.39), channel_id=1, source_target_pairs={{0,4},{4,8},{8,12},{12,16},{16,20},{20,24},{24,28},{1,5},{5,9},{9,... | collective-permute-start | bytes 196616 | tf_op jit(solution)/shard_map/ppermute | solution.py:456
  8.9 0.0 copy-done.5
  8.9 0.1 copy.9.rate_ref
  9.0 0.0 copy-done.6
  9.0 0.1 copy.10.residue_ref
  9.1 2.0 %tables.1 = (bf16[16,96,256]{2,1,0:T(8,128)(2,1)S(1)}, bf16[16,64,256]{2,1,0:T(8,128)(2,1)S(1)}, f32[16,2048]{1,0:T(8,128)S(1)}) custom-call(f32[128,16]{1,0:T(8,128)S(1)} %copy.9.rate_ref, f32[128,16]{1,0:T(8,128)S(1)} %copy.10.residue_ref), custom_call_target="tpu_custom_call" | custom-call | tf_op jit(solution)/shard_map/tables/pallas_call | solution.py:252
  11.0 0.0 collective-permute-done.halo_ref
  11.1 0.0 copy-done.1
  11.1 0.0 copy-done.3
  11.1 0.0 copy-start.2
  11.1 1.0 %copy-done.2 = bf16[1,128,2048]{2,1,0:T(8,128)(2,1)S(1)} copy-done((bf16[1,128,2048]{2,1,0:T(8,128)(2,1)S(1)}, bf16[1,128,2048]{2,1,0:T(8,128)(2,1)}, u32[]{:S(2)}) %copy-start.2) | copy-done | bytes 524312
  12.1 0.0 copy-start.7
  12.1 2.3 %kv_and_state.1 = (bf16[128,2048]{1,0:T(8,128)(2,1)S(1)}, f32[128,2048]{1,0:T(8,128)S(1)}, f32[64,2048]{1,0:T(8,128)S(1)}, f32[16,2048]{1,0:T(8,128)S(1)}) custom-call(bf16[128,2048]{1,0:T(8,128)(2,1)S(1)} %bitcast.22, bf16[128,2048]{1,0:T(8,128)(2,1)S(1)} %bitcast.24, f32[8,2048]{1,0:T(8,128)S(1)} %collective-permute-done.halo_ref, ...), custom_call_target="tpu_custom_call" | custom-call | tf_op jit(solution)/shard_map/kv_and_state/pallas_call | solution.py:275
  14.4 2.3 %collective-permute-start.1 = (f32[16,2048]{1,0:T(8,128)S(1)}, f32[16,2048]{1,0:T(8,128)S(1)}, u32[]{:S(2)}, u32[]{:S(2)}) collective-permute-start(f32[16,2048]{1,0:T(8,128)S(1)} %get-tuple-element.45.state_ref), channel_id=1, source_target_pairs={{0,4},{4,0},{8,12},{12,8},{16,20},{20,16},{24,28},{28,24},{1,5},{5... | collective-permute-start | bytes 393224 | tf_op jit(solution)/shard_map/ppermute | solution.py:293
  16.7 1.0 %collective-permute-done.1.other_ref = f32[16,2048]{1,0:T(8,128)S(1)} collective-permute-done((f32[16,2048]{1,0:T(8,128)S(1)}, f32[16,2048]{1,0:T(8,128)S(1)}, u32[]{:S(2)}, u32[]{:S(2)}) %collective-permute-start.1) | collective-permute-done | bytes 131104 | tf_op jit(solution)/shard_map/ppermute | solution.py:293
  17.7 0.1 blend_states.2
  17.8 2.0 %collective-permute-start.2 = (f32[16,2048]{1,0:T(8,128)S(1)}, f32[16,2048]{1,0:T(8,128)S(1)}, u32[]{:S(2)}, u32[]{:S(2)}) collective-permute-start(f32[16,2048]{1,0:T(8,128)S(1)} %get-tuple-element.46.state_ref), channel_id=1, source_target_pairs={{0,8},{4,12},{8,0},{12,4},{16,24},{20,28},{24,16},{28,20},{1,9},{5... | collective-permute-start | bytes 393224 | tf_op jit(solution)/shard_map/ppermute | solution.py:293
  19.7 0.0 collective-permute-done.9.refs_7_
  19.7 0.1 collective-permute-start.10
  19.9 0.0 collective-permute-done.5.refs_3_
  19.9 0.0 copy-done.7
  19.9 3.3 %collective-permute-start.6 = (bf16[512,256]{1,0:T(8,128)(2,1)S(1)}, bf16[512,256]{1,0:T(8,128)(2,1)}, u32[]{:S(2)}, u32[]{:S(2)}) collective-permute-start(bf16[512,256]{1,0:T(8,128)(2,1)S(1)} %copy-done.7), channel_id=1, source_target_pairs={{0,3},{1,2},{2,1},{3,0},{4,7},{5,6},{6,5},{7,4},{8,11},{9,10},{10,... | collective-permute-start | bytes 786440 | tf_op jit(solution)/shard_map/ppermute | solution.py:340
  23.2 0.4 collective-permute-done.2.other_ref
  23.6 0.1 blend_states.3
  23.7 2.7 %collective-permute-start.3 = (f32[16,2048]{1,0:T(8,128)S(1)}, f32[16,2048]{1,0:T(8,128)S(1)}, u32[]{:S(2)}, u32[]{:S(2)}) collective-permute-start(f32[16,2048]{1,0:T(8,128)S(1)} %get-tuple-element.49), channel_id=1, source_target_pairs={{0,16},{4,20},{8,24},{12,28},{16,0},{20,4},{24,8},{28,12},{1,17},{... | collective-permute-start | bytes 393224 | tf_op jit(solution)/shard_map/ppermute | solution.py:293
  26.4 0.1 collective-permute-start.11
  26.4 1.0 %collective-permute-start.14 = (bf16[512,256]{1,0:T(8,128)(2,1)S(1)}, bf16[512,256]{1,0:T(8,128)(2,1)}, u32[]{:S(2)}, u32[]{:S(2)}) collective-permute-start(bf16[512,256]{1,0:T(8,128)(2,1)S(1)} %collective-permute-done.5.refs_3_), channel_id=1, source_target_pairs={{0,8},{4,20},{8,0},{12,28},{16,24},{20,4},{24,16},{28,12},{1,9},{5... | collective-permute-start | bytes 786440 | tf_op jit(solution)/shard_map/ppermute | solution.py:334
  27.5 3.0 %collective-permute-done.3.other_ref = f32[16,2048]{1,0:T(8,128)S(1)} collective-permute-done((f32[16,2048]{1,0:T(8,128)S(1)}, f32[16,2048]{1,0:T(8,128)S(1)}, u32[]{:S(2)}, u32[]{:S(2)}) %collective-permute-start.3) | collective-permute-done | bytes 131104 | tf_op jit(solution)/shard_map/ppermute | solution.py:293
  30.5 0.0 copy-done.4
  30.5 0.0 copy-done
  30.5 1.9 %gate.1.refs_0_ = bf16[128,2048]{1,0:T(8,128)(2,1)S(1)} custom-call(s32[1]{0:T(128)} %bitcast.13.where_ref, bf16[128,2048]{1,0:T(8,128)(2,1)S(1)} %bitcast.20, f32[8,2048]{1,0:T(8,128)S(1)} %collective-permute-done.halo_ref, f32[3,3,2048]{2,1,0:T(4,128)S(1)} %copy-done.3, bf16[128,2048]{1,0:T(8,128)(2,1)S(1)} %get-tuple-element.42.kv_ref, ...), custom_call_target="tpu_custom_call" | custom-call | tf_op jit(solution)/shard_map/gate/pallas_call | solution.py:306
  32.4 0.1 collective-permute-start.4
  32.4 0.0 collective-permute-done.10.refs_8_
  32.5 2.4 %collective-permute-start.12 = (bf16[512,256]{1,0:T(8,128)(2,1)S(1)}, bf16[512,256]{1,0:T(8,128)(2,1)S(1)}, u32[]{:S(2)}, u32[]{:S(2)}) collective-permute-start(bf16[512,256]{1,0:T(8,128)(2,1)S(1)} %collective-permute-done.10.refs_8_), channel_id=1, source_target_pairs={{0,16},{4,12},{8,24},{12,4},{16,0},{20,28},{24,8},{28,20},{1,17},{... | collective-permute-start | bytes 786440 | tf_op jit(solution)/shard_map/ppermute | solution.py:334
  34.9 0.0 collective-permute-done.6.refs_2_
  34.9 0.6 %collective-permute-start.7 = (bf16[512,256]{1,0:T(8,128)(2,1)}, bf16[512,256]{1,0:T(8,128)(2,1)S(1)}, u32[]{:S(2)}, u32[]{:S(2)}) collective-permute-start(bf16[512,256]{1,0:T(8,128)(2,1)} %collective-permute-done.6.refs_2_), channel_id=1, source_target_pairs={{0,8},{4,20},{8,0},{12,28},{16,24},{20,4},{24,16},{28,12},{1,9},{5... | collective-permute-start | bytes 786440 | tf_op jit(solution)/shard_map/ppermute | solution.py:334
  35.5 0.0 collective-permute-done.14.refs_4_
  35.5 0.1 collective-permute-start.15
  35.5 0.0 collective-permute-done.11.refs_9_
  35.5 1.9 %collective-permute-start.8 = (bf16[512,256]{1,0:T(8,128)(2,1)}, bf16[512,256]{1,0:T(8,128)(2,1)}, u32[]{:S(2)}, u32[]{:S(2)}) collective-permute-start(bf16[512,256]{1,0:T(8,128)(2,1)} %collective-permute-done.6.refs_2_), channel_id=1, source_target_pairs={{0,16},{4,12},{8,24},{12,4},{16,0},{20,28},{24,8},{28,20},{1,17},{... | collective-permute-start | bytes 786440 | tf_op jit(solution)/shard_map/ppermute | solution.py:334
  37.5 4.3 %collective-permute-done.12.refs_10_ = bf16[512,256]{1,0:T(8,128)(2,1)S(1)} collective-permute-done((bf16[512,256]{1,0:T(8,128)(2,1)S(1)}, bf16[512,256]{1,0:T(8,128)(2,1)S(1)}, u32[]{:S(2)}, u32[]{:S(2)}) %collective-permute-start.12) | collective-permute-done | bytes 262176 | tf_op jit(solution)/shard_map/ppermute | solution.py:334
  41.8 2.3 %collective-permute-start.16 = (bf16[512,256]{1,0:T(8,128)(2,1)}, bf16[512,256]{1,0:T(8,128)(2,1)S(1)}, u32[]{:S(2)}, u32[]{:S(2)}) collective-permute-start(bf16[512,256]{1,0:T(8,128)(2,1)} %collective-permute-done.14.refs_4_), channel_id=1, source_target_pairs={{0,16},{4,12},{8,24},{12,4},{16,0},{20,28},{24,8},{28,20},{1,17},{... | collective-permute-start | bytes 786440 | tf_op jit(solution)/shard_map/ppermute | solution.py:334
  44.0 0.3 collective-permute-done.7.refs_3_
  44.3 0.0 collective-permute-start.13
  44.3 0.1 stack.51.nums_ref
  44.4 0.4 collective-permute-done.15.refs_5_
  44.8 5.6 %collective-permute-done.16.refs_6_ = bf16[512,256]{1,0:T(8,128)(2,1)S(1)} collective-permute-done((bf16[512,256]{1,0:T(8,128)(2,1)}, bf16[512,256]{1,0:T(8,128)(2,1)S(1)}, u32[]{:S(2)}, u32[]{:S(2)}) %collective-permute-start.16) | collective-permute-done | bytes 262176 | tf_op jit(solution)/shard_map/ppermute | solution.py:334
  50.4 0.0 collective-permute-done.4.refs_1_
  50.4 2.6 %project_near.1.refs_6_ = f32[256,1024]{1,0:T(8,128)S(1)} custom-call(s32[12]{0:T(128)S(1)} %stack.51.nums_ref, bf16[128,2048]{1,0:T(8,128)(2,1)S(1)} %gate.1.refs_0_, bf16[128,2048]{1,0:T(8,128)(2,1)S(1)} %collective-permute-done.4.refs_1_, bf16[512,2048]{1,0:T(8,128)(2,1)} %refs_2_.1, bf16[512,256]{1,0:T(8,128)(2,1)S(1)} %collective-permute-done.5.refs_3_, ...), custom_call_target="tpu_custom_call" | custom-call | tf_op jit(solution)/shard_map/project_near/pallas_call | solution.py:424
  53.1 0.0 collective-permute-done.8.refs_4_
  53.1 0.3 collective-permute-done.13.refs_5_
  53.4 1.6 %project_far.1 = (bf16[128,1024]{1,0:T(8,128)(2,1)S(1)}, bf16[128,1024]{1,0:T(8,128)(2,1)S(1)}) custom-call(s32[12]{0:T(128)S(1)} %constant_dynamic-update-slice_fusion.nums_ref, bf16[128,2048]{1,0:T(8,128)(2,1)S(1)} %gate.1.refs_0_, bf16[128,2048]{1,0:T(8,128)(2,1)S(1)} %collective-permute-done.4.refs_1_, bf16[512,256]{1,0:T(8,128)(2,1)} %collective-permute-done.6.refs_2_, ...), custom_call_target="tpu_custom_call" | custom-call | tf_op jit(solution)/shard_map/project_far/pallas_call | solution.py:433
  54.9 0.1 collective-permute-start.17
  55.0 1.5 %collective-permute-done.17.other_ref = bf16[128,1024]{1,0:T(8,128)(2,1)S(1)} collective-permute-done((bf16[128,1024]{1,0:T(8,128)(2,1)S(1)}, bf16[128,1024]{1,0:T(8,128)(2,1)S(1)}, u32[]{:S(2)}, u32[]{:S(2)}) %collective-permute-start.17) | collective-permute-done | bytes 262176 | tf_op jit(solution)/shard_map/ppermute | solution.py:441
  56.5 0.9 %join_columns.1 = bf16[128,2048]{1,0:T(8,128)(2,1)} custom-call(s32[1]{0:T(128)} %bitcast.nums_ref, bf16[128,1024]{1,0:T(8,128)(2,1)S(1)} %get-tuple-element.59.mine_ref, bf16[128,1024]{1,0:T(8,128)(2,1)S(1)} %collective-permute-done.17.other_ref), custom_call_target="tpu_custom_call" | custom-call | tf_op jit(solution)/shard_map/join_columns/pallas_call | solution.py:442
  (2 shorter events, 0.0 us)
Async XLA Ops:
  0.0 11.1 %copy-start.1 = (bf16[1,128,2048]{2,1,0:T(8,128)(2,1)S(1)}, bf16[1,128,2048]{2,1,0:T(8,128)(2,1)}, u32[]{:S(2)}) copy-start(bf16[1,128,2048]{2,1,0:T(8,128)(2,1)} %param.11) | copy-start | bytes 1572868
  0.0 8.9 %copy-start.5 = (f32[128,16]{0,1:T(8,128)S(1)}, f32[128,16]{0,1:T(8,128)}, u32[]{:S(2)}) copy-start(f32[128,16]{0,1:T(8,128)} %param.14) | copy-start | bytes 24580
  0.0 9.0 %copy-start.6 = (f32[128,16]{0,1:T(8,128)S(1)}, f32[128,16]{0,1:T(8,128)}, u32[]{:S(2)}) copy-start(f32[128,16]{0,1:T(8,128)} %param.15) | copy-start | bytes 24580
  0.0 11.1 %copy-start.3 = (f32[3,3,2048]{2,1,0:T(4,128)S(1)}, f32[3,3,2048]{2,1,0:T(4,128)}, u32[]{:S(2)}) copy-start(f32[3,3,2048]{2,1,0:T(4,128)} %taps_ref.3) | copy-start | bytes 221188
  0.0 30.5 %copy-start.4 = (f32[2048]{0:T(1024)S(1)}, f32[2048]{0:T(1024)}, u32[]{:S(2)}) copy-start(f32[2048]{0:T(1024)} %param.16) | copy-start | bytes 24580
  1.8 28.6 %copy-start = (bf16[1,128,2048]{2,1,0:T(8,128)(2,1)S(1)}, bf16[1,128,2048]{2,1,0:T(8,128)(2,1)}, u32[]{:S(2)}) copy-start(bf16[1,128,2048]{2,1,0:T(8,128)(2,1)} %param.10) | copy-start | bytes 1572868
  1.9 17.9 %collective-permute-start.9 = (bf16[512,256]{1,0:T(8,128)(2,1)}, bf16[512,256]{1,0:T(8,128)(2,1)S(1)}, u32[]{:S(2)}, u32[]{:S(2)}) collective-permute-start(bf16[512,256]{1,0:T(8,128)(2,1)} %get-tuple-element.52), channel_id=1, source_target_pairs={{0,2},{1,3},{2,0},{3,1},{4,6},{5,7},{6,4},{7,5},{8,10},{9,11},{10,... | collective-permute-start | bytes 786440 | tf_op jit(solution)/shard_map/ppermute | solution.py:339
  6.0 13.9 %collective-permute-start.5 = (bf16[512,256]{1,0:T(8,128)(2,1)}, bf16[512,256]{1,0:T(8,128)(2,1)S(1)}, u32[]{:S(2)}, u32[]{:S(2)}) collective-permute-start(bf16[512,256]{1,0:T(8,128)(2,1)} %get-tuple-element.52), channel_id=1, source_target_pairs={{0,1},{1,0},{2,3},{3,2},{4,5},{5,4},{6,7},{7,6},{8,9},{9,8},{10,11... | collective-permute-start | bytes 786440 | tf_op jit(solution)/shard_map/ppermute | solution.py:338
  7.6 3.5 %collective-permute-start = (f32[8,2048]{1,0:T(8,128)}, f32[8,2048]{1,0:T(8,128)S(1)}, u32[]{:S(2)}, u32[]{:S(2)}) collective-permute-start(f32[8,2048]{1,0:T(8,128)} %get-tuple-element.39), channel_id=1, source_target_pairs={{0,4},{4,8},{8,12},{12,16},{16,20},{20,24},{24,28},{1,5},{5,9},{9,... | collective-permute-start | bytes 196616 | tf_op jit(solution)/shard_map/ppermute | solution.py:456
  11.1 1.0 %copy-start.2 = (bf16[1,128,2048]{2,1,0:T(8,128)(2,1)S(1)}, bf16[1,128,2048]{2,1,0:T(8,128)(2,1)}, u32[]{:S(2)}) copy-start(bf16[1,128,2048]{2,1,0:T(8,128)(2,1)} %param.12) | copy-start | bytes 1572868
  12.1 7.8 %copy-start.7 = (bf16[512,256]{1,0:T(8,128)(2,1)S(1)}, bf16[512,256]{1,0:T(8,128)(2,1)}, u32[]{:S(2)}) copy-start(bf16[512,256]{1,0:T(8,128)(2,1)} %get-tuple-element.52) | copy-start | bytes 786436
  14.4 3.3 %collective-permute-start.1 = (f32[16,2048]{1,0:T(8,128)S(1)}, f32[16,2048]{1,0:T(8,128)S(1)}, u32[]{:S(2)}, u32[]{:S(2)}) collective-permute-start(f32[16,2048]{1,0:T(8,128)S(1)} %get-tuple-element.45.state_ref), channel_id=1, source_target_pairs={{0,4},{4,0},{8,12},{12,8},{16,20},{20,16},{24,28},{28,24},{1,5},{5... | collective-permute-start | bytes 393224 | tf_op jit(solution)/shard_map/ppermute | solution.py:293
  17.8 5.8 %collective-permute-start.2 = (f32[16,2048]{1,0:T(8,128)S(1)}, f32[16,2048]{1,0:T(8,128)S(1)}, u32[]{:S(2)}, u32[]{:S(2)}) collective-permute-start(f32[16,2048]{1,0:T(8,128)S(1)} %get-tuple-element.46.state_ref), channel_id=1, source_target_pairs={{0,8},{4,12},{8,0},{12,4},{16,24},{20,28},{24,16},{28,20},{1,9},{5... | collective-permute-start | bytes 393224 | tf_op jit(solution)/shard_map/ppermute | solution.py:293
  19.7 12.7 %collective-permute-start.10 = (bf16[512,256]{1,0:T(8,128)(2,1)S(1)}, bf16[512,256]{1,0:T(8,128)(2,1)S(1)}, u32[]{:S(2)}, u32[]{:S(2)}) collective-permute-start(bf16[512,256]{1,0:T(8,128)(2,1)S(1)} %collective-permute-done.9.refs_7_), channel_id=1, source_target_pairs={{0,8},{4,20},{8,0},{12,28},{16,24},{20,4},{24,16},{28,12},{1,9},{5... | collective-permute-start | bytes 786440 | tf_op jit(solution)/shard_map/ppermute | solution.py:334
  19.9 15.0 %collective-permute-start.6 = (bf16[512,256]{1,0:T(8,128)(2,1)S(1)}, bf16[512,256]{1,0:T(8,128)(2,1)}, u32[]{:S(2)}, u32[]{:S(2)}) collective-permute-start(bf16[512,256]{1,0:T(8,128)(2,1)S(1)} %copy-done.7), channel_id=1, source_target_pairs={{0,3},{1,2},{2,1},{3,0},{4,7},{5,6},{6,5},{7,4},{8,11},{9,10},{10,... | collective-permute-start | bytes 786440 | tf_op jit(solution)/shard_map/ppermute | solution.py:340
  23.7 6.8 %collective-permute-start.3 = (f32[16,2048]{1,0:T(8,128)S(1)}, f32[16,2048]{1,0:T(8,128)S(1)}, u32[]{:S(2)}, u32[]{:S(2)}) collective-permute-start(f32[16,2048]{1,0:T(8,128)S(1)} %get-tuple-element.49), channel_id=1, source_target_pairs={{0,16},{4,20},{8,24},{12,28},{16,0},{20,4},{24,8},{28,12},{1,17},{... | collective-permute-start | bytes 393224 | tf_op jit(solution)/shard_map/ppermute | solution.py:293
  26.4 9.2 %collective-permute-start.11 = (bf16[512,256]{1,0:T(8,128)(2,1)S(1)}, bf16[512,256]{1,0:T(8,128)(2,1)S(1)}, u32[]{:S(2)}, u32[]{:S(2)}) collective-permute-start(bf16[512,256]{1,0:T(8,128)(2,1)S(1)} %collective-permute-done.9.refs_7_), channel_id=1, source_target_pairs={{0,16},{4,12},{8,24},{12,4},{16,0},{20,28},{24,8},{28,20},{1,17},{... | collective-permute-start | bytes 786440 | tf_op jit(solution)/shard_map/ppermute | solution.py:334
  26.4 9.0 %collective-permute-start.14 = (bf16[512,256]{1,0:T(8,128)(2,1)S(1)}, bf16[512,256]{1,0:T(8,128)(2,1)}, u32[]{:S(2)}, u32[]{:S(2)}) collective-permute-start(bf16[512,256]{1,0:T(8,128)(2,1)S(1)} %collective-permute-done.5.refs_3_), channel_id=1, source_target_pairs={{0,8},{4,20},{8,0},{12,28},{16,24},{20,4},{24,16},{28,12},{1,9},{5... | collective-permute-start | bytes 786440 | tf_op jit(solution)/shard_map/ppermute | solution.py:334
  32.4 18.1 %collective-permute-start.4 = (bf16[128,2048]{1,0:T(8,128)(2,1)S(1)}, bf16[128,2048]{1,0:T(8,128)(2,1)S(1)}, u32[]{:S(2)}, u32[]{:S(2)}) collective-permute-start(bf16[128,2048]{1,0:T(8,128)(2,1)S(1)} %gate.1.refs_0_), channel_id=1, source_target_pairs={{0,4},{4,0},{8,12},{12,8},{16,20},{20,16},{24,28},{28,24},{1,5},{5... | collective-permute-start | bytes 1572872 | tf_op jit(solution)/shard_map/ppermute | solution.py:415
  32.5 9.3 %collective-permute-start.12 = (bf16[512,256]{1,0:T(8,128)(2,1)S(1)}, bf16[512,256]{1,0:T(8,128)(2,1)S(1)}, u32[]{:S(2)}, u32[]{:S(2)}) collective-permute-start(bf16[512,256]{1,0:T(8,128)(2,1)S(1)} %collective-permute-done.10.refs_8_), channel_id=1, source_target_pairs={{0,16},{4,12},{8,24},{12,4},{16,0},{20,28},{24,8},{28,20},{1,17},{... | collective-permute-start | bytes 786440 | tf_op jit(solution)/shard_map/ppermute | solution.py:334
  34.9 9.5 %collective-permute-start.7 = (bf16[512,256]{1,0:T(8,128)(2,1)}, bf16[512,256]{1,0:T(8,128)(2,1)S(1)}, u32[]{:S(2)}, u32[]{:S(2)}) collective-permute-start(bf16[512,256]{1,0:T(8,128)(2,1)} %collective-permute-done.6.refs_2_), channel_id=1, source_target_pairs={{0,8},{4,20},{8,0},{12,28},{16,24},{20,4},{24,16},{28,12},{1,9},{5... | collective-permute-start | bytes 786440 | tf_op jit(solution)/shard_map/ppermute | solution.py:334
  35.5 9.4 %collective-permute-start.15 = (bf16[512,256]{1,0:T(8,128)(2,1)S(1)}, bf16[512,256]{1,0:T(8,128)(2,1)S(1)}, u32[]{:S(2)}, u32[]{:S(2)}) collective-permute-start(bf16[512,256]{1,0:T(8,128)(2,1)S(1)} %collective-permute-done.5.refs_3_), channel_id=1, source_target_pairs={{0,16},{4,12},{8,24},{12,4},{16,0},{20,28},{24,8},{28,20},{1,17},{... | collective-permute-start | bytes 786440 | tf_op jit(solution)/shard_map/ppermute | solution.py:334
  35.5 17.5 %collective-permute-start.8 = (bf16[512,256]{1,0:T(8,128)(2,1)}, bf16[512,256]{1,0:T(8,128)(2,1)}, u32[]{:S(2)}, u32[]{:S(2)}) collective-permute-start(bf16[512,256]{1,0:T(8,128)(2,1)} %collective-permute-done.6.refs_2_), channel_id=1, source_target_pairs={{0,16},{4,12},{8,24},{12,4},{16,0},{20,28},{24,8},{28,20},{1,17},{... | collective-permute-start | bytes 786440 | tf_op jit(solution)/shard_map/ppermute | solution.py:334
  41.8 8.7 %collective-permute-start.16 = (bf16[512,256]{1,0:T(8,128)(2,1)}, bf16[512,256]{1,0:T(8,128)(2,1)S(1)}, u32[]{:S(2)}, u32[]{:S(2)}) collective-permute-start(bf16[512,256]{1,0:T(8,128)(2,1)} %collective-permute-done.14.refs_4_), channel_id=1, source_target_pairs={{0,16},{4,12},{8,24},{12,4},{16,0},{20,28},{24,8},{28,20},{1,17},{... | collective-permute-start | bytes 786440 | tf_op jit(solution)/shard_map/ppermute | solution.py:334
  44.3 9.0 %collective-permute-start.13 = (bf16[512,256]{1,0:T(8,128)(2,1)S(1)}, bf16[512,256]{1,0:T(8,128)(2,1)}, u32[]{:S(2)}, u32[]{:S(2)}) collective-permute-start(bf16[512,256]{1,0:T(8,128)(2,1)S(1)} %collective-permute-done.7.refs_3_), channel_id=1, source_target_pairs={{0,16},{4,12},{8,24},{12,4},{16,0},{20,28},{24,8},{28,20},{1,17},{... | collective-permute-start | bytes 786440 | tf_op jit(solution)/shard_map/ppermute | solution.py:334
  54.9 1.6 %collective-permute-start.17 = (bf16[128,1024]{1,0:T(8,128)(2,1)S(1)}, bf16[128,1024]{1,0:T(8,128)(2,1)S(1)}, u32[]{:S(2)}, u32[]{:S(2)}) collective-permute-start(bf16[128,1024]{1,0:T(8,128)(2,1)S(1)} %get-tuple-element.60), channel_id=1, source_target_pairs={{0,4},{4,0},{8,12},{12,8},{16,20},{20,16},{24,28},{28,24},{1,5},{5... | collective-permute-start | bytes 786440 | tf_op jit(solution)/shard_map/ppermute | solution.py:441

commit v4 on v3

--- a/solution.py
+++ b/solution.py
@@ -8,18 +8,25 @@
 from jax.sharding import PartitionSpec as P
 
 GROUP = 16
+HOLD = [[], [], [], []]
+RELAY = {'z1': [], 'a1': ['s1'], 'mine': ['z1'], 'z2': ['s1'], 'z3': ['s2'], 'a3': []}
 FEAT = 3
 WIDE = 512
 LANES = 128
 SUB = 32
 VMEM_LIMIT = 48 << 20
+PREP = 63
+COST = pl.CostEstimate(flops=0, bytes_accessed=0, transcendentals=0)
 
 bf16 = jnp.bfloat16
 f32 = jnp.float32
 
 
-def after(x, *deps):
-    return lax.optimization_barrier((x,) + deps)[0]
+def waiting(kernel, count, first):
+    def body(*refs):
+        kernel(*refs[:first], *refs[first + count :])
+
+    return body
 
 
 def params(limit=VMEM_LIMIT):
@@ -200,7 +207,7 @@
     keep = FEAT - 1
     height = rows_ref.shape[1]
     width = piece_ref.shape[1]
-    at = pl.multiple_of(which_ref[0] * width, width)
+    at = pl.multiple_of((which_ref[0] & 7) * width, width)
     copies = [pltpu.make_async_copy(weight_ref.at[:, pl.ds(at, width)], piece_ref, sems.at[3])]
     for i, ref in enumerate((query_ref, key_ref, value_ref)):
         first = ref.shape[0] - height
@@ -220,7 +227,7 @@
 def prepare(query, key, value, weight):
     chans = query.shape[1]
     depth, cols = weight.shape
-    which = (lax.axis_index("ctx") % 8)[None].astype(jnp.int32)
+    which = lax.axis_index("ctx")[None].astype(jnp.int32)
     hbm = pl.BlockSpec(memory_space=pltpu.HBM)
     vmem = pl.BlockSpec(memory_space=pltpu.VMEM)
     return pl.pallas_call(
@@ -232,18 +239,36 @@
             jax.ShapeDtypeStruct((depth, cols // 8), bf16),
         ],
         scratch_shapes=[pltpu.VMEM((3, 16, chans), bf16), pltpu.SemaphoreType.DMA((4,))],
-        compiler_params=params(63 << 20),
+        compiler_params=params(PREP << 20),
         name="prepare",
     )(which, query, key, value, weight)
 
 
-def conv_path(query, key, value, halo, near, taps, rate, residues, skip):
+def relay_kernel(in_ref, *refs):
+    del in_ref, refs
+
+
+def relay(x, *held):
+    unused = pl.BlockSpec(memory_space=pl.ANY)
+    return pl.pallas_call(
+        relay_kernel,
+        in_specs=[unused] * (1 + len(held)),
+        out_specs=unused,
+        out_shape=jax.ShapeDtypeStruct(x.shape, x.dtype),
+        input_output_aliases={0: 0},
+        compiler_params=params(),
+        cost_estimate=COST,
+        name="relay",
+    )(x, *held)
+
+
+def conv_path(query, key, value, halo, near, two, mine, rate, residues, taps, skip):
     rows, chans = query.shape
     groups, modes = rate.shape
+    blocks = chans // LANES
+    depth = LANES // GROUP * SUB
     count = lax.axis_size("ctx")
     here = lax.axis_index("ctx")[None].astype(jnp.int32)
-    blocks = chans // LANES
-    depth = LANES // GROUP * SUB
     steps = chans // WIDE
     per = WIDE // LANES
     vmem = pl.BlockSpec(memory_space=pltpu.VMEM)
@@ -259,10 +284,9 @@
             state_shape,
         ],
         compiler_params=params(),
+        cost_estimate=COST,
         name="tables",
     )(rate, residues)
-    near = after(near, halo, left)
-    near_one, near_two = hop(near, True), hop(near, False)
 
     def wide(height):
         return pl.BlockSpec((height, WIDE), lambda b: (0, b))
@@ -272,10 +296,13 @@
 
     taps_spec = pl.BlockSpec((3, FEAT, WIDE), lambda b: (0, 0, b))
     subs = rows // SUB
+    unused = pl.BlockSpec(memory_space=pl.ANY)
+    pieces = dict(z1=near, z2=two)
+    held = [pieces[n] for n in HOLD[0]]
     kv, inner, before, state = pl.pallas_call(
-        product_kernel,
+        waiting(product_kernel, len(held), 6),
         grid=(steps,),
-        in_specs=[wide(rows), wide(rows), wide(8), taps_spec, stack(left), wide(modes)],
+        in_specs=[wide(rows), wide(rows), wide(8), taps_spec, stack(left), wide(modes)] + [unused] * len(held),
         out_specs=[wide(rows), wide(rows), wide(subs * modes), wide(modes)],
         out_shape=[
             jax.ShapeDtypeStruct((rows, chans), bf16),
@@ -284,27 +311,51 @@
             state_shape,
         ],
         compiler_params=params(),
+        cost_estimate=COST,
         name="kv_and_state",
-    )(key, value, halo, taps, left, rate_chan)
+    )(key, value, halo, taps, left, rate_chan, *held)
     enter = jnp.zeros_like(state)
+    pieces["k"] = state
     step = 1
-    states = [state]
+    at = lambda array, name: relay(array, *[pieces[n] for n in RELAY[name]]) if RELAY[name] else array
     while True:
+        if step == 1:
+            near = at(near, "z1")
+            pieces["a1"], pieces["b1"] = hop(near, True), hop(near, False)
         other = lax.ppermute(state, "ctx", [(i, i ^ step) for i in range(count)])
         if 2 * step >= count:
             break
+        held = [pieces[n] for n in HOLD[1 if step == 1 else 2]]
         state, enter = pl.pallas_call(
-            functools.partial(blend_kernel, rows, step),
-            in_specs=[smem] + [vmem] * 4,
+            waiting(functools.partial(blend_kernel, rows, step), len(held), 5),
+            in_specs=[smem] + [vmem] * 4 + [unused] * len(held),
             out_specs=[vmem] * 2,
             out_shape=[state_shape] * 2,
             compiler_params=params(),
+            cost_estimate=COST,
             name="blend_states",
-        )(here, state, other, enter, rate_chan)
+        )(here, state, other, enter, rate_chan, *held)
+        if step == 1:
+            pieces["s1"] = state
+            pieces["c1"] = hop(at(pieces["a1"], "a1"), False)
+            three = lax.ppermute(at(mine, "mine"), "fsdp", [(i, i ^ 3) for i in range(4)])
+            pieces["z3"] = three
+        if step == 2:
+            pieces["s2"] = state
+            two = at(two, "z2")
+            pieces["a2"], pieces["b2"] = hop(two, True), hop(two, False)
+            pieces["c2"] = hop(pieces["a2"], False)
         step *= 2
-        states.append(state)
+    pieces["y"] = other
+    three = at(three, "z3")
+    pieces["a3"], pieces["b3"] = hop(three, True), hop(three, False)
+    pieces["c3"] = hop(at(pieces["a3"], "a3"), False)
+    held = [pieces[n] for n in HOLD[3]]
+    slots = [
+        [first] + [pieces[n + i] for n in "abc"] for first, i in ((near, "1"), (two, "2"), (three, "3"))
+    ]
     gated = pl.pallas_call(
-        functools.partial(gate_kernel, step),
+        waiting(functools.partial(gate_kernel, step), len(held), 12),
         grid=(steps,),
         in_specs=[
             smem,
@@ -319,13 +370,15 @@
             wide(modes),
             stack(lag),
             wide(1),
-        ],
+        ]
+        + [unused] * len(held),
         out_specs=wide(rows),
         out_shape=jax.ShapeDtypeStruct((rows, chans), bf16),
         compiler_params=params(),
+        cost_estimate=COST,
         name="gate",
-    )(here, query, halo, taps, kv, inner, before, enter, other, rate_chan, lag, skip[None])
-    return gated, states, (near, near_one, near_two)
+    )(here, query, halo, taps, kv, inner, before, enter, other, rate_chan, lag, skip[None], *held)
+    return gated, slots
 
 
 def hop(x, first):
@@ -334,69 +387,45 @@
     return lax.ppermute(x, "ctx", [(i, i ^ (odd if i % 2 else even)) for i in range(count)])
 
 
-def send_weight(mine):
-    near = lax.ppermute(mine, "fsdp", [(i, i ^ 1) for i in range(4)])
-    two = lax.ppermute(mine, "fsdp", [(i, i ^ 2) for i in range(4)])
-    three = lax.ppermute(after(mine, near), "fsdp", [(i, i ^ 3) for i in range(4)])
-    return near, two, three
-
-
-def spread_weight(near, two, three, states):
-    near, one, side = near
-    corner = hop(after(one, states[1]), False)
-    slot_one = (near, one, side, corner)
-    two = after(two, states[1])
-    one, side = hop(two, True), hop(two, False)
-    corner = hop(after(one, states[-1]), False)
-    slot_two = (two, one, side, corner)
-    three = after(three, states[-1])
-    one, side = hop(three, True), hop(three, False)
-    corner = hop(after(one, *slot_two), False)
-    return slot_one, slot_two, (three, one, side, corner)
-
-
-def matmul_kernel(slot_count, has_own, has_acc, last, nums_ref, *refs):
-    refs = list(refs)
-    mine_ref, other_ref = refs[0], refs[1]
-    refs = refs[2:]
-    if has_own:
-        weight_ref = refs.pop(0)
-    slots = [refs[4 * s : 4 * s + 4] for s in range(slot_count)]
-    refs = refs[4 * slot_count :]
-    if has_acc:
-        acc_ref = refs.pop(0)
+def block_order(index):
+    core = index & 1
+    block = index & 7
+    return [block, block ^ (2 + 2 * core), block ^ (4 - 2 * core), block ^ 6]
+
+
+def both_rows(mine_ref, other_ref, part, depth):
+    at = pl.ds(pl.multiple_of(part * depth, depth), depth)
+    return jnp.concatenate([mine_ref[:, at], other_ref[:, at]], axis=0)
+
+
+def near_kernel(index_ref, place_ref, mine_ref, other_ref, weight_ref, *refs):
+    index, place = index_ref[0], place_ref[0]
+    one, two, acc_ref = refs[:4], refs[4:8], refs[8]
+    depth, block = one[0].shape
+    own, left_one, left_two = [both_rows(mine_ref, other_ref, place ^ n, depth) for n in (0, 1, 2)]
+    for r, at in enumerate(block_order(index)):
+        total = dot(own, weight_ref[:, pl.ds(pl.multiple_of(at * block, block), block)])
+        total = total + dot(left_one, one[r][...]) + dot(left_two, two[r][...])
+        acc_ref[:, r * block : (r + 1) * block] = total
+
+
+def far_kernel(index_ref, place_ref, mine_ref, other_ref, *refs):
+    index, place = index_ref[0], place_ref[0]
+    three, acc_ref, own_ref, out_ref = refs[:4], refs[4], refs[5], refs[6]
+    depth, block = three[0].shape
     rows = mine_ref.shape[0]
-    depth, block = slots[0][0].shape
-
-    def rows_of(part):
-        at = pl.multiple_of(nums_ref[part] * depth, depth)
-        return jnp.concatenate(
-            [mine_ref[:, pl.ds(at, depth)], other_ref[:, pl.ds(at, depth)]], axis=0
-        )
-
-    lhs = [rows_of(1 + s) for s in range(slot_count)]
-    if has_own:
-        own = rows_of(0)
-    for r in range(4):
-        total = acc_ref[:, r * block : (r + 1) * block] if has_acc else None
-        if has_own:
-            at = pl.multiple_of(nums_ref[4 + r] * block, block)
-            total = dot(own, weight_ref[:, pl.ds(at, block)])
-        for s in range(slot_count):
-            part = dot(lhs[s], slots[s][r][...])
-            total = part if total is None else total + part
-        if last:
-            at = pl.multiple_of(nums_ref[8 + r] * block, block)
-            done = total.astype(bf16)
-            refs[0][:, pl.ds(at, block)] = done[:rows]
-            refs[1][:, pl.ds(at, block)] = done[rows:]
-        else:
-            refs[0][:, r * block : (r + 1) * block] = total
+    left = both_rows(mine_ref, other_ref, place ^ 3, depth)
+    for r, at in enumerate(block_order(index)):
+        total = acc_ref[:, r * block : (r + 1) * block] + dot(left, three[r][...])
+        total = total.astype(bf16)
+        cols = pl.ds(pl.multiple_of((at >> 1) * block, block), block)
+        own_ref[:, cols] = total[:rows]
+        out_ref[:, cols] = total[rows:]
 
 
 def join_kernel(nums_ref, mine_ref, other_ref, out_ref):
     block = mine_ref.shape[1] // 4
-    core = nums_ref[0]
+    core = nums_ref[0] & 1
     for h in range(4):
         at = pl.multiple_of((2 * h + core) * block, block)
         out_ref[:, pl.ds(at, block)] = mine_ref[:, h * block : (h + 1) * block]
@@ -406,47 +435,46 @@
 
 def project(gated, weight, slots):
     count = lax.axis_size("ctx")
-    index = lax.axis_index("ctx")
-    place = lax.axis_index("fsdp")
+    index = lax.axis_index("ctx")[None].astype(jnp.int32)
+    place = lax.axis_index("fsdp")[None].astype(jnp.int32)
     rows = gated.shape[0]
-    depth, cols = weight.shape
-    half = cols // 2
+    cols = weight.shape[1]
     swap = [(i, i ^ 1) for i in range(count)]
     other = lax.ppermute(gated, "ctx", swap)
-    core = index % 2
-    first, second = jnp.where(core == 0, 2, 4), jnp.where(core == 0, 4, 2)
-    rel = index % 8
-    order = [rel, rel ^ first, rel ^ second, rel ^ 6]
-    parts = [place, place ^ 1, place ^ 2, place ^ 3]
-    nums = jnp.stack(parts + order + [n // 2 for n in order]).astype(jnp.int32)
     vmem = pl.BlockSpec(memory_space=pltpu.VMEM)
     smem = pl.BlockSpec(memory_space=pltpu.SMEM)
-    acc = pl.pallas_call(
-        functools.partial(matmul_kernel, 2, True, False, False),
-        in_specs=[smem] + [vmem] * 11,
-        out_specs=vmem,
-        out_shape=jax.ShapeDtypeStruct((2 * rows, half), f32),
-        compiler_params=params(),
-        name="project_near",
-    )(nums, gated, other, weight, *slots[0], *slots[1])
-    late = nums.at[1].set(nums[3])
-    mine, theirs = pl.pallas_call(
-        functools.partial(matmul_kernel, 1, False, True, True),
-        in_specs=[smem] + [vmem] * 7,
-        out_specs=[vmem, vmem],
-        out_shape=[jax.ShapeDtypeStruct((rows, half), bf16)] * 2,
-        compiler_params=params(),
-        name="project_far",
-    )(late, gated, other, *slots[2], acc)
+
+    def call(kernel, name, shapes, scalars, *args):
+        return pl.pallas_call(
+            kernel,
+            in_specs=[smem] * len(scalars) + [vmem] * len(args),
+            out_specs=[vmem] * len(shapes),
+            out_shape=shapes,
+            compiler_params=params(),
+            cost_estimate=COST,
+            name=name,
+        )(*scalars, *args)
+
+    (acc,) = call(
+        near_kernel,
+        "project_near",
+        [jax.ShapeDtypeStruct((2 * rows, cols // 2), f32)],
+        (index, place), gated, other, weight, *slots[0], *slots[1],
+    )
+    mine, theirs = call(
+        far_kernel,
+        "project_far",
+        [jax.ShapeDtypeStruct((rows, cols // 2), bf16)] * 2,
+        (index, place), gated, other, *slots[2], acc,
+    )
     back = lax.ppermute(theirs, "ctx", swap)
-    return pl.pallas_call(
+    (out,) = call(
         join_kernel,
-        in_specs=[smem, vmem, vmem],
-        out_specs=vmem,
-        out_shape=jax.ShapeDtypeStruct((rows, cols), bf16),
-        compiler_params=params(),
-        name="join_columns",
-    )(core[None].astype(jnp.int32), mine, back)
+        "join_columns",
+        [jax.ShapeDtypeStruct((rows, cols), bf16)],
+        (index,), mine, back,
+    )
+    return out
 
 
 def local(query_in, key_in, value_in, feature_taps, decay_rate, residues, skip_gain, out_weight):
@@ -454,11 +482,12 @@
     tails, mine = prepare(query, key, value, out_weight)
     count = lax.axis_size("ctx")
     halo = lax.ppermute(tails, "ctx", [(i, i + 1) for i in range(count - 1)])
-    near, two, three = send_weight(mine)
-    gated, states, near = conv_path(
-        query, key, value, halo, near, feature_taps, decay_rate, residues, skip_gain
+    near = lax.ppermute(mine, "fsdp", [(i, i ^ 1) for i in range(4)])
+    two = lax.ppermute(mine, "fsdp", [(i, i ^ 2) for i in range(4)])
+    gated, slots = conv_path(
+        query, key, value, halo, near, two, mine, decay_rate, residues, feature_taps, skip_gain
     )
-    return project(gated, out_weight, spread_weight(near, two, three, states))[None]
+    return project(gated, out_weight, slots)[None]
 
 
 def solution(mesh):

time: 57.6 us -> 55.1 us (0.957)
  waiting for transfers between devices: 16.9 us -> 11.8 us
  local copies, waits for them, and re-layouts: 1.38 us -> 4.6 us
  Pallas kernels: 13.1 us -> 12.1 us
    ppermute x9, waiting for transfers between devices: 10.9 us -> 6 us  [hop(): lax.ppermute(x, 'ctx', [(i, i ^ (odd if i % 2 else even)) for i in range(...]
    unnamed x18 -> x25, local copies, waits for them, and re-layouts: 1.27 us -> 4.59 us
    ppermute x9, starting transfers between devices: 8.51 us -> 9.73 us  [hop(): lax.ppermute(x, 'ctx', [(i, i ^ (odd if i % 2 else even)) for i in range(...]
    ppermute x3, starting transfers between devices: 8.98 us -> 7.93 us  [the longest x1 3.11 us: local(): near = lax.ppermute(mine, 'fsdp', [(i, i ^ 1) for i in range(4)])]
    pallas_call x7 -> x11, Pallas kernels: 9.31 us -> 8.34 us  [the longest x3 4.02 us: call(): pl.pallas_call(kernel, in_specs=[smem] * len(scalars) + [vmem] * len(args...]
  transfers between devices with their start and end apart: 18 -> 18, of which waited for: 9 -> 8; matrix products, arithmetic and copies ran while one was open for 1% -> 0% of each run, Pallas kernels for 15% -> 16%
where the time goes in v4:
time: 55.1 us; the launch traced here: 54.8 us
  starting transfers between devices  26.2 us (48%)
  Pallas kernels  12.1 us (22%)
  waiting for transfers between devices  11.8 us (21%)
  local copies, waits for them, and re-layouts  4.6 us (8%)
    ppermute x9, starting transfers between devices, hop(): lax.ppermute(x, 'ctx', [(i, i ^ (odd if i % 2 else even)) for i in range(...  9.73 us
    ppermute x3, starting transfers between devices, conv_path(): other = lax.ppermute(state, 'ctx', [(i, i ^ step) for i in range(count)])  6.96 us
    ppermute x9, waiting for transfers between devices, hop(): lax.ppermute(x, 'ctx', [(i, i ^ (odd if i % 2 else even)) for i in range(...  6 us
    unnamed x25, local copies, waits for them, and re-layouts  4.59 us
    ppermute x3, waiting for transfers between devices, conv_path(): other = lax.ppermute(state, 'ctx', [(i, i ^ step) for i in range(count)])  4.33 us
    pallas_call x3, Pallas kernels, call(): pl.pallas_call(kernel, in_specs=[smem] * len(scalars) + [vmem] * len(args...  4.02 us
    ppermute x1, starting transfers between devices, local(): near = lax.ppermute(mine, 'fsdp', [(i, i ^ 1) for i in range(4)])  3.11 us
    ppermute x1, starting transfers between devices, local(): two = lax.ppermute(mine, 'fsdp', [(i, i ^ 2) for i in range(4)])  2.59 us
  transfers between devices with their start and end apart: 18, of which 8 were waited for; matrix products, arithmetic and copies ran while one was open for 0% of the time, Pallas kernels for 16%

profile of v4, /device:TPU:0, one launch (start us, length us, event | category | flops | bytes accessed | tf_op | source)
XLA Modules:
  0.0 54.8 jit_solution(3801649652417888149)
XLA Ops:
  0.0 0.0 copy-start.1
  0.0 0.0 copy-start.9
  0.0 0.0 copy-start.10
  0.0 0.0 copy-start.3
  0.0 1.8 %prepare.1 = (f32[8,2048]{1,0:T(8,128)}, bf16[512,256]{1,0:T(8,128)(2,1)}) custom-call(s32[1]{0:T(128)} %bitcast.which_ref.refs_0_.index_ref.nums_ref, bf16[128,2048]{1,0:T(8,128)(2,1)} %bitcast.7, bf16[128,2048]{1,0:T(8,128)(2,1)} %bitcast.9, bf16[128,2048]{1,0:T(8,128)(2,1)} %bitcast.11, bf16[512,2048]{1,0:T(8,128)(2,1)} %weight_ref.3), custom_call_target="tpu_custom_call" | custom-call | tf_op jit(solution)/shard_map/prepare/pallas_call | solution.py:233
  1.8 3.1 %collective-permute-start.5 = (bf16[512,256]{1,0:T(8,128)(2,1)}, bf16[512,256]{1,0:T(8,128)(2,1)S(1)}, u32[]{:S(2)}, u32[]{:S(2)}) collective-permute-start(bf16[512,256]{1,0:T(8,128)(2,1)} %get-tuple-element.32.in_ref), channel_id=1, source_target_pairs={{0,1},{1,0},{2,3},{3,2},{4,5},{5,4},{6,7},{7,6},{8,9},{9,8},{10,11... | collective-permute-start | bytes 786440 | tf_op jit(solution)/shard_map/ppermute | solution.py:485
  4.9 2.6 %collective-permute-start.13 = (bf16[512,256]{1,0:T(8,128)(2,1)}, bf16[512,256]{1,0:T(8,128)(2,1)S(1)}, u32[]{:S(2)}, u32[]{:S(2)}) collective-permute-start(bf16[512,256]{1,0:T(8,128)(2,1)} %get-tuple-element.32.in_ref), channel_id=1, source_target_pairs={{0,2},{1,3},{2,0},{3,1},{4,6},{5,7},{6,4},{7,5},{8,10},{9,11},{10,... | collective-permute-start | bytes 786440 | tf_op jit(solution)/shard_map/ppermute | solution.py:486
  7.5 1.3 %collective-permute-start = (f32[8,2048]{1,0:T(8,128)}, f32[8,2048]{1,0:T(8,128)S(1)}, u32[]{:S(2)}, u32[]{:S(2)}) collective-permute-start(f32[8,2048]{1,0:T(8,128)} %get-tuple-element.20), channel_id=1, source_target_pairs={{0,4},{4,8},{8,12},{12,16},{16,20},{20,24},{24,28},{1,5},{5,9},{9,... | collective-permute-start | bytes 196616 | tf_op jit(solution)/shard_map/ppermute | solution.py:484
  8.8 0.0 copy-done.9
  8.8 0.1 copy.13.rate_ref
  8.9 0.0 copy-done.10
  8.9 0.1 copy.14.residue_ref
  9.0 2.0 %tables.1 = (bf16[16,96,256]{2,1,0:T(8,128)(2,1)S(1)}, bf16[16,64,256]{2,1,0:T(8,128)(2,1)S(1)}, f32[16,2048]{1,0:T(8,128)S(1)}) custom-call(f32[128,16]{1,0:T(8,128)S(1)} %copy.13.rate_ref, f32[128,16]{1,0:T(8,128)S(1)} %copy.14.residue_ref), custom_call_target="tpu_custom_call" | custom-call | tf_op jit(solution)/shard_map/tables/pallas_call | solution.py:277
  11.0 0.0 collective-permute-done.refs_2_
  11.0 0.0 copy-done.1
  11.0 0.0 copy-done.3
  11.0 0.0 copy-start.2
  11.1 1.0 %copy-done.2 = bf16[1,128,2048]{2,1,0:T(8,128)(2,1)S(1)} copy-done((bf16[1,128,2048]{2,1,0:T(8,128)(2,1)S(1)}, bf16[1,128,2048]{2,1,0:T(8,128)(2,1)}, u32[]{:S(2)}) %copy-start.2) | copy-done | bytes 524312
  12.1 0.0 copy-start
  12.1 2.3 %kv_and_state.1 = (bf16[128,2048]{1,0:T(8,128)(2,1)S(1)}, f32[128,2048]{1,0:T(8,128)S(1)}, f32[64,2048]{1,0:T(8,128)S(1)}, f32[16,2048]{1,0:T(8,128)S(1)}) custom-call(bf16[128,2048]{1,0:T(8,128)(2,1)S(1)} %bitcast.10, bf16[128,2048]{1,0:T(8,128)(2,1)S(1)} %bitcast.12, f32[8,2048]{1,0:T(8,128)S(1)} %collective-permute-done.refs_2_, ...), custom_call_target="tpu_custom_call" | custom-call | tf_op jit(solution)/shard_map/kv_and_state/pallas_call | solution.py:302
  14.4 2.3 %collective-permute-start.1 = (f32[16,2048]{1,0:T(8,128)S(1)}, f32[16,2048]{1,0:T(8,128)S(1)}, u32[]{:S(2)}, u32[]{:S(2)}) collective-permute-start(f32[16,2048]{1,0:T(8,128)S(1)} %get-tuple-element.26.refs_1_), channel_id=1, source_target_pairs={{0,4},{4,0},{8,12},{12,8},{16,20},{20,16},{24,28},{28,24},{1,5},{5... | collective-permute-start | bytes 393224 | tf_op jit(solution)/shard_map/ppermute | solution.py:325
  16.7 1.0 %collective-permute-done.1.refs_2_ = f32[16,2048]{1,0:T(8,128)S(1)} collective-permute-done((f32[16,2048]{1,0:T(8,128)S(1)}, f32[16,2048]{1,0:T(8,128)S(1)}, u32[]{:S(2)}, u32[]{:S(2)}) %collective-permute-start.1) | collective-permute-done | bytes 131104 | tf_op jit(solution)/shard_map/ppermute | solution.py:325
  17.7 0.1 blend_states.2
  17.7 2.0 %collective-permute-start.2 = (f32[16,2048]{1,0:T(8,128)S(1)}, f32[16,2048]{1,0:T(8,128)S(1)}, u32[]{:S(2)}, u32[]{:S(2)}) collective-permute-start(f32[16,2048]{1,0:T(8,128)S(1)} %get-tuple-element.27.refs_1_.refs_0_), channel_id=1, source_target_pairs={{0,8},{4,12},{8,0},{12,4},{16,24},{20,28},{24,16},{28,20},{1,9},{5... | collective-permute-start | bytes 393224 | tf_op jit(solution)/shard_map/ppermute | solution.py:325
  19.7 0.0 collective-permute-done.5.refs_0_
  19.7 0.0 collective-permute-done.13.in_ref
  19.7 2.2 %collective-permute-start.6 = (bf16[512,256]{1,0:T(8,128)(2,1)}, bf16[512,256]{1,0:T(8,128)(2,1)S(1)}, u32[]{:S(2)}, u32[]{:S(2)}) collective-permute-start(bf16[512,256]{1,0:T(8,128)(2,1)} %relay.4), channel_id=1, source_target_pairs={{0,3},{1,2},{2,1},{3,0},{4,7},{5,6},{6,5},{7,4},{8,11},{9,10},{10,... | collective-permute-start | bytes 786440 | tf_op jit(solution)/shard_map/ppermute | solution.py:341
  22.0 1.5 %collective-permute-start.10 = (bf16[512,256]{1,0:T(8,128)(2,1)S(1)}, bf16[512,256]{1,0:T(8,128)(2,1)S(1)}, u32[]{:S(2)}, u32[]{:S(2)}) collective-permute-start(bf16[512,256]{1,0:T(8,128)(2,1)S(1)} %collective-permute-done.5.refs_0_), channel_id=1, source_target_pairs={{0,8},{4,20},{8,0},{12,28},{16,24},{20,4},{24,16},{28,12},{1,9},{5... | collective-permute-start | bytes 786440 | tf_op jit(solution)/shard_map/ppermute | solution.py:387
  23.5 0.1 collective-permute-done.2.refs_2_
  23.6 0.1 blend_states.3
  23.7 2.7 %collective-permute-start.3 = (f32[16,2048]{1,0:T(8,128)S(1)}, f32[16,2048]{1,0:T(8,128)S(1)}, u32[]{:S(2)}, u32[]{:S(2)}) collective-permute-start(f32[16,2048]{1,0:T(8,128)S(1)} %get-tuple-element.30.refs_0_), channel_id=1, source_target_pairs={{0,16},{4,20},{8,24},{12,28},{16,0},{20,4},{24,8},{28,12},{1,17},{... | collective-permute-start | bytes 393224 | tf_op jit(solution)/shard_map/ppermute | solution.py:325
  26.3 0.6 %collective-permute-start.14 = (bf16[512,256]{1,0:T(8,128)(2,1)S(1)}, bf16[512,256]{1,0:T(8,128)(2,1)}, u32[]{:S(2)}, u32[]{:S(2)}) collective-permute-start(bf16[512,256]{1,0:T(8,128)(2,1)S(1)} %relay.7.refs_4_), channel_id=1, source_target_pairs={{0,8},{4,20},{8,0},{12,28},{16,24},{20,4},{24,16},{28,12},{1,9},{5... | collective-permute-start | bytes 786440 | tf_op jit(solution)/shard_map/ppermute | solution.py:387
  26.9 0.5 collective-permute-start.15
  27.4 3.2 %collective-permute-done.3.refs_8_ = f32[16,2048]{1,0:T(8,128)S(1)} collective-permute-done((f32[16,2048]{1,0:T(8,128)S(1)}, f32[16,2048]{1,0:T(8,128)S(1)}, u32[]{:S(2)}, u32[]{:S(2)}) %collective-permute-start.3) | collective-permute-done | bytes 131104 | tf_op jit(solution)/shard_map/ppermute | solution.py:325
  30.7 2.1 %collective-permute-start.11 = (bf16[512,256]{1,0:T(8,128)(2,1)S(1)}, bf16[512,256]{1,0:T(8,128)(2,1)S(1)}, u32[]{:S(2)}, u32[]{:S(2)}) collective-permute-start(bf16[512,256]{1,0:T(8,128)(2,1)S(1)} %collective-permute-done.5.refs_0_), channel_id=1, source_target_pairs={{0,16},{4,12},{8,24},{12,4},{16,0},{20,28},{24,8},{28,20},{1,17},{... | collective-permute-start | bytes 786440 | tf_op jit(solution)/shard_map/ppermute | solution.py:387
  32.8 0.0 copy-done
  32.8 0.0 copy-done.8
  32.8 1.9 %gate.1.mine_ref = bf16[128,2048]{1,0:T(8,128)(2,1)S(1)} custom-call(s32[1]{0:T(128)} %bitcast.which_ref.refs_0_.index_ref.nums_ref, bf16[128,2048]{1,0:T(8,128)(2,1)S(1)} %bitcast.8, f32[8,2048]{1,0:T(8,128)S(1)} %collective-permute-done.refs_2_, f32[3,3,2048]{2,1,0:T(4,128)S(1)} %copy-done.3, bf16[128,2048]{1,0:T(8,128)(2,1)S(1)} %get-tuple-element.23.refs_4_, ...), custom_call_target="tpu_custom_call" | custom-call | tf_op jit(solution)/shard_map/gate/pallas_call | solution.py:357
  34.7 0.0 collective-permute-done.6.in_ref
  34.7 0.1 collective-permute-start.4
  34.8 0.0 collective-permute-done.10.refs_1_
  34.8 0.7 %collective-permute-start.7 = (bf16[512,256]{1,0:T(8,128)(2,1)S(1)}, bf16[512,256]{1,0:T(8,128)(2,1)S(1)}, u32[]{:S(2)}, u32[]{:S(2)}) collective-permute-start(bf16[512,256]{1,0:T(8,128)(2,1)S(1)} %relay.5.refs_0_), channel_id=1, source_target_pairs={{0,8},{4,20},{8,0},{12,28},{16,24},{20,4},{24,16},{28,12},{1,9},{5... | collective-permute-start | bytes 786440 | tf_op jit(solution)/shard_map/ppermute | solution.py:387
  35.5 0.2 collective-permute-done.14.refs_5_
  35.7 0.4 collective-permute-start.12
  36.1 0.0 collective-permute-done.15.refs_6_
  36.1 0.7 %copy-done.4 = bf16[512,256]{1,0:T(8,128)(2,1)} copy-done((bf16[512,256]{1,0:T(8,128)(2,1)}, bf16[512,256]{1,0:T(8,128)(2,1)S(1)}, u32[]{:S(2)}) %copy-start.4) | copy-done | bytes 262168
  36.8 1.7 %collective-permute-start.16 = (bf16[512,256]{1,0:T(8,128)(2,1)}, bf16[512,256]{1,0:T(8,128)(2,1)}, u32[]{:S(2)}, u32[]{:S(2)}) collective-permute-start(bf16[512,256]{1,0:T(8,128)(2,1)} %collective-permute-done.14.refs_5_), channel_id=1, source_target_pairs={{0,16},{4,12},{8,24},{12,4},{16,0},{20,28},{24,8},{28,20},{1,17},{... | collective-permute-start | bytes 786440 | tf_op jit(solution)/shard_map/ppermute | solution.py:387
  38.4 0.0 collective-permute-done.11.refs_2_
  38.4 0.7 %copy-done.6 = bf16[512,256]{1,0:T(8,128)(2,1)} copy-done((bf16[512,256]{1,0:T(8,128)(2,1)}, bf16[512,256]{1,0:T(8,128)(2,1)S(1)}, u32[]{:S(2)}) %copy-start.6) | copy-done | bytes 262168
  39.1 2.3 %collective-permute-start.8 = (bf16[512,256]{1,0:T(8,128)(2,1)S(1)}, bf16[512,256]{1,0:T(8,128)(2,1)S(1)}, u32[]{:S(2)}, u32[]{:S(2)}) collective-permute-start(bf16[512,256]{1,0:T(8,128)(2,1)S(1)} %relay.5.refs_0_), channel_id=1, source_target_pairs={{0,16},{4,12},{8,24},{12,4},{16,0},{20,28},{24,8},{28,20},{1,17},{... | collective-permute-start | bytes 786440 | tf_op jit(solution)/shard_map/ppermute | solution.py:387
  41.5 2.5 %collective-permute-done.7.refs_1_ = bf16[512,256]{1,0:T(8,128)(2,1)S(1)} collective-permute-done((bf16[512,256]{1,0:T(8,128)(2,1)S(1)}, bf16[512,256]{1,0:T(8,128)(2,1)S(1)}, u32[]{:S(2)}, u32[]{:S(2)}) %collective-permute-start.7) | collective-permute-done | bytes 262176 | tf_op jit(solution)/shard_map/ppermute | solution.py:387
  43.9 0.0 collective-permute-start.9
  43.9 0.0 collective-permute-done.12.refs_3_
  44.0 2.4 %collective-permute-done.16.refs_7_ = bf16[512,256]{1,0:T(8,128)(2,1)} collective-permute-done((bf16[512,256]{1,0:T(8,128)(2,1)}, bf16[512,256]{1,0:T(8,128)(2,1)}, u32[]{:S(2)}, u32[]{:S(2)}) %collective-permute-start.16) | collective-permute-done | bytes 262176 | tf_op jit(solution)/shard_map/ppermute | solution.py:387
  46.4 0.0 collective-permute-done.4.other_ref
  46.4 0.9 %copy-done.5 = bf16[512,256]{1,0:T(8,128)(2,1)S(1)} copy-done((bf16[512,256]{1,0:T(8,128)(2,1)S(1)}, bf16[512,256]{1,0:T(8,128)(2,1)}, u32[]{:S(2)}) %copy-start.5) | copy-done | bytes 262168
  47.3 0.9 %copy-done.7 = bf16[512,256]{1,0:T(8,128)(2,1)S(1)} copy-done((bf16[512,256]{1,0:T(8,128)(2,1)S(1)}, bf16[512,256]{1,0:T(8,128)(2,1)}, u32[]{:S(2)}) %copy-start.7) | copy-done | bytes 262168
  48.3 2.7 %project_near.1.refs_4_ = f32[256,1024]{1,0:T(8,128)S(1)} custom-call(s32[1]{0:T(128)} %bitcast.which_ref.refs_0_.index_ref.nums_ref, s32[1]{0:T(128)} %bitcast.1.place_ref, bf16[128,2048]{1,0:T(8,128)(2,1)S(1)} %gate.1.mine_ref, bf16[128,2048]{1,0:T(8,128)(2,1)S(1)} %collective-permute-done.4.other_ref, bf16[512,2048]{1,0:T(8,128)(2,1)} %weight_ref.3, ...), custom_call_target="tpu_custom_call" | custom-call | tf_op jit(solution)/shard_map/project_near/pallas_call | solution.py:448
  51.0 0.0 collective-permute-done.8.refs_2_
  51.0 0.9 %collective-permute-done.9.refs_3_ = bf16[512,256]{1,0:T(8,128)(2,1)S(1)} collective-permute-done((bf16[512,256]{1,0:T(8,128)(2,1)S(1)}, bf16[512,256]{1,0:T(8,128)(2,1)S(1)}, u32[]{:S(2)}, u32[]{:S(2)}) %collective-permute-start.9) | collective-permute-done | bytes 262176 | tf_op jit(solution)/shard_map/ppermute | solution.py:387
  51.9 0.5 project_far.1
  52.4 0.2 collective-permute-start.17
  52.6 1.4 %collective-permute-done.17.other_ref = bf16[128,1024]{1,0:T(8,128)(2,1)S(1)} collective-permute-done((bf16[128,1024]{1,0:T(8,128)(2,1)S(1)}, bf16[128,1024]{1,0:T(8,128)(2,1)S(1)}, u32[]{:S(2)}, u32[]{:S(2)}) %collective-permute-start.17) | collective-permute-done | bytes 262176 | tf_op jit(solution)/shard_map/ppermute | solution.py:470
  54.0 0.8 %join_columns.1 = bf16[128,2048]{1,0:T(8,128)(2,1)} custom-call(s32[1]{0:T(128)} %bitcast.which_ref.refs_0_.index_ref.nums_ref, bf16[128,1024]{1,0:T(8,128)(2,1)S(1)} %get-tuple-element.33.mine_ref, bf16[128,1024]{1,0:T(8,128)(2,1)S(1)} %collective-permute-done.17.other_ref), custom_call_target="tpu_custom_call" | custom-call | tf_op jit(solution)/shard_map/join_columns/pallas_call | solution.py:448
  (11 shorter events, 0.0 us)
Async XLA Ops:
  0.0 11.0 %copy-start.1 = (bf16[1,128,2048]{2,1,0:T(8,128)(2,1)S(1)}, bf16[1,128,2048]{2,1,0:T(8,128)(2,1)}, u32[]{:S(2)}) copy-start(bf16[1,128,2048]{2,1,0:T(8,128)(2,1)} %param.9) | copy-start | bytes 1572868
  0.0 8.8 %copy-start.9 = (f32[128,16]{0,1:T(8,128)S(1)}, f32[128,16]{0,1:T(8,128)}, u32[]{:S(2)}) copy-start(f32[128,16]{0,1:T(8,128)} %param.12) | copy-start | bytes 24580
  0.0 8.9 %copy-start.10 = (f32[128,16]{0,1:T(8,128)S(1)}, f32[128,16]{0,1:T(8,128)}, u32[]{:S(2)}) copy-start(f32[128,16]{0,1:T(8,128)} %param.13) | copy-start | bytes 24580
  0.0 11.0 %copy-start.3 = (f32[3,3,2048]{2,1,0:T(4,128)S(1)}, f32[3,3,2048]{2,1,0:T(4,128)}, u32[]{:S(2)}) copy-start(f32[3,3,2048]{2,1,0:T(4,128)} %refs_3_.3) | copy-start | bytes 221188
  1.8 17.9 %collective-permute-start.5 = (bf16[512,256]{1,0:T(8,128)(2,1)}, bf16[512,256]{1,0:T(8,128)(2,1)S(1)}, u32[]{:S(2)}, u32[]{:S(2)}) collective-permute-start(bf16[512,256]{1,0:T(8,128)(2,1)} %get-tuple-element.32.in_ref), channel_id=1, source_target_pairs={{0,1},{1,0},{2,3},{3,2},{4,5},{5,4},{6,7},{7,6},{8,9},{9,8},{10,11... | collective-permute-start | bytes 786440 | tf_op jit(solution)/shard_map/ppermute | solution.py:485
  4.9 14.8 %collective-permute-start.13 = (bf16[512,256]{1,0:T(8,128)(2,1)}, bf16[512,256]{1,0:T(8,128)(2,1)S(1)}, u32[]{:S(2)}, u32[]{:S(2)}) collective-permute-start(bf16[512,256]{1,0:T(8,128)(2,1)} %get-tuple-element.32.in_ref), channel_id=1, source_target_pairs={{0,2},{1,3},{2,0},{3,1},{4,6},{5,7},{6,4},{7,5},{8,10},{9,11},{10,... | collective-permute-start | bytes 786440 | tf_op jit(solution)/shard_map/ppermute | solution.py:486
  7.5 3.5 %collective-permute-start = (f32[8,2048]{1,0:T(8,128)}, f32[8,2048]{1,0:T(8,128)S(1)}, u32[]{:S(2)}, u32[]{:S(2)}) collective-permute-start(f32[8,2048]{1,0:T(8,128)} %get-tuple-element.20), channel_id=1, source_target_pairs={{0,4},{4,8},{8,12},{12,16},{16,20},{20,24},{24,28},{1,5},{5,9},{9,... | collective-permute-start | bytes 196616 | tf_op jit(solution)/shard_map/ppermute | solution.py:484
  11.0 1.0 %copy-start.2 = (bf16[1,128,2048]{2,1,0:T(8,128)(2,1)S(1)}, bf16[1,128,2048]{2,1,0:T(8,128)(2,1)}, u32[]{:S(2)}) copy-start(bf16[1,128,2048]{2,1,0:T(8,128)(2,1)} %param.10) | copy-start | bytes 1572868
  12.1 20.7 %copy-start = (bf16[1,128,2048]{2,1,0:T(8,128)(2,1)S(1)}, bf16[1,128,2048]{2,1,0:T(8,128)(2,1)}, u32[]{:S(2)}) copy-start(bf16[1,128,2048]{2,1,0:T(8,128)(2,1)} %param.8) | copy-start | bytes 1572868
  12.1 20.7 %copy-start.8 = (f32[2048]{0:T(1024)S(1)}, f32[2048]{0:T(1024)}, u32[]{:S(2)}) copy-start(f32[2048]{0:T(1024)} %param.14) | copy-start | bytes 24580
  14.4 3.3 %collective-permute-start.1 = (f32[16,2048]{1,0:T(8,128)S(1)}, f32[16,2048]{1,0:T(8,128)S(1)}, u32[]{:S(2)}, u32[]{:S(2)}) collective-permute-start(f32[16,2048]{1,0:T(8,128)S(1)} %get-tuple-element.26.refs_1_), channel_id=1, source_target_pairs={{0,4},{4,0},{8,12},{12,8},{16,20},{20,16},{24,28},{28,24},{1,5},{5... | collective-permute-start | bytes 393224 | tf_op jit(solution)/shard_map/ppermute | solution.py:325
  17.7 5.8 %collective-permute-start.2 = (f32[16,2048]{1,0:T(8,128)S(1)}, f32[16,2048]{1,0:T(8,128)S(1)}, u32[]{:S(2)}, u32[]{:S(2)}) collective-permute-start(f32[16,2048]{1,0:T(8,128)S(1)} %get-tuple-element.27.refs_1_.refs_0_), channel_id=1, source_target_pairs={{0,8},{4,12},{8,0},{12,4},{16,24},{20,28},{24,16},{28,20},{1,9},{5... | collective-permute-start | bytes 393224 | tf_op jit(solution)/shard_map/ppermute | solution.py:325
  19.7 14.9 %collective-permute-start.6 = (bf16[512,256]{1,0:T(8,128)(2,1)}, bf16[512,256]{1,0:T(8,128)(2,1)S(1)}, u32[]{:S(2)}, u32[]{:S(2)}) collective-permute-start(bf16[512,256]{1,0:T(8,128)(2,1)} %relay.4), channel_id=1, source_target_pairs={{0,3},{1,2},{2,1},{3,0},{4,7},{5,6},{6,5},{7,4},{8,11},{9,10},{10,... | collective-permute-start | bytes 786440 | tf_op jit(solution)/shard_map/ppermute | solution.py:341
  22.0 12.8 %collective-permute-start.10 = (bf16[512,256]{1,0:T(8,128)(2,1)S(1)}, bf16[512,256]{1,0:T(8,128)(2,1)S(1)}, u32[]{:S(2)}, u32[]{:S(2)}) collective-permute-start(bf16[512,256]{1,0:T(8,128)(2,1)S(1)} %collective-permute-done.5.refs_0_), channel_id=1, source_target_pairs={{0,8},{4,20},{8,0},{12,28},{16,24},{20,4},{24,16},{28,12},{1,9},{5... | collective-permute-start | bytes 786440 | tf_op jit(solution)/shard_map/ppermute | solution.py:387
  23.7 7.0 %collective-permute-start.3 = (f32[16,2048]{1,0:T(8,128)S(1)}, f32[16,2048]{1,0:T(8,128)S(1)}, u32[]{:S(2)}, u32[]{:S(2)}) collective-permute-start(f32[16,2048]{1,0:T(8,128)S(1)} %get-tuple-element.30.refs_0_), channel_id=1, source_target_pairs={{0,16},{4,20},{8,24},{12,28},{16,0},{20,4},{24,8},{28,12},{1,17},{... | collective-permute-start | bytes 393224 | tf_op jit(solution)/shard_map/ppermute | solution.py:325
  26.3 9.3 %collective-permute-start.14 = (bf16[512,256]{1,0:T(8,128)(2,1)S(1)}, bf16[512,256]{1,0:T(8,128)(2,1)}, u32[]{:S(2)}, u32[]{:S(2)}) collective-permute-start(bf16[512,256]{1,0:T(8,128)(2,1)S(1)} %relay.7.refs_4_), channel_id=1, source_target_pairs={{0,8},{4,20},{8,0},{12,28},{16,24},{20,4},{24,16},{28,12},{1,9},{5... | collective-permute-start | bytes 786440 | tf_op jit(solution)/shard_map/ppermute | solution.py:387
  26.9 9.1 %collective-permute-start.15 = (bf16[512,256]{1,0:T(8,128)(2,1)S(1)}, bf16[512,256]{1,0:T(8,128)(2,1)S(1)}, u32[]{:S(2)}, u32[]{:S(2)}) collective-permute-start(bf16[512,256]{1,0:T(8,128)(2,1)S(1)} %relay.7.refs_4_), channel_id=1, source_target_pairs={{0,16},{4,12},{8,24},{12,4},{16,0},{20,28},{24,8},{28,20},{1,17},{... | collective-permute-start | bytes 786440 | tf_op jit(solution)/shard_map/ppermute | solution.py:387
  30.7 7.8 %collective-permute-start.11 = (bf16[512,256]{1,0:T(8,128)(2,1)S(1)}, bf16[512,256]{1,0:T(8,128)(2,1)S(1)}, u32[]{:S(2)}, u32[]{:S(2)}) collective-permute-start(bf16[512,256]{1,0:T(8,128)(2,1)S(1)} %collective-permute-done.5.refs_0_), channel_id=1, source_target_pairs={{0,16},{4,12},{8,24},{12,4},{16,0},{20,28},{24,8},{28,20},{1,17},{... | collective-permute-start | bytes 786440 | tf_op jit(solution)/shard_map/ppermute | solution.py:387
  34.7 11.7 %collective-permute-start.4 = (bf16[128,2048]{1,0:T(8,128)(2,1)S(1)}, bf16[128,2048]{1,0:T(8,128)(2,1)S(1)}, u32[]{:S(2)}, u32[]{:S(2)}) collective-permute-start(bf16[128,2048]{1,0:T(8,128)(2,1)S(1)} %gate.1.mine_ref), channel_id=1, source_target_pairs={{0,4},{4,0},{8,12},{12,8},{16,20},{20,16},{24,28},{28,24},{1,5},{5... | collective-permute-start | bytes 1572872 | tf_op jit(solution)/shard_map/ppermute | solution.py:443
  34.8 9.2 %collective-permute-start.7 = (bf16[512,256]{1,0:T(8,128)(2,1)S(1)}, bf16[512,256]{1,0:T(8,128)(2,1)S(1)}, u32[]{:S(2)}, u32[]{:S(2)}) collective-permute-start(bf16[512,256]{1,0:T(8,128)(2,1)S(1)} %relay.5.refs_0_), channel_id=1, source_target_pairs={{0,8},{4,20},{8,0},{12,28},{16,24},{20,4},{24,16},{28,12},{1,9},{5... | collective-permute-start | bytes 786440 | tf_op jit(solution)/shard_map/ppermute | solution.py:387
  35.7 8.3 %collective-permute-start.12 = (bf16[512,256]{1,0:T(8,128)(2,1)S(1)}, bf16[512,256]{1,0:T(8,128)(2,1)}, u32[]{:S(2)}, u32[]{:S(2)}) collective-permute-start(bf16[512,256]{1,0:T(8,128)(2,1)S(1)} %relay.6), channel_id=1, source_target_pairs={{0,16},{4,12},{8,24},{12,4},{16,0},{20,28},{24,8},{28,20},{1,17},{... | collective-permute-start | bytes 786440 | tf_op jit(solution)/shard_map/ppermute | solution.py:387
  36.1 0.7 %copy-start.4 = (bf16[512,256]{1,0:T(8,128)(2,1)}, bf16[512,256]{1,0:T(8,128)(2,1)S(1)}, u32[]{:S(2)}) copy-start(bf16[512,256]{1,0:T(8,128)(2,1)S(1)} %collective-permute-done.15.refs_6_) | copy-start | bytes 786436
  36.8 9.6 %collective-permute-start.16 = (bf16[512,256]{1,0:T(8,128)(2,1)}, bf16[512,256]{1,0:T(8,128)(2,1)}, u32[]{:S(2)}, u32[]{:S(2)}) collective-permute-start(bf16[512,256]{1,0:T(8,128)(2,1)} %collective-permute-done.14.refs_5_), channel_id=1, source_target_pairs={{0,16},{4,12},{8,24},{12,4},{16,0},{20,28},{24,8},{28,20},{1,17},{... | collective-permute-start | bytes 786440 | tf_op jit(solution)/shard_map/ppermute | solution.py:387
  38.4 0.7 %copy-start.6 = (bf16[512,256]{1,0:T(8,128)(2,1)}, bf16[512,256]{1,0:T(8,128)(2,1)S(1)}, u32[]{:S(2)}) copy-start(bf16[512,256]{1,0:T(8,128)(2,1)S(1)} %collective-permute-done.11.refs_2_) | copy-start | bytes 786436
  39.1 11.9 %collective-permute-start.8 = (bf16[512,256]{1,0:T(8,128)(2,1)S(1)}, bf16[512,256]{1,0:T(8,128)(2,1)S(1)}, u32[]{:S(2)}, u32[]{:S(2)}) collective-permute-start(bf16[512,256]{1,0:T(8,128)(2,1)S(1)} %relay.5.refs_0_), channel_id=1, source_target_pairs={{0,16},{4,12},{8,24},{12,4},{16,0},{20,28},{24,8},{28,20},{1,17},{... | collective-permute-start | bytes 786440 | tf_op jit(solution)/shard_map/ppermute | solution.py:387
  43.9 8.0 %collective-permute-start.9 = (bf16[512,256]{1,0:T(8,128)(2,1)S(1)}, bf16[512,256]{1,0:T(8,128)(2,1)S(1)}, u32[]{:S(2)}, u32[]{:S(2)}) collective-permute-start(bf16[512,256]{1,0:T(8,128)(2,1)S(1)} %collective-permute-done.7.refs_1_), channel_id=1, source_target_pairs={{0,16},{4,12},{8,24},{12,4},{16,0},{20,28},{24,8},{28,20},{1,17},{... | collective-permute-start | bytes 786440 | tf_op jit(solution)/shard_map/ppermute | solution.py:387
  46.4 1.0 %copy-start.5 = (bf16[512,256]{1,0:T(8,128)(2,1)S(1)}, bf16[512,256]{1,0:T(8,128)(2,1)}, u32[]{:S(2)}) copy-start(bf16[512,256]{1,0:T(8,128)(2,1)} %copy-done.4) | copy-start | bytes 786436
  47.3 0.9 %copy-start.7 = (bf16[512,256]{1,0:T(8,128)(2,1)S(1)}, bf16[512,256]{1,0:T(8,128)(2,1)}, u32[]{:S(2)}) copy-start(bf16[512,256]{1,0:T(8,128)(2,1)} %copy-done.6) | copy-start | bytes 786436
  52.4 1.6 %collective-permute-start.17 = (bf16[128,1024]{1,0:T(8,128)(2,1)S(1)}, bf16[128,1024]{1,0:T(8,128)(2,1)S(1)}, u32[]{:S(2)}, u32[]{:S(2)}) collective-permute-start(bf16[128,1024]{1,0:T(8,128)(2,1)S(1)} %get-tuple-element.34), channel_id=1, source_target_pairs={{0,4},{4,0},{8,12},{12,8},{16,20},{20,16},{24,28},{28,24},{1,5},{5... | collective-permute-start | bytes 786440 | tf_op jit(solution)/shard_map/ppermute | solution.py:470

commit v5 on v4

--- a/solution.py
+++ b/solution.py
@@ -9,13 +9,13 @@
 
 GROUP = 16
 HOLD = [[], [], [], []]
-RELAY = {'z1': [], 'a1': ['s1'], 'mine': ['z1'], 'z2': ['s1'], 'z3': ['s2'], 'a3': []}
+RELAY = {'z1': [], 'a1': [], 'mine': ['z1'], 'z2': ['s1'], 'z3': ['s2'], 'a3': []}
 FEAT = 3
 WIDE = 512
 LANES = 128
 SUB = 32
 VMEM_LIMIT = 48 << 20
-PREP = 63
+PREP = 61
 COST = pl.CostEstimate(flops=0, bytes_accessed=0, transcendentals=0)
 
 bf16 = jnp.bfloat16
@@ -244,6 +244,26 @@
     )(which, query, key, value, weight)
 
 
+def stack_kernel(one_ref, two_ref, out_ref):
+    depth = one_ref.shape[0]
+    out_ref[:depth] = one_ref[...]
+    out_ref[depth:] = two_ref[...]
+
+
+def stack_rows(one, two):
+    depth, block = one.shape
+    vmem = pl.BlockSpec(memory_space=pltpu.VMEM)
+    return pl.pallas_call(
+        stack_kernel,
+        in_specs=[vmem, vmem],
+        out_specs=vmem,
+        out_shape=jax.ShapeDtypeStruct((2 * depth, block), bf16),
+        compiler_params=params(),
+        cost_estimate=COST,
+        name="stack_rows",
+    )(one, two)
+
+
 def relay_kernel(in_ref, *refs):
     del in_ref, refs
 
@@ -321,7 +341,7 @@
     while True:
         if step == 1:
             near = at(near, "z1")
-            pieces["a1"], pieces["b1"] = hop(near, True), hop(near, False)
+            pieces["a1"] = hop(near, True)
         other = lax.ppermute(state, "ctx", [(i, i ^ step) for i in range(count)])
         if 2 * step >= count:
             break
@@ -337,14 +357,14 @@
         )(here, state, other, enter, rate_chan, *held)
         if step == 1:
             pieces["s1"] = state
-            pieces["c1"] = hop(at(pieces["a1"], "a1"), False)
             three = lax.ppermute(at(mine, "mine"), "fsdp", [(i, i ^ 3) for i in range(4)])
             pieces["z3"] = three
         if step == 2:
             pieces["s2"] = state
             two = at(two, "z2")
-            pieces["a2"], pieces["b2"] = hop(two, True), hop(two, False)
-            pieces["c2"] = hop(pieces["a2"], False)
+            pieces["a2"] = hop(two, True)
+            pieces["b"] = hop(stack_rows(near, two), False)
+            pieces["c"] = hop(stack_rows(pieces["a1"], pieces["a2"]), False)
         step *= 2
     pieces["y"] = other
     three = at(three, "z3")
@@ -352,7 +372,8 @@
     pieces["c3"] = hop(at(pieces["a3"], "a3"), False)
     held = [pieces[n] for n in HOLD[3]]
     slots = [
-        [first] + [pieces[n + i] for n in "abc"] for first, i in ((near, "1"), (two, "2"), (three, "3"))
+        [near, pieces["a1"], two, pieces["a2"], pieces["b"], pieces["c"]],
+        [three, pieces["a3"], pieces["b3"], pieces["c3"]],
     ]
     gated = pl.pallas_call(
         waiting(functools.partial(gate_kernel, step), len(held), 12),
@@ -400,12 +421,17 @@
 
 def near_kernel(index_ref, place_ref, mine_ref, other_ref, weight_ref, *refs):
     index, place = index_ref[0], place_ref[0]
-    one, two, acc_ref = refs[:4], refs[4:8], refs[8]
-    depth, block = one[0].shape
+    near_ref, near_one, two_ref, two_one, side, corner, acc_ref = refs
+    depth, block = near_ref.shape
     own, left_one, left_two = [both_rows(mine_ref, other_ref, place ^ n, depth) for n in (0, 1, 2)]
+    left = jnp.concatenate([left_one, left_two], axis=1)
     for r, at in enumerate(block_order(index)):
         total = dot(own, weight_ref[:, pl.ds(pl.multiple_of(at * block, block), block)])
-        total = total + dot(left_one, one[r][...]) + dot(left_two, two[r][...])
+        if r < 2:
+            one, two = ((near_ref, two_ref), (near_one, two_one))[r]
+            total = total + dot(left_one, one[...]) + dot(left_two, two[...])
+        else:
+            total = total + dot(left, (side, corner)[r - 2][...])
         acc_ref[:, r * block : (r + 1) * block] = total
 
 
@@ -459,13 +485,13 @@
         near_kernel,
         "project_near",
         [jax.ShapeDtypeStruct((2 * rows, cols // 2), f32)],
-        (index, place), gated, other, weight, *slots[0], *slots[1],
+        (index, place), gated, other, weight, *slots[0],
     )
     mine, theirs = call(
         far_kernel,
         "project_far",
         [jax.ShapeDtypeStruct((rows, cols // 2), bf16)] * 2,
-        (index, place), gated, other, *slots[2], acc,
+        (index, place), gated, other, *slots[1], acc,
     )
     back = lax.ppermute(theirs, "ctx", swap)
     (out,) = call(

time: 55.1 us -> 54.6 us (level)
  waiting for transfers between devices: 11.8 us -> 19.3 us
  starting transfers between devices: 26.2 us -> 21.2 us
  local copies, waits for them, and re-layouts: 4.6 us -> 0.24 us
  Pallas kernels: 12.1 us -> 13.4 us
    ppermute x9 -> x7, waiting for transfers between devices: 6 us -> 12.3 us  [hop(): lax.ppermute(x, 'ctx', [(i, i ^ (odd if i % 2 else even)) for i in range(...]
    unnamed x25 -> x16, local copies, waits for them, and re-layouts: 4.59 us -> 0.23 us
    ppermute x9 -> x7, starting transfers between devices: 9.73 us -> 5.57 us  [hop(): lax.ppermute(x, 'ctx', [(i, i ^ (odd if i % 2 else even)) for i in range(...]
    pallas_call x3, Pallas kernels: 4.02 us -> 5.22 us  [call(): pl.pallas_call(kernel, in_specs=[smem] * len(scalars) + [vmem] * len(args...]
    ppermute x3, starting transfers between devices: 6.96 us -> 6.06 us  [conv_path(): other = lax.ppermute(state, 'ctx', [(i, i ^ step) for i in range(count)])]
    ppermute x1, waiting for transfers between devices: 0.01 us -> 0.65 us  [local(): two = lax.ppermute(mine, 'fsdp', [(i, i ^ 2) for i in range(4)])]
  transfers between devices with their start and end apart: 18 -> 16, of which waited for: 8 -> 7; matrix products, arithmetic and copies ran while one was open for 0% -> 0% of each run, Pallas kernels for 16% -> 17%
where the time goes in v5:
time: 54.6 us; the launch traced here: 54.4 us
  starting transfers between devices  21.2 us (39%)
  waiting for transfers between devices  19.3 us (35%)
  Pallas kernels  13.4 us (25%)
    ppermute x7, waiting for transfers between devices, hop(): lax.ppermute(x, 'ctx', [(i, i ^ (odd if i % 2 else even)) for i in range(...  12.3 us
    ppermute x3, starting transfers between devices, conv_path(): other = lax.ppermute(state, 'ctx', [(i, i ^ step) for i in range(count)])  6.06 us
    ppermute x7, starting transfers between devices, hop(): lax.ppermute(x, 'ctx', [(i, i ^ (odd if i % 2 else even)) for i in range(...  5.57 us
    pallas_call x3, Pallas kernels, call(): pl.pallas_call(kernel, in_specs=[smem] * len(scalars) + [vmem] * len(args...  5.22 us
    ppermute x3, waiting for transfers between devices, conv_path(): other = lax.ppermute(state, 'ctx', [(i, i ^ step) for i in range(count)])  4.86 us
    ppermute x1, starting transfers between devices, local(): near = lax.ppermute(mine, 'fsdp', [(i, i ^ 1) for i in range(4)])  3.1 us
    ppermute x1, starting transfers between devices, local(): two = lax.ppermute(mine, 'fsdp', [(i, i ^ 2) for i in range(4)])  2.59 us
    ppermute x1, starting transfers between devices, conv_path(): lax.ppermute(at(mine, 'mine'), 'fsdp', [(i, i ^ 3) for i in range(4)])  2.45 us
  transfers between devices with their start and end apart: 16, of which 7 were waited for; matrix products, arithmetic and copies ran while one was open for 0% of the time, Pallas kernels for 17%

profile of v5, /device:TPU:0, one launch (start us, length us, event | category | flops | bytes accessed | tf_op | source)
XLA Modules:
  0.0 54.4 jit_solution(4914896880471476887)
XLA Ops:
  0.0 0.0 copy-start.2
  0.0 0.0 copy-start.1
  0.0 0.0 copy-start.5
  0.0 0.0 copy-start.6
  0.0 0.0 copy-start.3
  0.0 1.9 %prepare.1 = (f32[8,2048]{1,0:T(8,128)}, bf16[512,256]{1,0:T(8,128)(2,1)}) custom-call(s32[1]{0:T(128)} %bitcast.which_ref.refs_0_.index_ref.nums_ref, bf16[128,2048]{1,0:T(8,128)(2,1)} %bitcast.7, bf16[128,2048]{1,0:T(8,128)(2,1)} %bitcast.9, bf16[128,2048]{1,0:T(8,128)(2,1)} %bitcast.11, bf16[512,2048]{1,0:T(8,128)(2,1)} %weight_ref.3), custom_call_target="tpu_custom_call" | custom-call | tf_op jit(solution)/shard_map/prepare/pallas_call | solution.py:233
  1.9 3.1 %collective-permute-start.5 = (bf16[512,256]{1,0:T(8,128)(2,1)}, bf16[512,256]{1,0:T(8,128)(2,1)S(1)}, u32[]{:S(2)}, u32[]{:S(2)}) collective-permute-start(bf16[512,256]{1,0:T(8,128)(2,1)} %get-tuple-element.32.in_ref), channel_id=1, source_target_pairs={{0,1},{1,0},{2,3},{3,2},{4,5},{5,4},{6,7},{7,6},{8,9},{9,8},{10,11... | collective-permute-start | bytes 786440 | tf_op jit(solution)/shard_map/ppermute | solution.py:511
  5.0 2.6 %collective-permute-start.11 = (bf16[512,256]{1,0:T(8,128)(2,1)}, bf16[512,256]{1,0:T(8,128)(2,1)S(1)}, u32[]{:S(2)}, u32[]{:S(2)}) collective-permute-start(bf16[512,256]{1,0:T(8,128)(2,1)} %get-tuple-element.32.in_ref), channel_id=1, source_target_pairs={{0,2},{1,3},{2,0},{3,1},{4,6},{5,7},{6,4},{7,5},{8,10},{9,11},{10,... | collective-permute-start | bytes 786440 | tf_op jit(solution)/shard_map/ppermute | solution.py:512
  7.6 1.3 %collective-permute-start = (f32[8,2048]{1,0:T(8,128)}, f32[8,2048]{1,0:T(8,128)S(1)}, u32[]{:S(2)}, u32[]{:S(2)}) collective-permute-start(f32[8,2048]{1,0:T(8,128)} %get-tuple-element.20), channel_id=1, source_target_pairs={{0,4},{4,8},{8,12},{12,16},{16,20},{20,24},{24,28},{1,5},{5,9},{9,... | collective-permute-start | bytes 196616 | tf_op jit(solution)/shard_map/ppermute | solution.py:510
  8.9 0.0 copy-done.5
  8.9 0.1 copy.12.rate_ref
  9.0 0.0 copy-done.6
  9.0 0.1 copy.13.residue_ref
  9.1 2.0 %tables.1 = (bf16[16,96,256]{2,1,0:T(8,128)(2,1)S(1)}, bf16[16,64,256]{2,1,0:T(8,128)(2,1)S(1)}, f32[16,2048]{1,0:T(8,128)S(1)}) custom-call(f32[128,16]{1,0:T(8,128)S(1)} %copy.12.rate_ref, f32[128,16]{1,0:T(8,128)S(1)} %copy.13.residue_ref), custom_call_target="tpu_custom_call" | custom-call | tf_op jit(solution)/shard_map/tables/pallas_call | solution.py:297
  11.1 0.0 collective-permute-done.refs_2_
  11.1 0.0 copy-done.2
  11.1 0.0 copy-done.1
  11.1 0.0 copy-done.3
  11.1 2.3 %kv_and_state.1 = (bf16[128,2048]{1,0:T(8,128)(2,1)S(1)}, f32[128,2048]{1,0:T(8,128)S(1)}, f32[64,2048]{1,0:T(8,128)S(1)}, f32[16,2048]{1,0:T(8,128)S(1)}) custom-call(bf16[128,2048]{1,0:T(8,128)(2,1)S(1)} %bitcast.10, bf16[128,2048]{1,0:T(8,128)(2,1)S(1)} %bitcast.12, f32[8,2048]{1,0:T(8,128)S(1)} %collective-permute-done.refs_2_, ...), custom_call_target="tpu_custom_call" | custom-call | tf_op jit(solution)/shard_map/kv_and_state/pallas_call | solution.py:322
  13.4 0.0 copy-start
  13.4 0.0 copy-start.4
  13.4 2.3 %collective-permute-start.1 = (f32[16,2048]{1,0:T(8,128)S(1)}, f32[16,2048]{1,0:T(8,128)S(1)}, u32[]{:S(2)}, u32[]{:S(2)}) collective-permute-start(f32[16,2048]{1,0:T(8,128)S(1)} %get-tuple-element.26.refs_1_), channel_id=1, source_target_pairs={{0,4},{4,0},{8,12},{12,8},{16,20},{20,16},{24,28},{28,24},{1,5},{5... | collective-permute-start | bytes 393224 | tf_op jit(solution)/shard_map/ppermute | solution.py:345
  15.7 1.0 %collective-permute-done.1.refs_2_ = f32[16,2048]{1,0:T(8,128)S(1)} collective-permute-done((f32[16,2048]{1,0:T(8,128)S(1)}, f32[16,2048]{1,0:T(8,128)S(1)}, u32[]{:S(2)}, u32[]{:S(2)}) %collective-permute-start.1) | collective-permute-done | bytes 131104 | tf_op jit(solution)/shard_map/ppermute | solution.py:345
  16.7 0.1 blend_states.2
  16.8 2.0 %collective-permute-start.2 = (f32[16,2048]{1,0:T(8,128)S(1)}, f32[16,2048]{1,0:T(8,128)S(1)}, u32[]{:S(2)}, u32[]{:S(2)}) collective-permute-start(f32[16,2048]{1,0:T(8,128)S(1)} %get-tuple-element.27.refs_1_.refs_0_), channel_id=1, source_target_pairs={{0,8},{4,12},{8,0},{12,4},{16,24},{20,28},{24,16},{28,20},{1,9},{5... | collective-permute-start | bytes 393224 | tf_op jit(solution)/shard_map/ppermute | solution.py:345
  18.8 0.0 collective-permute-done.5.refs_0_.one_ref
  18.8 0.1 collective-permute-start.10
  18.9 0.7 %collective-permute-done.11.in_ref = bf16[512,256]{1,0:T(8,128)(2,1)S(1)} collective-permute-done((bf16[512,256]{1,0:T(8,128)(2,1)}, bf16[512,256]{1,0:T(8,128)(2,1)S(1)}, u32[]{:S(2)}, u32[]{:S(2)}) %collective-permute-start.11) | collective-permute-done | bytes 262176 | tf_op jit(solution)/shard_map/ppermute | solution.py:512
  19.5 1.5 %collective-permute-start.12 = (bf16[512,256]{1,0:T(8,128)(2,1)S(1)}, bf16[512,256]{1,0:T(8,128)(2,1)S(1)}, u32[]{:S(2)}, u32[]{:S(2)}) collective-permute-start(bf16[512,256]{1,0:T(8,128)(2,1)S(1)} %relay.5.two_ref.refs_2_), channel_id=1, source_target_pairs={{0,8},{4,20},{8,0},{12,28},{16,24},{20,4},{24,16},{28,12},{1,9},{5... | collective-permute-start | bytes 786440 | tf_op jit(solution)/shard_map/ppermute | solution.py:408
  21.0 2.5 %collective-permute-start.6 = (bf16[512,256]{1,0:T(8,128)(2,1)}, bf16[512,256]{1,0:T(8,128)(2,1)S(1)}, u32[]{:S(2)}, u32[]{:S(2)}) collective-permute-start(bf16[512,256]{1,0:T(8,128)(2,1)} %relay.3), channel_id=1, source_target_pairs={{0,3},{1,2},{2,1},{3,0},{4,7},{5,6},{6,5},{7,4},{8,11},{9,10},{10,... | collective-permute-start | bytes 786440 | tf_op jit(solution)/shard_map/ppermute | solution.py:360
  23.5 0.0 collective-permute-done.2.refs_2_
  23.5 0.1 blend_states.3
  23.6 1.8 %collective-permute-start.3 = (f32[16,2048]{1,0:T(8,128)S(1)}, f32[16,2048]{1,0:T(8,128)S(1)}, u32[]{:S(2)}, u32[]{:S(2)}) collective-permute-start(f32[16,2048]{1,0:T(8,128)S(1)} %get-tuple-element.30.refs_0_), channel_id=1, source_target_pairs={{0,16},{4,20},{8,24},{12,28},{16,0},{20,4},{24,8},{28,12},{1,17},{... | collective-permute-start | bytes 393224 | tf_op jit(solution)/shard_map/ppermute | solution.py:345
  25.4 0.4 collective-permute-start.13
  25.8 3.9 %collective-permute-done.3.refs_8_ = f32[16,2048]{1,0:T(8,128)S(1)} collective-permute-done((f32[16,2048]{1,0:T(8,128)S(1)}, f32[16,2048]{1,0:T(8,128)S(1)}, u32[]{:S(2)}, u32[]{:S(2)}) %collective-permute-start.3) | collective-permute-done | bytes 131104 | tf_op jit(solution)/shard_map/ppermute | solution.py:345
  29.6 0.0 copy-done
  29.6 0.0 copy-done.4
  29.7 1.9 %gate.1.mine_ref = bf16[128,2048]{1,0:T(8,128)(2,1)S(1)} custom-call(s32[1]{0:T(128)} %bitcast.which_ref.refs_0_.index_ref.nums_ref, bf16[128,2048]{1,0:T(8,128)(2,1)S(1)} %bitcast.8, f32[8,2048]{1,0:T(8,128)S(1)} %collective-permute-done.refs_2_, f32[3,3,2048]{2,1,0:T(4,128)S(1)} %copy-done.3, bf16[128,2048]{1,0:T(8,128)(2,1)S(1)} %get-tuple-element.23.refs_4_, ...), custom_call_target="tpu_custom_call" | custom-call | tf_op jit(solution)/shard_map/gate/pallas_call | solution.py:378
  31.5 0.1 collective-permute-start.4
  31.6 0.0 collective-permute-done.10.one_ref.refs_1_
  31.6 0.0 collective-permute-done.12.two_ref.refs_3_
  31.7 2.6 %collective-permute-start.14 = (bf16[1024,256]{1,0:T(8,128)(2,1)S(1)}, bf16[1024,256]{1,0:T(8,128)(2,1)}, u32[]{:S(2)}, u32[]{:S(2)}) collective-permute-start(bf16[1024,256]{1,0:T(8,128)(2,1)S(1)} %stack_rows.3), channel_id=1, source_target_pairs={{0,16},{4,12},{8,24},{12,4},{16,0},{20,28},{24,8},{28,20},{1,17},{... | collective-permute-start | bytes 1572872 | tf_op jit(solution)/shard_map/ppermute | solution.py:408
  34.3 0.0 collective-permute-done.6.in_ref
  34.3 0.8 %collective-permute-start.7 = (bf16[512,256]{1,0:T(8,128)(2,1)S(1)}, bf16[512,256]{1,0:T(8,128)(2,1)}, u32[]{:S(2)}, u32[]{:S(2)}) collective-permute-start(bf16[512,256]{1,0:T(8,128)(2,1)S(1)} %relay.4.refs_0_), channel_id=1, source_target_pairs={{0,8},{4,20},{8,0},{12,28},{16,24},{20,4},{24,16},{28,12},{1,9},{5... | collective-permute-start | bytes 786440 | tf_op jit(solution)/shard_map/ppermute | solution.py:408
  35.1 0.1 collective-permute-start.8
  35.2 8.5 %collective-permute-done.7.refs_1_ = bf16[512,256]{1,0:T(8,128)(2,1)} collective-permute-done((bf16[512,256]{1,0:T(8,128)(2,1)S(1)}, bf16[512,256]{1,0:T(8,128)(2,1)}, u32[]{:S(2)}, u32[]{:S(2)}) %collective-permute-start.7) | collective-permute-done | bytes 262176 | tf_op jit(solution)/shard_map/ppermute | solution.py:408
  43.7 0.1 collective-permute-start.9
  43.8 0.0 collective-permute-done.13.refs_4_
  43.8 0.0 collective-permute-done.4.other_ref
  43.8 0.5 collective-permute-done.14.refs_5_
  44.3 2.8 %project_near.1.refs_4_ = f32[256,1024]{1,0:T(8,128)S(1)} custom-call(s32[1]{0:T(128)} %bitcast.which_ref.refs_0_.index_ref.nums_ref, s32[1]{0:T(128)} %bitcast.1.place_ref, bf16[128,2048]{1,0:T(8,128)(2,1)S(1)} %gate.1.mine_ref, bf16[128,2048]{1,0:T(8,128)(2,1)S(1)} %collective-permute-done.4.other_ref, bf16[512,2048]{1,0:T(8,128)(2,1)} %weight_ref.3, ...), custom_call_target="tpu_custom_call" | custom-call | tf_op jit(solution)/shard_map/project_near/pallas_call | solution.py:474
  47.1 0.0 collective-permute-done.8.refs_2_
  47.1 3.2 %collective-permute-done.9.refs_3_ = bf16[512,256]{1,0:T(8,128)(2,1)} collective-permute-done((bf16[512,256]{1,0:T(8,128)(2,1)}, bf16[512,256]{1,0:T(8,128)(2,1)}, u32[]{:S(2)}, u32[]{:S(2)}) %collective-permute-start.9) | collective-permute-done | bytes 262176 | tf_op jit(solution)/shard_map/ppermute | solution.py:408
  50.4 1.6 %project_far.1 = (bf16[128,1024]{1,0:T(8,128)(2,1)S(1)}, bf16[128,1024]{1,0:T(8,128)(2,1)S(1)}) custom-call(s32[1]{0:T(128)} %bitcast.which_ref.refs_0_.index_ref.nums_ref, s32[1]{0:T(128)} %bitcast.1.place_ref, bf16[128,2048]{1,0:T(8,128)(2,1)S(1)} %gate.1.mine_ref, bf16[128,2048]{1,0:T(8,128)(2,1)S(1)} %collective-permute-done.4.other_ref, ...), custom_call_target="tpu_custom_call" | custom-call | tf_op jit(solution)/shard_map/project_far/pallas_call | solution.py:474
  51.9 0.1 collective-permute-start.15
  52.0 1.5 %collective-permute-done.15.other_ref = bf16[128,1024]{1,0:T(8,128)(2,1)S(1)} collective-permute-done((bf16[128,1024]{1,0:T(8,128)(2,1)S(1)}, bf16[128,1024]{1,0:T(8,128)(2,1)S(1)}, u32[]{:S(2)}, u32[]{:S(2)}) %collective-permute-start.15) | collective-permute-done | bytes 262176 | tf_op jit(solution)/shard_map/ppermute | solution.py:496
  53.5 0.8 %join_columns.1 = bf16[128,2048]{1,0:T(8,128)(2,1)} custom-call(s32[1]{0:T(128)} %bitcast.which_ref.refs_0_.index_ref.nums_ref, bf16[128,1024]{1,0:T(8,128)(2,1)S(1)} %get-tuple-element.33.mine_ref, bf16[128,1024]{1,0:T(8,128)(2,1)S(1)} %collective-permute-done.15.other_ref), custom_call_target="tpu_custom_call" | custom-call | tf_op jit(solution)/shard_map/join_columns/pallas_call | solution.py:474
  (6 shorter events, 0.1 us)
Async XLA Ops:
  0.0 11.1 %copy-start.2 = (bf16[1,128,2048]{2,1,0:T(8,128)(2,1)S(1)}, bf16[1,128,2048]{2,1,0:T(8,128)(2,1)}, u32[]{:S(2)}) copy-start(bf16[1,128,2048]{2,1,0:T(8,128)(2,1)} %param.10) | copy-start | bytes 1572868
  0.0 11.1 %copy-start.1 = (bf16[1,128,2048]{2,1,0:T(8,128)(2,1)S(1)}, bf16[1,128,2048]{2,1,0:T(8,128)(2,1)}, u32[]{:S(2)}) copy-start(bf16[1,128,2048]{2,1,0:T(8,128)(2,1)} %param.9) | copy-start | bytes 1572868
  0.0 8.9 %copy-start.5 = (f32[128,16]{0,1:T(8,128)S(1)}, f32[128,16]{0,1:T(8,128)}, u32[]{:S(2)}) copy-start(f32[128,16]{0,1:T(8,128)} %param.12) | copy-start | bytes 24580
  0.0 9.0 %copy-start.6 = (f32[128,16]{0,1:T(8,128)S(1)}, f32[128,16]{0,1:T(8,128)}, u32[]{:S(2)}) copy-start(f32[128,16]{0,1:T(8,128)} %param.13) | copy-start | bytes 24580
  0.0 11.1 %copy-start.3 = (f32[3,3,2048]{2,1,0:T(4,128)S(1)}, f32[3,3,2048]{2,1,0:T(4,128)}, u32[]{:S(2)}) copy-start(f32[3,3,2048]{2,1,0:T(4,128)} %refs_3_.3) | copy-start | bytes 221188
  1.9 16.9 %collective-permute-start.5 = (bf16[512,256]{1,0:T(8,128)(2,1)}, bf16[512,256]{1,0:T(8,128)(2,1)S(1)}, u32[]{:S(2)}, u32[]{:S(2)}) collective-permute-start(bf16[512,256]{1,0:T(8,128)(2,1)} %get-tuple-element.32.in_ref), channel_id=1, source_target_pairs={{0,1},{1,0},{2,3},{3,2},{4,5},{5,4},{6,7},{7,6},{8,9},{9,8},{10,11... | collective-permute-start | bytes 786440 | tf_op jit(solution)/shard_map/ppermute | solution.py:511
  5.0 14.6 %collective-permute-start.11 = (bf16[512,256]{1,0:T(8,128)(2,1)}, bf16[512,256]{1,0:T(8,128)(2,1)S(1)}, u32[]{:S(2)}, u32[]{:S(2)}) collective-permute-start(bf16[512,256]{1,0:T(8,128)(2,1)} %get-tuple-element.32.in_ref), channel_id=1, source_target_pairs={{0,2},{1,3},{2,0},{3,1},{4,6},{5,7},{6,4},{7,5},{8,10},{9,11},{10,... | collective-permute-start | bytes 786440 | tf_op jit(solution)/shard_map/ppermute | solution.py:512
  7.6 3.5 %collective-permute-start = (f32[8,2048]{1,0:T(8,128)}, f32[8,2048]{1,0:T(8,128)S(1)}, u32[]{:S(2)}, u32[]{:S(2)}) collective-permute-start(f32[8,2048]{1,0:T(8,128)} %get-tuple-element.20), channel_id=1, source_target_pairs={{0,4},{4,8},{8,12},{12,16},{16,20},{20,24},{24,28},{1,5},{5,9},{9,... | collective-permute-start | bytes 196616 | tf_op jit(solution)/shard_map/ppermute | solution.py:510
  13.4 16.3 %copy-start = (bf16[1,128,2048]{2,1,0:T(8,128)(2,1)S(1)}, bf16[1,128,2048]{2,1,0:T(8,128)(2,1)}, u32[]{:S(2)}) copy-start(bf16[1,128,2048]{2,1,0:T(8,128)(2,1)} %param.8) | copy-start | bytes 1572868
  13.4 16.3 %copy-start.4 = (f32[2048]{0:T(1024)S(1)}, f32[2048]{0:T(1024)}, u32[]{:S(2)}) copy-start(f32[2048]{0:T(1024)} %param.14) | copy-start | bytes 24580
  13.4 3.3 %collective-permute-start.1 = (f32[16,2048]{1,0:T(8,128)S(1)}, f32[16,2048]{1,0:T(8,128)S(1)}, u32[]{:S(2)}, u32[]{:S(2)}) collective-permute-start(f32[16,2048]{1,0:T(8,128)S(1)} %get-tuple-element.26.refs_1_), channel_id=1, source_target_pairs={{0,4},{4,0},{8,12},{12,8},{16,20},{20,16},{24,28},{28,24},{1,5},{5... | collective-permute-start | bytes 393224 | tf_op jit(solution)/shard_map/ppermute | solution.py:345
  16.8 6.7 %collective-permute-start.2 = (f32[16,2048]{1,0:T(8,128)S(1)}, f32[16,2048]{1,0:T(8,128)S(1)}, u32[]{:S(2)}, u32[]{:S(2)}) collective-permute-start(f32[16,2048]{1,0:T(8,128)S(1)} %get-tuple-element.27.refs_1_.refs_0_), channel_id=1, source_target_pairs={{0,8},{4,12},{8,0},{12,4},{16,24},{20,28},{24,16},{28,20},{1,9},{5... | collective-permute-start | bytes 393224 | tf_op jit(solution)/shard_map/ppermute | solution.py:345
  18.8 12.9 %collective-permute-start.10 = (bf16[512,256]{1,0:T(8,128)(2,1)S(1)}, bf16[512,256]{1,0:T(8,128)(2,1)S(1)}, u32[]{:S(2)}, u32[]{:S(2)}) collective-permute-start(bf16[512,256]{1,0:T(8,128)(2,1)S(1)} %collective-permute-done.5.refs_0_.one_ref), channel_id=1, source_target_pairs={{0,8},{4,20},{8,0},{12,28},{16,24},{20,4},{24,16},{28,12},{1,9},{5... | collective-permute-start | bytes 786440 | tf_op jit(solution)/shard_map/ppermute | solution.py:408
  19.5 12.1 %collective-permute-start.12 = (bf16[512,256]{1,0:T(8,128)(2,1)S(1)}, bf16[512,256]{1,0:T(8,128)(2,1)S(1)}, u32[]{:S(2)}, u32[]{:S(2)}) collective-permute-start(bf16[512,256]{1,0:T(8,128)(2,1)S(1)} %relay.5.two_ref.refs_2_), channel_id=1, source_target_pairs={{0,8},{4,20},{8,0},{12,28},{16,24},{20,4},{24,16},{28,12},{1,9},{5... | collective-permute-start | bytes 786440 | tf_op jit(solution)/shard_map/ppermute | solution.py:408
  21.0 13.3 %collective-permute-start.6 = (bf16[512,256]{1,0:T(8,128)(2,1)}, bf16[512,256]{1,0:T(8,128)(2,1)S(1)}, u32[]{:S(2)}, u32[]{:S(2)}) collective-permute-start(bf16[512,256]{1,0:T(8,128)(2,1)} %relay.3), channel_id=1, source_target_pairs={{0,3},{1,2},{2,1},{3,0},{4,7},{5,6},{6,5},{7,4},{8,11},{9,10},{10,... | collective-permute-start | bytes 786440 | tf_op jit(solution)/shard_map/ppermute | solution.py:360
  23.6 6.1 %collective-permute-start.3 = (f32[16,2048]{1,0:T(8,128)S(1)}, f32[16,2048]{1,0:T(8,128)S(1)}, u32[]{:S(2)}, u32[]{:S(2)}) collective-permute-start(f32[16,2048]{1,0:T(8,128)S(1)} %get-tuple-element.30.refs_0_), channel_id=1, source_target_pairs={{0,16},{4,20},{8,24},{12,28},{16,0},{20,4},{24,8},{28,12},{1,17},{... | collective-permute-start | bytes 393224 | tf_op jit(solution)/shard_map/ppermute | solution.py:345
  25.4 18.4 %collective-permute-start.13 = (bf16[1024,256]{1,0:T(8,128)(2,1)S(1)}, bf16[1024,256]{1,0:T(8,128)(2,1)}, u32[]{:S(2)}, u32[]{:S(2)}) collective-permute-start(bf16[1024,256]{1,0:T(8,128)(2,1)S(1)} %stack_rows.2), channel_id=1, source_target_pairs={{0,16},{4,12},{8,24},{12,4},{16,0},{20,28},{24,8},{28,20},{1,17},{... | collective-permute-start | bytes 1572872 | tf_op jit(solution)/shard_map/ppermute | solution.py:408
  31.5 12.2 %collective-permute-start.4 = (bf16[128,2048]{1,0:T(8,128)(2,1)S(1)}, bf16[128,2048]{1,0:T(8,128)(2,1)S(1)}, u32[]{:S(2)}, u32[]{:S(2)}) collective-permute-start(bf16[128,2048]{1,0:T(8,128)(2,1)S(1)} %gate.1.mine_ref), channel_id=1, source_target_pairs={{0,4},{4,0},{8,12},{12,8},{16,20},{20,16},{24,28},{28,24},{1,5},{5... | collective-permute-start | bytes 1572872 | tf_op jit(solution)/shard_map/ppermute | solution.py:469
  31.7 12.6 %collective-permute-start.14 = (bf16[1024,256]{1,0:T(8,128)(2,1)S(1)}, bf16[1024,256]{1,0:T(8,128)(2,1)}, u32[]{:S(2)}, u32[]{:S(2)}) collective-permute-start(bf16[1024,256]{1,0:T(8,128)(2,1)S(1)} %stack_rows.3), channel_id=1, source_target_pairs={{0,16},{4,12},{8,24},{12,4},{16,0},{20,28},{24,8},{28,20},{1,17},{... | collective-permute-start | bytes 1572872 | tf_op jit(solution)/shard_map/ppermute | solution.py:408
  34.3 9.3 %collective-permute-start.7 = (bf16[512,256]{1,0:T(8,128)(2,1)S(1)}, bf16[512,256]{1,0:T(8,128)(2,1)}, u32[]{:S(2)}, u32[]{:S(2)}) collective-permute-start(bf16[512,256]{1,0:T(8,128)(2,1)S(1)} %relay.4.refs_0_), channel_id=1, source_target_pairs={{0,8},{4,20},{8,0},{12,28},{16,24},{20,4},{24,16},{28,12},{1,9},{5... | collective-permute-start | bytes 786440 | tf_op jit(solution)/shard_map/ppermute | solution.py:408
  35.1 12.0 %collective-permute-start.8 = (bf16[512,256]{1,0:T(8,128)(2,1)S(1)}, bf16[512,256]{1,0:T(8,128)(2,1)}, u32[]{:S(2)}, u32[]{:S(2)}) collective-permute-start(bf16[512,256]{1,0:T(8,128)(2,1)S(1)} %relay.4.refs_0_), channel_id=1, source_target_pairs={{0,16},{4,12},{8,24},{12,4},{16,0},{20,28},{24,8},{28,20},{1,17},{... | collective-permute-start | bytes 786440 | tf_op jit(solution)/shard_map/ppermute | solution.py:408
  43.7 6.7 %collective-permute-start.9 = (bf16[512,256]{1,0:T(8,128)(2,1)}, bf16[512,256]{1,0:T(8,128)(2,1)}, u32[]{:S(2)}, u32[]{:S(2)}) collective-permute-start(bf16[512,256]{1,0:T(8,128)(2,1)} %collective-permute-done.7.refs_1_), channel_id=1, source_target_pairs={{0,16},{4,12},{8,24},{12,4},{16,0},{20,28},{24,8},{28,20},{1,17},{... | collective-permute-start | bytes 786440 | tf_op jit(solution)/shard_map/ppermute | solution.py:408
  51.9 1.6 %collective-permute-start.15 = (bf16[128,1024]{1,0:T(8,128)(2,1)S(1)}, bf16[128,1024]{1,0:T(8,128)(2,1)S(1)}, u32[]{:S(2)}, u32[]{:S(2)}) collective-permute-start(bf16[128,1024]{1,0:T(8,128)(2,1)S(1)} %get-tuple-element.34), channel_id=1, source_target_pairs={{0,4},{4,0},{8,12},{12,8},{16,20},{20,16},{24,28},{28,24},{1,5},{5... | collective-permute-start | bytes 786440 | tf_op jit(solution)/shard_map/ppermute | solution.py:496

commit v6 on v5

--- a/solution.py
+++ b/solution.py
@@ -435,18 +435,16 @@
         acc_ref[:, r * block : (r + 1) * block] = total
 
 
-def far_kernel(index_ref, place_ref, mine_ref, other_ref, *refs):
+def far_kernel(first, index_ref, place_ref, gated_ref, *refs):
     index, place = index_ref[0], place_ref[0]
-    three, acc_ref, own_ref, out_ref = refs[:4], refs[4], refs[5], refs[6]
+    three, acc_ref, out_ref = refs[:4], refs[4], refs[5]
     depth, block = three[0].shape
-    rows = mine_ref.shape[0]
-    left = both_rows(mine_ref, other_ref, place ^ 3, depth)
+    rows = gated_ref.shape[0]
+    left = gated_ref[:, pl.ds(pl.multiple_of((place ^ 3) * depth, depth), depth)]
     for r, at in enumerate(block_order(index)):
-        total = acc_ref[:, r * block : (r + 1) * block] + dot(left, three[r][...])
-        total = total.astype(bf16)
+        total = acc_ref[first : first + rows, r * block : (r + 1) * block] + dot(left, three[r][...])
         cols = pl.ds(pl.multiple_of((at >> 1) * block, block), block)
-        own_ref[:, cols] = total[:rows]
-        out_ref[:, cols] = total[rows:]
+        out_ref[:, cols] = total.astype(bf16)
 
 
 def join_kernel(nums_ref, mine_ref, other_ref, out_ref):
@@ -487,13 +485,14 @@
         [jax.ShapeDtypeStruct((2 * rows, cols // 2), f32)],
         (index, place), gated, other, weight, *slots[0],
     )
-    mine, theirs = call(
-        far_kernel,
-        "project_far",
-        [jax.ShapeDtypeStruct((rows, cols // 2), bf16)] * 2,
-        (index, place), gated, other, *slots[1], acc,
+    half = [jax.ShapeDtypeStruct((rows, cols // 2), bf16)]
+    (theirs,) = call(
+        functools.partial(far_kernel, rows), "project_theirs", half, (index, place), other, *slots[1], acc
     )
     back = lax.ppermute(theirs, "ctx", swap)
+    (mine,) = call(
+        functools.partial(far_kernel, 0), "project_mine", half, (index, place), gated, *slots[1], acc
+    )
     (out,) = call(
         join_kernel,
         "join_columns",

time: 54.6 us -> 53.2 us (0.974)
  waiting for transfers between devices: 19.3 us -> 17.4 us
  Pallas kernels: 13.4 us -> 14.1 us
    pallas_call x2, Pallas kernels: 0.07 us -> 1.65 us  [stack_rows(): pl.pallas_call(stack_kernel, in_specs=[vmem, vmem], out_specs=vmem, out_s...]
    pallas_call x3 -> x4, Pallas kernels: 5.22 us -> 4.29 us  [call(): pl.pallas_call(kernel, in_specs=[smem] * len(scalars) + [vmem] * len(args...]
    ppermute x7, waiting for transfers between devices: 12.3 us -> 11.4 us  [hop(): lax.ppermute(x, 'ctx', [(i, i ^ (odd if i % 2 else even)) for i in range(...]
    ppermute x3, waiting for transfers between devices: 4.86 us -> 4.13 us  [conv_path(): other = lax.ppermute(state, 'ctx', [(i, i ^ step) for i in range(count)])]
  transfers between devices with their start and end apart: 16 -> 16, of which waited for: 7 -> 7; matrix products, arithmetic and copies ran while one was open for 0% -> 0% of each run, Pallas kernels for 17% -> 21%
where the time goes in v6:
time: 53.2 us; the launch traced here: 53.1 us
  starting transfers between devices  21.2 us (40%)
  waiting for transfers between devices  17.4 us (33%)
  Pallas kernels  14.1 us (27%)
    ppermute x7, waiting for transfers between devices, hop(): lax.ppermute(x, 'ctx', [(i, i ^ (odd if i % 2 else even)) for i in range(...  11.4 us
    ppermute x3, starting transfers between devices, conv_path(): other = lax.ppermute(state, 'ctx', [(i, i ^ step) for i in range(count)])  6.06 us
    ppermute x7, starting transfers between devices, hop(): lax.ppermute(x, 'ctx', [(i, i ^ (odd if i % 2 else even)) for i in range(...  5.54 us
    pallas_call x4, Pallas kernels, call(): pl.pallas_call(kernel, in_specs=[smem] * len(scalars) + [vmem] * len(args...  4.29 us
    ppermute x3, waiting for transfers between devices, conv_path(): other = lax.ppermute(state, 'ctx', [(i, i ^ step) for i in range(count)])  4.13 us
    ppermute x1, starting transfers between devices, local(): near = lax.ppermute(mine, 'fsdp', [(i, i ^ 1) for i in range(4)])  3.1 us
    ppermute x1, starting transfers between devices, local(): two = lax.ppermute(mine, 'fsdp', [(i, i ^ 2) for i in range(4)])  2.59 us
    ppermute x1, starting transfers between devices, conv_path(): lax.ppermute(at(mine, 'mine'), 'fsdp', [(i, i ^ 3) for i in range(4)])  2.45 us
  transfers between devices with their start and end apart: 16, of which 7 were waited for; matrix products, arithmetic and copies ran while one was open for 0% of the time, Pallas kernels for 21%

profile of v6, /device:TPU:0, one launch (start us, length us, event | category | flops | bytes accessed | tf_op | source)
XLA Modules:
  0.0 53.1 jit_solution(15271153098543325252)
XLA Ops:
  0.0 0.0 copy-start.2
  0.0 0.0 copy-start.1
  0.0 0.0 copy-start.6
  0.0 0.0 copy-start.7
  0.0 0.0 copy-start.3
  0.0 1.9 %prepare.1 = (f32[8,2048]{1,0:T(8,128)}, bf16[512,256]{1,0:T(8,128)(2,1)}) custom-call(s32[1]{0:T(128)} %bitcast.which_ref.refs_0_.index_ref.nums_ref, bf16[128,2048]{1,0:T(8,128)(2,1)} %bitcast.7, bf16[128,2048]{1,0:T(8,128)(2,1)} %bitcast.9, bf16[128,2048]{1,0:T(8,128)(2,1)} %bitcast.11, bf16[512,2048]{1,0:T(8,128)(2,1)} %weight_ref.3), custom_call_target="tpu_custom_call" | custom-call | tf_op jit(solution)/shard_map/prepare/pallas_call | solution.py:233
  1.9 0.0 copy-start.4
  1.9 3.1 %collective-permute-start.4 = (bf16[512,256]{1,0:T(8,128)(2,1)}, bf16[512,256]{1,0:T(8,128)(2,1)S(1)}, u32[]{:S(2)}, u32[]{:S(2)}) collective-permute-start(bf16[512,256]{1,0:T(8,128)(2,1)} %get-tuple-element.30.in_ref), channel_id=1, source_target_pairs={{0,1},{1,0},{2,3},{3,2},{4,5},{5,4},{6,7},{7,6},{8,9},{9,8},{10,11... | collective-permute-start | bytes 786440 | tf_op jit(solution)/shard_map/ppermute | solution.py:510
  5.0 2.6 %collective-permute-start.11 = (bf16[512,256]{1,0:T(8,128)(2,1)}, bf16[512,256]{1,0:T(8,128)(2,1)S(1)}, u32[]{:S(2)}, u32[]{:S(2)}) collective-permute-start(bf16[512,256]{1,0:T(8,128)(2,1)} %get-tuple-element.30.in_ref), channel_id=1, source_target_pairs={{0,2},{1,3},{2,0},{3,1},{4,6},{5,7},{6,4},{7,5},{8,10},{9,11},{10,... | collective-permute-start | bytes 786440 | tf_op jit(solution)/shard_map/ppermute | solution.py:511
  7.6 1.3 %collective-permute-start = (f32[8,2048]{1,0:T(8,128)}, f32[8,2048]{1,0:T(8,128)S(1)}, u32[]{:S(2)}, u32[]{:S(2)}) collective-permute-start(f32[8,2048]{1,0:T(8,128)} %get-tuple-element.18), channel_id=1, source_target_pairs={{0,4},{4,8},{8,12},{12,16},{16,20},{20,24},{24,28},{1,5},{5,9},{9,... | collective-permute-start | bytes 196616 | tf_op jit(solution)/shard_map/ppermute | solution.py:509
  8.9 0.0 copy-done.6
  8.9 0.1 copy.12.rate_ref
  9.0 0.0 copy-done.7
  9.0 0.1 copy.13.residue_ref
  9.1 2.0 %tables.1 = (bf16[16,96,256]{2,1,0:T(8,128)(2,1)S(1)}, bf16[16,64,256]{2,1,0:T(8,128)(2,1)S(1)}, f32[16,2048]{1,0:T(8,128)S(1)}) custom-call(f32[128,16]{1,0:T(8,128)S(1)} %copy.12.rate_ref, f32[128,16]{1,0:T(8,128)S(1)} %copy.13.residue_ref), custom_call_target="tpu_custom_call" | custom-call | tf_op jit(solution)/shard_map/tables/pallas_call | solution.py:297
  11.1 0.0 collective-permute-done.refs_2_
  11.1 0.0 copy-done.2
  11.1 0.0 copy-done.1
  11.1 0.0 copy-done.3
  11.1 2.3 %kv_and_state.1 = (bf16[128,2048]{1,0:T(8,128)(2,1)S(1)}, f32[128,2048]{1,0:T(8,128)S(1)}, f32[64,2048]{1,0:T(8,128)S(1)}, f32[16,2048]{1,0:T(8,128)S(1)}) custom-call(bf16[128,2048]{1,0:T(8,128)(2,1)S(1)} %bitcast.10, bf16[128,2048]{1,0:T(8,128)(2,1)S(1)} %bitcast.12, f32[8,2048]{1,0:T(8,128)S(1)} %collective-permute-done.refs_2_, ...), custom_call_target="tpu_custom_call" | custom-call | tf_op jit(solution)/shard_map/kv_and_state/pallas_call | solution.py:322
  13.4 0.0 copy-start
  13.4 0.0 copy-start.5
  13.4 2.3 %collective-permute-start.1 = (f32[16,2048]{1,0:T(8,128)S(1)}, f32[16,2048]{1,0:T(8,128)S(1)}, u32[]{:S(2)}, u32[]{:S(2)}) collective-permute-start(f32[16,2048]{1,0:T(8,128)S(1)} %get-tuple-element.24.refs_1_), channel_id=1, source_target_pairs={{0,4},{4,0},{8,12},{12,8},{16,20},{20,16},{24,28},{28,24},{1,5},{5... | collective-permute-start | bytes 393224 | tf_op jit(solution)/shard_map/ppermute | solution.py:345
  15.7 1.0 %collective-permute-done.1.refs_2_ = f32[16,2048]{1,0:T(8,128)S(1)} collective-permute-done((f32[16,2048]{1,0:T(8,128)S(1)}, f32[16,2048]{1,0:T(8,128)S(1)}, u32[]{:S(2)}, u32[]{:S(2)}) %collective-permute-start.1) | collective-permute-done | bytes 131104 | tf_op jit(solution)/shard_map/ppermute | solution.py:345
  16.7 0.1 blend_states.2
  16.8 2.0 %collective-permute-start.2 = (f32[16,2048]{1,0:T(8,128)S(1)}, f32[16,2048]{1,0:T(8,128)S(1)}, u32[]{:S(2)}, u32[]{:S(2)}) collective-permute-start(f32[16,2048]{1,0:T(8,128)S(1)} %get-tuple-element.25.refs_1_.refs_0_), channel_id=1, source_target_pairs={{0,8},{4,12},{8,0},{12,4},{16,24},{20,28},{24,16},{28,20},{1,9},{5... | collective-permute-start | bytes 393224 | tf_op jit(solution)/shard_map/ppermute | solution.py:345
  18.8 0.0 collective-permute-done.4.refs_0_.one_ref
  18.8 0.1 collective-permute-start.10
  18.9 0.7 %collective-permute-done.11.in_ref = bf16[512,256]{1,0:T(8,128)(2,1)S(1)} collective-permute-done((bf16[512,256]{1,0:T(8,128)(2,1)}, bf16[512,256]{1,0:T(8,128)(2,1)S(1)}, u32[]{:S(2)}, u32[]{:S(2)}) %collective-permute-start.11) | collective-permute-done | bytes 262176 | tf_op jit(solution)/shard_map/ppermute | solution.py:511
  19.6 1.5 %collective-permute-start.12 = (bf16[512,256]{1,0:T(8,128)(2,1)S(1)}, bf16[512,256]{1,0:T(8,128)(2,1)S(1)}, u32[]{:S(2)}, u32[]{:S(2)}) collective-permute-start(bf16[512,256]{1,0:T(8,128)(2,1)S(1)} %relay.5.two_ref.refs_2_), channel_id=1, source_target_pairs={{0,8},{4,20},{8,0},{12,28},{16,24},{20,4},{24,16},{28,12},{1,9},{5... | collective-permute-start | bytes 786440 | tf_op jit(solution)/shard_map/ppermute | solution.py:408
  21.0 0.0 copy-done.4
  21.1 2.5 %collective-permute-start.5 = (bf16[512,256]{1,0:T(8,128)(2,1)S(1)}, bf16[512,256]{1,0:T(8,128)(2,1)S(1)}, u32[]{:S(2)}, u32[]{:S(2)}) collective-permute-start(bf16[512,256]{1,0:T(8,128)(2,1)S(1)} %relay.3), channel_id=1, source_target_pairs={{0,3},{1,2},{2,1},{3,0},{4,7},{5,6},{6,5},{7,4},{8,11},{9,10},{10,... | collective-permute-start | bytes 786440 | tf_op jit(solution)/shard_map/ppermute | solution.py:360
  23.5 0.0 collective-permute-done.2.refs_2_
  23.5 0.1 blend_states.3
  23.6 1.8 %collective-permute-start.3 = (f32[16,2048]{1,0:T(8,128)S(1)}, f32[16,2048]{1,0:T(8,128)S(1)}, u32[]{:S(2)}, u32[]{:S(2)}) collective-permute-start(f32[16,2048]{1,0:T(8,128)S(1)} %get-tuple-element.28.refs_0_), channel_id=1, source_target_pairs={{0,16},{4,20},{8,24},{12,28},{16,0},{20,4},{24,8},{28,12},{1,17},{... | collective-permute-start | bytes 393224 | tf_op jit(solution)/shard_map/ppermute | solution.py:345
  25.4 0.8 %stack_rows.2 = bf16[1024,256]{1,0:T(8,128)(2,1)} custom-call(bf16[512,256]{1,0:T(8,128)(2,1)S(1)} %collective-permute-done.4.refs_0_.one_ref, bf16[512,256]{1,0:T(8,128)(2,1)S(1)} %relay.5.two_ref.refs_2_), custom_call_target="tpu_custom_call" | custom-call | tf_op jit(solution)/shard_map/stack_rows/pallas_call | solution.py:256
  26.2 0.3 collective-permute-start.13
  26.5 3.1 %collective-permute-done.3.refs_8_ = f32[16,2048]{1,0:T(8,128)S(1)} collective-permute-done((f32[16,2048]{1,0:T(8,128)S(1)}, f32[16,2048]{1,0:T(8,128)S(1)}, u32[]{:S(2)}, u32[]{:S(2)}) %collective-permute-start.3) | collective-permute-done | bytes 131104 | tf_op jit(solution)/shard_map/ppermute | solution.py:345
  29.7 0.0 copy-done
  29.7 0.0 copy-done.5
  29.7 1.9 %gate.1.mine_ref.gated_ref = bf16[128,2048]{1,0:T(8,128)(2,1)S(1)} custom-call(s32[1]{0:T(128)} %bitcast.which_ref.refs_0_.index_ref.nums_ref, bf16[128,2048]{1,0:T(8,128)(2,1)S(1)} %bitcast.8, f32[8,2048]{1,0:T(8,128)S(1)} %collective-permute-done.refs_2_, f32[3,3,2048]{2,1,0:T(4,128)S(1)} %copy-done.3, bf16[128,2048]{1,0:T(8,128)(2,1)S(1)} %get-tuple-element.21.refs_4_, ...), custom_call_target="tpu_custom_call" | custom-call | tf_op jit(solution)/shard_map/gate/pallas_call | solution.py:378
  31.6 0.1 collective-permute-start.9
  31.6 0.0 collective-permute-done.10.one_ref.refs_1_
  31.6 0.0 collective-permute-done.12.two_ref.refs_3_
  31.7 0.8 %stack_rows.3 = bf16[1024,256]{1,0:T(8,128)(2,1)} custom-call(bf16[512,256]{1,0:T(8,128)(2,1)S(1)} %collective-permute-done.10.one_ref.refs_1_, bf16[512,256]{1,0:T(8,128)(2,1)S(1)} %collective-permute-done.12.two_ref.refs_3_), custom_call_target="tpu_custom_call" | custom-call | tf_op jit(solution)/shard_map/stack_rows/pallas_call | solution.py:256
  32.5 1.6 %collective-permute-start.14 = (bf16[1024,256]{1,0:T(8,128)(2,1)}, bf16[1024,256]{1,0:T(8,128)(2,1)}, u32[]{:S(2)}, u32[]{:S(2)}) collective-permute-start(bf16[1024,256]{1,0:T(8,128)(2,1)} %stack_rows.3), channel_id=1, source_target_pairs={{0,16},{4,12},{8,24},{12,4},{16,0},{20,28},{24,8},{28,20},{1,17},{... | collective-permute-start | bytes 1572872 | tf_op jit(solution)/shard_map/ppermute | solution.py:408
  34.1 0.0 collective-permute-done.5.in_ref
  34.1 1.7 %collective-permute-start.6 = (bf16[512,256]{1,0:T(8,128)(2,1)S(1)}, bf16[512,256]{1,0:T(8,128)(2,1)S(1)}, u32[]{:S(2)}, u32[]{:S(2)}) collective-permute-start(bf16[512,256]{1,0:T(8,128)(2,1)S(1)} %relay.4.refs_0_), channel_id=1, source_target_pairs={{0,8},{4,20},{8,0},{12,28},{16,24},{20,4},{24,16},{28,12},{1,9},{5... | collective-permute-start | bytes 786440 | tf_op jit(solution)/shard_map/ppermute | solution.py:408
  35.8 0.0 collective-permute-start.7
  35.8 7.5 %collective-permute-done.6.refs_1_ = bf16[512,256]{1,0:T(8,128)(2,1)S(1)} collective-permute-done((bf16[512,256]{1,0:T(8,128)(2,1)S(1)}, bf16[512,256]{1,0:T(8,128)(2,1)S(1)}, u32[]{:S(2)}, u32[]{:S(2)}) %collective-permute-start.6) | collective-permute-done | bytes 262176 | tf_op jit(solution)/shard_map/ppermute | solution.py:408
  43.4 0.3 collective-permute-start.8
  43.7 0.0 collective-permute-done.13.refs_4_
  43.7 0.0 collective-permute-done.9.other_ref.gated_ref
  43.7 1.1 %collective-permute-done.14.refs_5_ = bf16[1024,256]{1,0:T(8,128)(2,1)} collective-permute-done((bf16[1024,256]{1,0:T(8,128)(2,1)}, bf16[1024,256]{1,0:T(8,128)(2,1)}, u32[]{:S(2)}, u32[]{:S(2)}) %collective-permute-start.14) | collective-permute-done | bytes 524320 | tf_op jit(solution)/shard_map/ppermute | solution.py:408
  44.8 2.8 %project_near.1.refs_4_ = f32[256,1024]{1,0:T(8,128)S(1)} custom-call(s32[1]{0:T(128)} %bitcast.which_ref.refs_0_.index_ref.nums_ref, s32[1]{0:T(128)} %bitcast.1.place_ref, bf16[128,2048]{1,0:T(8,128)(2,1)S(1)} %gate.1.mine_ref.gated_ref, bf16[128,2048]{1,0:T(8,128)(2,1)S(1)} %collective-permute-done.9.other_ref.gated_ref, bf16[512,2048]{1,0:T(8,128)(2,1)} %weight_ref.3, ...), custom_call_target="tpu_custom_call" | custom-call | tf_op jit(solution)/shard_map/project_near/pallas_call | solution.py:472
  47.6 0.0 collective-permute-done.7.refs_2_
  47.6 2.7 %collective-permute-done.8.refs_3_ = bf16[512,256]{1,0:T(8,128)(2,1)S(1)} collective-permute-done((bf16[512,256]{1,0:T(8,128)(2,1)S(1)}, bf16[512,256]{1,0:T(8,128)(2,1)S(1)}, u32[]{:S(2)}, u32[]{:S(2)}) %collective-permute-start.8) | collective-permute-done | bytes 262176 | tf_op jit(solution)/shard_map/ppermute | solution.py:408
  50.3 0.3 project_theirs.1
  50.6 0.1 collective-permute-start.15
  50.7 0.3 project_mine.1.mine_ref
  51.0 1.2 %collective-permute-done.15.other_ref = bf16[128,1024]{1,0:T(8,128)(2,1)S(1)} collective-permute-done((bf16[128,1024]{1,0:T(8,128)(2,1)S(1)}, bf16[128,1024]{1,0:T(8,128)(2,1)S(1)}, u32[]{:S(2)}, u32[]{:S(2)}) %collective-permute-start.15) | collective-permute-done | bytes 262176 | tf_op jit(solution)/shard_map/ppermute | solution.py:492
  52.2 0.8 %join_columns.1 = bf16[128,2048]{1,0:T(8,128)(2,1)} custom-call(s32[1]{0:T(128)} %bitcast.which_ref.refs_0_.index_ref.nums_ref, bf16[128,1024]{1,0:T(8,128)(2,1)S(1)} %project_mine.1.mine_ref, bf16[128,1024]{1,0:T(8,128)(2,1)S(1)} %collective-permute-done.15.other_ref), custom_call_target="tpu_custom_call" | custom-call | tf_op jit(solution)/shard_map/join_columns/pallas_call | solution.py:472
  (4 shorter events, 0.0 us)
Async XLA Ops:
  0.0 11.1 %copy-start.2 = (bf16[1,128,2048]{2,1,0:T(8,128)(2,1)S(1)}, bf16[1,128,2048]{2,1,0:T(8,128)(2,1)}, u32[]{:S(2)}) copy-start(bf16[1,128,2048]{2,1,0:T(8,128)(2,1)} %param.10) | copy-start | bytes 1572868
  0.0 11.1 %copy-start.1 = (bf16[1,128,2048]{2,1,0:T(8,128)(2,1)S(1)}, bf16[1,128,2048]{2,1,0:T(8,128)(2,1)}, u32[]{:S(2)}) copy-start(bf16[1,128,2048]{2,1,0:T(8,128)(2,1)} %param.9) | copy-start | bytes 1572868
  0.0 8.9 %copy-start.6 = (f32[128,16]{0,1:T(8,128)S(1)}, f32[128,16]{0,1:T(8,128)}, u32[]{:S(2)}) copy-start(f32[128,16]{0,1:T(8,128)} %param.12) | copy-start | bytes 24580
  0.0 9.0 %copy-start.7 = (f32[128,16]{0,1:T(8,128)S(1)}, f32[128,16]{0,1:T(8,128)}, u32[]{:S(2)}) copy-start(f32[128,16]{0,1:T(8,128)} %param.13) | copy-start | bytes 24580
  0.0 11.1 %copy-start.3 = (f32[3,3,2048]{2,1,0:T(4,128)S(1)}, f32[3,3,2048]{2,1,0:T(4,128)}, u32[]{:S(2)}) copy-start(f32[3,3,2048]{2,1,0:T(4,128)} %refs_3_.3) | copy-start | bytes 221188
  1.9 19.2 %copy-start.4 = (bf16[512,256]{1,0:T(8,128)(2,1)S(1)}, bf16[512,256]{1,0:T(8,128)(2,1)}, u32[]{:S(2)}) copy-start(bf16[512,256]{1,0:T(8,128)(2,1)} %get-tuple-element.30.in_ref) | copy-start | bytes 786436
  1.9 16.9 %collective-permute-start.4 = (bf16[512,256]{1,0:T(8,128)(2,1)}, bf16[512,256]{1,0:T(8,128)(2,1)S(1)}, u32[]{:S(2)}, u32[]{:S(2)}) collective-permute-start(bf16[512,256]{1,0:T(8,128)(2,1)} %get-tuple-element.30.in_ref), channel_id=1, source_target_pairs={{0,1},{1,0},{2,3},{3,2},{4,5},{5,4},{6,7},{7,6},{8,9},{9,8},{10,11... | collective-permute-start | bytes 786440 | tf_op jit(solution)/shard_map/ppermute | solution.py:510
  5.0 14.6 %collective-permute-start.11 = (bf16[512,256]{1,0:T(8,128)(2,1)}, bf16[512,256]{1,0:T(8,128)(2,1)S(1)}, u32[]{:S(2)}, u32[]{:S(2)}) collective-permute-start(bf16[512,256]{1,0:T(8,128)(2,1)} %get-tuple-element.30.in_ref), channel_id=1, source_target_pairs={{0,2},{1,3},{2,0},{3,1},{4,6},{5,7},{6,4},{7,5},{8,10},{9,11},{10,... | collective-permute-start | bytes 786440 | tf_op jit(solution)/shard_map/ppermute | solution.py:511
  7.6 3.5 %collective-permute-start = (f32[8,2048]{1,0:T(8,128)}, f32[8,2048]{1,0:T(8,128)S(1)}, u32[]{:S(2)}, u32[]{:S(2)}) collective-permute-start(f32[8,2048]{1,0:T(8,128)} %get-tuple-element.18), channel_id=1, source_target_pairs={{0,4},{4,8},{8,12},{12,16},{16,20},{20,24},{24,28},{1,5},{5,9},{9,... | collective-permute-start | bytes 196616 | tf_op jit(solution)/shard_map/ppermute | solution.py:509
  13.4 16.3 %copy-start = (bf16[1,128,2048]{2,1,0:T(8,128)(2,1)S(1)}, bf16[1,128,2048]{2,1,0:T(8,128)(2,1)}, u32[]{:S(2)}) copy-start(bf16[1,128,2048]{2,1,0:T(8,128)(2,1)} %param.8) | copy-start | bytes 1572868
  13.4 16.3 %copy-start.5 = (f32[2048]{0:T(1024)S(1)}, f32[2048]{0:T(1024)}, u32[]{:S(2)}) copy-start(f32[2048]{0:T(1024)} %param.14) | copy-start | bytes 24580
  13.4 3.3 %collective-permute-start.1 = (f32[16,2048]{1,0:T(8,128)S(1)}, f32[16,2048]{1,0:T(8,128)S(1)}, u32[]{:S(2)}, u32[]{:S(2)}) collective-permute-start(f32[16,2048]{1,0:T(8,128)S(1)} %get-tuple-element.24.refs_1_), channel_id=1, source_target_pairs={{0,4},{4,0},{8,12},{12,8},{16,20},{20,16},{24,28},{28,24},{1,5},{5... | collective-permute-start | bytes 393224 | tf_op jit(solution)/shard_map/ppermute | solution.py:345
  16.8 6.7 %collective-permute-start.2 = (f32[16,2048]{1,0:T(8,128)S(1)}, f32[16,2048]{1,0:T(8,128)S(1)}, u32[]{:S(2)}, u32[]{:S(2)}) collective-permute-start(f32[16,2048]{1,0:T(8,128)S(1)} %get-tuple-element.25.refs_1_.refs_0_), channel_id=1, source_target_pairs={{0,8},{4,12},{8,0},{12,4},{16,24},{20,28},{24,16},{28,20},{1,9},{5... | collective-permute-start | bytes 393224 | tf_op jit(solution)/shard_map/ppermute | solution.py:345
  18.8 12.9 %collective-permute-start.10 = (bf16[512,256]{1,0:T(8,128)(2,1)S(1)}, bf16[512,256]{1,0:T(8,128)(2,1)S(1)}, u32[]{:S(2)}, u32[]{:S(2)}) collective-permute-start(bf16[512,256]{1,0:T(8,128)(2,1)S(1)} %collective-permute-done.4.refs_0_.one_ref), channel_id=1, source_target_pairs={{0,8},{4,20},{8,0},{12,28},{16,24},{20,4},{24,16},{28,12},{1,9},{5... | collective-permute-start | bytes 786440 | tf_op jit(solution)/shard_map/ppermute | solution.py:408
  19.6 12.1 %collective-permute-start.12 = (bf16[512,256]{1,0:T(8,128)(2,1)S(1)}, bf16[512,256]{1,0:T(8,128)(2,1)S(1)}, u32[]{:S(2)}, u32[]{:S(2)}) collective-permute-start(bf16[512,256]{1,0:T(8,128)(2,1)S(1)} %relay.5.two_ref.refs_2_), channel_id=1, source_target_pairs={{0,8},{4,20},{8,0},{12,28},{16,24},{20,4},{24,16},{28,12},{1,9},{5... | collective-permute-start | bytes 786440 | tf_op jit(solution)/shard_map/ppermute | solution.py:408
  21.1 13.1 %collective-permute-start.5 = (bf16[512,256]{1,0:T(8,128)(2,1)S(1)}, bf16[512,256]{1,0:T(8,128)(2,1)S(1)}, u32[]{:S(2)}, u32[]{:S(2)}) collective-permute-start(bf16[512,256]{1,0:T(8,128)(2,1)S(1)} %relay.3), channel_id=1, source_target_pairs={{0,3},{1,2},{2,1},{3,0},{4,7},{5,6},{6,5},{7,4},{8,11},{9,10},{10,... | collective-permute-start | bytes 786440 | tf_op jit(solution)/shard_map/ppermute | solution.py:360
  23.6 6.1 %collective-permute-start.3 = (f32[16,2048]{1,0:T(8,128)S(1)}, f32[16,2048]{1,0:T(8,128)S(1)}, u32[]{:S(2)}, u32[]{:S(2)}) collective-permute-start(f32[16,2048]{1,0:T(8,128)S(1)} %get-tuple-element.28.refs_0_), channel_id=1, source_target_pairs={{0,16},{4,20},{8,24},{12,28},{16,0},{20,4},{24,8},{28,12},{1,17},{... | collective-permute-start | bytes 393224 | tf_op jit(solution)/shard_map/ppermute | solution.py:345
  26.2 17.4 %collective-permute-start.13 = (bf16[1024,256]{1,0:T(8,128)(2,1)}, bf16[1024,256]{1,0:T(8,128)(2,1)}, u32[]{:S(2)}, u32[]{:S(2)}) collective-permute-start(bf16[1024,256]{1,0:T(8,128)(2,1)} %stack_rows.2), channel_id=1, source_target_pairs={{0,16},{4,12},{8,24},{12,4},{16,0},{20,28},{24,8},{28,20},{1,17},{... | collective-permute-start | bytes 1572872 | tf_op jit(solution)/shard_map/ppermute | solution.py:408
  31.6 12.1 %collective-permute-start.9 = (bf16[128,2048]{1,0:T(8,128)(2,1)S(1)}, bf16[128,2048]{1,0:T(8,128)(2,1)S(1)}, u32[]{:S(2)}, u32[]{:S(2)}) collective-permute-start(bf16[128,2048]{1,0:T(8,128)(2,1)S(1)} %gate.1.mine_ref.gated_ref), channel_id=1, source_target_pairs={{0,4},{4,0},{8,12},{12,8},{16,20},{20,16},{24,28},{28,24},{1,5},{5... | collective-permute-start | bytes 1572872 | tf_op jit(solution)/shard_map/ppermute | solution.py:467
  32.5 12.3 %collective-permute-start.14 = (bf16[1024,256]{1,0:T(8,128)(2,1)}, bf16[1024,256]{1,0:T(8,128)(2,1)}, u32[]{:S(2)}, u32[]{:S(2)}) collective-permute-start(bf16[1024,256]{1,0:T(8,128)(2,1)} %stack_rows.3), channel_id=1, source_target_pairs={{0,16},{4,12},{8,24},{12,4},{16,0},{20,28},{24,8},{28,20},{1,17},{... | collective-permute-start | bytes 1572872 | tf_op jit(solution)/shard_map/ppermute | solution.py:408
  34.1 9.2 %collective-permute-start.6 = (bf16[512,256]{1,0:T(8,128)(2,1)S(1)}, bf16[512,256]{1,0:T(8,128)(2,1)S(1)}, u32[]{:S(2)}, u32[]{:S(2)}) collective-permute-start(bf16[512,256]{1,0:T(8,128)(2,1)S(1)} %relay.4.refs_0_), channel_id=1, source_target_pairs={{0,8},{4,20},{8,0},{12,28},{16,24},{20,4},{24,16},{28,12},{1,9},{5... | collective-permute-start | bytes 786440 | tf_op jit(solution)/shard_map/ppermute | solution.py:408
  35.8 11.8 %collective-permute-start.7 = (bf16[512,256]{1,0:T(8,128)(2,1)S(1)}, bf16[512,256]{1,0:T(8,128)(2,1)S(1)}, u32[]{:S(2)}, u32[]{:S(2)}) collective-permute-start(bf16[512,256]{1,0:T(8,128)(2,1)S(1)} %relay.4.refs_0_), channel_id=1, source_target_pairs={{0,16},{4,12},{8,24},{12,4},{16,0},{20,28},{24,8},{28,20},{1,17},{... | collective-permute-start | bytes 786440 | tf_op jit(solution)/shard_map/ppermute | solution.py:408
  43.4 6.9 %collective-permute-start.8 = (bf16[512,256]{1,0:T(8,128)(2,1)S(1)}, bf16[512,256]{1,0:T(8,128)(2,1)S(1)}, u32[]{:S(2)}, u32[]{:S(2)}) collective-permute-start(bf16[512,256]{1,0:T(8,128)(2,1)S(1)} %collective-permute-done.6.refs_1_), channel_id=1, source_target_pairs={{0,16},{4,12},{8,24},{12,4},{16,0},{20,28},{24,8},{28,20},{1,17},{... | collective-permute-start | bytes 786440 | tf_op jit(solution)/shard_map/ppermute | solution.py:408
  50.6 1.6 %collective-permute-start.15 = (bf16[128,1024]{1,0:T(8,128)(2,1)S(1)}, bf16[128,1024]{1,0:T(8,128)(2,1)S(1)}, u32[]{:S(2)}, u32[]{:S(2)}) collective-permute-start(bf16[128,1024]{1,0:T(8,128)(2,1)S(1)} %project_theirs.1), channel_id=1, source_target_pairs={{0,4},{4,0},{8,12},{12,8},{16,20},{20,16},{24,28},{28,24},{1,5},{5... | collective-permute-start | bytes 786440 | tf_op jit(solution)/shard_map/ppermute | solution.py:492

commit v7 on v6

--- a/solution.py
+++ b/solution.py
@@ -11,7 +11,7 @@
 HOLD = [[], [], [], []]
 RELAY = {'z1': [], 'a1': [], 'mine': ['z1'], 'z2': ['s1'], 'z3': ['s2'], 'a3': []}
 FEAT = 3
-WIDE = 512
+WIDE = 1024
 LANES = 128
 SUB = 32
 VMEM_LIMIT = 48 << 20
@@ -89,8 +89,9 @@
     end_high, end_low = split(ends)
     causal = iota((sub, LANES), 0) >= iota((sub, LANES), 1) % sub
     start = iota((1, LANES), 1) % sub == 0
-    mode_pick = iota((modes, each * modes), 0) == iota((modes, each * modes), 1) % modes
-    group_at = iota((groups, each * modes), 1) // modes
+    spread = rate_chan_ref[...] if modes == GROUP else expand(rate_turned, modes, groups * modes)
+    mode_pick = iota((modes, groups * modes), 0) == iota((modes, groups * modes), 1) % modes
+    rate_lane = jnp.sum(jnp.where(mode_pick, spread, 0.0), axis=0, keepdims=True)
     ahead = (iota((sub, each * modes), 0) + 1).astype(f32)
     for b in range(blocks):
         for part in range(depth // LANES):
@@ -105,14 +106,8 @@
         cols = slice(b * depth, (b + 1) * depth)
         left_ref[b, 2 * sub : 2 * sub + modes] = end_high[:, cols]
         left_ref[b, 2 * sub + modes :] = end_low[:, cols]
-        spread = jnp.dot(
-            (iota((groups, each * modes), 0) == b * each + group_at).astype(f32).T,
-            rate,
-            precision=lax.Precision.HIGHEST,
-            preferred_element_type=f32,
-        )
-        rate_lane = jnp.sum(jnp.where(mode_pick, spread.T, 0.0), axis=0, keepdims=True)
-        high, low = split(jnp.exp(-rate_lane * ahead))
+        lane = rate_lane[:, b * each * modes : (b + 1) * each * modes]
+        high, low = split(jnp.exp(-lane * ahead))
         lag_ref[b, :sub] = jnp.concatenate([high, high], axis=1)
         lag_ref[b, sub:] = jnp.concatenate([low, jnp.zeros_like(low)], axis=1)
 
@@ -507,8 +502,8 @@
     tails, mine = prepare(query, key, value, out_weight)
     count = lax.axis_size("ctx")
     halo = lax.ppermute(tails, "ctx", [(i, i + 1) for i in range(count - 1)])
+    two = lax.ppermute(mine, "fsdp", [(i, i ^ 2) for i in range(4)])
     near = lax.ppermute(mine, "fsdp", [(i, i ^ 1) for i in range(4)])
-    two = lax.ppermute(mine, "fsdp", [(i, i ^ 2) for i in range(4)])
     gated, slots = conv_path(
         query, key, value, halo, near, two, mine, decay_rate, residues, feature_taps, skip_gain
     )

time: 53.2 us -> 52.7 us (level)
  Pallas kernels: 14.1 us -> 12.7 us
  starting transfers between devices: 21.2 us -> 21.9 us
    pallas_call x1, Pallas kernels: 1.98 us -> 1.08 us  [conv_path(): pl.pallas_call(table_kernel, in_specs=[vmem, vmem], out_specs=[vmem] * 3,...]
    ppermute x3, starting transfers between devices: 6.06 us -> 6.73 us  [conv_path(): other = lax.ppermute(state, 'ctx', [(i, i ^ step) for i in range(count)])]
  transfers between devices with their start and end apart: 16 -> 16, of which waited for: 7 -> 7; matrix products, arithmetic and copies ran while one was open for 0% -> 0% of each run, Pallas kernels for 21% -> 18%
where the time goes in v7:
time: 52.7 us; the launch traced here: 52.6 us
  starting transfers between devices  21.9 us (42%)
  waiting for transfers between devices  17.5 us (33%)
  Pallas kernels  12.7 us (24%)
    ppermute x7, waiting for transfers between devices, hop(): lax.ppermute(x, 'ctx', [(i, i ^ (odd if i % 2 else even)) for i in range(...  11.6 us
    ppermute x3, starting transfers between devices, conv_path(): other = lax.ppermute(state, 'ctx', [(i, i ^ step) for i in range(count)])  6.73 us
    ppermute x7, starting transfers between devices, hop(): lax.ppermute(x, 'ctx', [(i, i ^ (odd if i % 2 else even)) for i in range(...  5.65 us
    pallas_call x4, Pallas kernels, call(): pl.pallas_call(kernel, in_specs=[smem] * len(scalars) + [vmem] * len(args...  4.29 us
    ppermute x3, waiting for transfers between devices, conv_path(): other = lax.ppermute(state, 'ctx', [(i, i ^ step) for i in range(count)])  3.76 us
    ppermute x1, starting transfers between devices, local(): near = lax.ppermute(mine, 'fsdp', [(i, i ^ 1) for i in range(4)])  3.1 us
    ppermute x1, starting transfers between devices, local(): two = lax.ppermute(mine, 'fsdp', [(i, i ^ 2) for i in range(4)])  2.59 us
    ppermute x1, starting transfers between devices, conv_path(): lax.ppermute(at(mine, 'mine'), 'fsdp', [(i, i ^ 3) for i in range(4)])  2.45 us
  transfers between devices with their start and end apart: 16, of which 7 were waited for; matrix products, arithmetic and copies ran while one was open for 0% of the time, Pallas kernels for 18%

profile of v7, /device:TPU:0, one launch (start us, length us, event | category | flops | bytes accessed | tf_op | source)
XLA Modules:
  0.0 52.6 jit_solution(8230896062526861203)
XLA Ops:
  0.0 0.0 copy-start.2
  0.0 0.0 copy-start.1
  0.0 0.0 copy-start.6
  0.0 0.0 copy-start.7
  0.0 0.0 copy-start.3
  0.0 1.9 %prepare.1 = (f32[8,2048]{1,0:T(8,128)}, bf16[512,256]{1,0:T(8,128)(2,1)}) custom-call(s32[1]{0:T(128)} %bitcast.which_ref.refs_0_.index_ref.nums_ref, bf16[128,2048]{1,0:T(8,128)(2,1)} %bitcast.7, bf16[128,2048]{1,0:T(8,128)(2,1)} %bitcast.9, bf16[128,2048]{1,0:T(8,128)(2,1)} %bitcast.11, bf16[512,2048]{1,0:T(8,128)(2,1)} %weight_ref.3), custom_call_target="tpu_custom_call" | custom-call | tf_op jit(solution)/shard_map/prepare/pallas_call | solution.py:228
  1.9 0.0 copy-start.4
  1.9 3.1 %collective-permute-start.4 = (bf16[512,256]{1,0:T(8,128)(2,1)}, bf16[512,256]{1,0:T(8,128)(2,1)S(1)}, u32[]{:S(2)}, u32[]{:S(2)}) collective-permute-start(bf16[512,256]{1,0:T(8,128)(2,1)} %get-tuple-element.30.in_ref), channel_id=1, source_target_pairs={{0,1},{1,0},{2,3},{3,2},{4,5},{5,4},{6,7},{7,6},{8,9},{9,8},{10,11... | collective-permute-start | bytes 786440 | tf_op jit(solution)/shard_map/ppermute | solution.py:506
  5.0 2.6 %collective-permute-start.11 = (bf16[512,256]{1,0:T(8,128)(2,1)}, bf16[512,256]{1,0:T(8,128)(2,1)S(1)}, u32[]{:S(2)}, u32[]{:S(2)}) collective-permute-start(bf16[512,256]{1,0:T(8,128)(2,1)} %get-tuple-element.30.in_ref), channel_id=1, source_target_pairs={{0,2},{1,3},{2,0},{3,1},{4,6},{5,7},{6,4},{7,5},{8,10},{9,11},{10,... | collective-permute-start | bytes 786440 | tf_op jit(solution)/shard_map/ppermute | solution.py:505
  7.6 1.3 %collective-permute-start = (f32[8,2048]{1,0:T(8,128)}, f32[8,2048]{1,0:T(8,128)S(1)}, u32[]{:S(2)}, u32[]{:S(2)}) collective-permute-start(f32[8,2048]{1,0:T(8,128)} %get-tuple-element.18), channel_id=1, source_target_pairs={{0,4},{4,8},{8,12},{12,16},{16,20},{20,24},{24,28},{1,5},{5,9},{9,... | collective-permute-start | bytes 196616 | tf_op jit(solution)/shard_map/ppermute | solution.py:504
  8.9 0.0 copy-done.6
  8.9 0.1 copy.12.rate_ref
  9.0 0.0 copy-done.7
  9.0 0.1 copy.13.residue_ref
  9.1 1.1 %tables.1 = (bf16[16,96,256]{2,1,0:T(8,128)(2,1)S(1)}, bf16[16,64,256]{2,1,0:T(8,128)(2,1)S(1)}, f32[16,2048]{1,0:T(8,128)S(1)}) custom-call(f32[128,16]{1,0:T(8,128)S(1)} %copy.12.rate_ref, f32[128,16]{1,0:T(8,128)S(1)} %copy.13.residue_ref), custom_call_target="tpu_custom_call" | custom-call | tf_op jit(solution)/shard_map/tables/pallas_call | solution.py:292
  10.2 0.0 collective-permute-done.refs_2_
  10.2 0.0 copy-done.2
  10.2 0.0 copy-done.1
  10.2 0.0 copy-done.3
  10.2 1.9 %kv_and_state.1 = (bf16[128,2048]{1,0:T(8,128)(2,1)S(1)}, f32[128,2048]{1,0:T(8,128)S(1)}, f32[64,2048]{1,0:T(8,128)S(1)}, f32[16,2048]{1,0:T(8,128)S(1)}) custom-call(bf16[128,2048]{1,0:T(8,128)(2,1)S(1)} %bitcast.10, bf16[128,2048]{1,0:T(8,128)(2,1)S(1)} %bitcast.12, f32[8,2048]{1,0:T(8,128)S(1)} %collective-permute-done.refs_2_, ...), custom_call_target="tpu_custom_call" | custom-call | tf_op jit(solution)/shard_map/kv_and_state/pallas_call | solution.py:317
  12.1 0.0 copy-start
  12.2 0.0 copy-start.5
  12.2 2.6 %collective-permute-start.1 = (f32[16,2048]{1,0:T(8,128)S(1)}, f32[16,2048]{1,0:T(8,128)S(1)}, u32[]{:S(2)}, u32[]{:S(2)}) collective-permute-start(f32[16,2048]{1,0:T(8,128)S(1)} %get-tuple-element.24.refs_1_), channel_id=1, source_target_pairs={{0,4},{4,0},{8,12},{12,8},{16,20},{20,16},{24,28},{28,24},{1,5},{5... | collective-permute-start | bytes 393224 | tf_op jit(solution)/shard_map/ppermute | solution.py:340
  14.7 1.0 %collective-permute-done.1.refs_2_ = f32[16,2048]{1,0:T(8,128)S(1)} collective-permute-done((f32[16,2048]{1,0:T(8,128)S(1)}, f32[16,2048]{1,0:T(8,128)S(1)}, u32[]{:S(2)}, u32[]{:S(2)}) %collective-permute-start.1) | collective-permute-done | bytes 131104 | tf_op jit(solution)/shard_map/ppermute | solution.py:340
  15.7 0.1 blend_states.2
  15.8 2.6 %collective-permute-start.2 = (f32[16,2048]{1,0:T(8,128)S(1)}, f32[16,2048]{1,0:T(8,128)S(1)}, u32[]{:S(2)}, u32[]{:S(2)}) collective-permute-start(f32[16,2048]{1,0:T(8,128)S(1)} %get-tuple-element.25.refs_1_.refs_0_), channel_id=1, source_target_pairs={{0,8},{4,12},{8,0},{12,4},{16,24},{20,28},{24,16},{28,20},{1,9},{5... | collective-permute-start | bytes 393224 | tf_op jit(solution)/shard_map/ppermute | solution.py:340
  18.4 0.0 collective-permute-done.4.refs_0_.one_ref
  18.4 0.3 collective-permute-start.10
  18.7 0.9 %collective-permute-done.11.in_ref = bf16[512,256]{1,0:T(8,128)(2,1)S(1)} collective-permute-done((bf16[512,256]{1,0:T(8,128)(2,1)}, bf16[512,256]{1,0:T(8,128)(2,1)S(1)}, u32[]{:S(2)}, u32[]{:S(2)}) %collective-permute-start.11) | collective-permute-done | bytes 262176 | tf_op jit(solution)/shard_map/ppermute | solution.py:505
  19.6 1.5 %collective-permute-start.12 = (bf16[512,256]{1,0:T(8,128)(2,1)S(1)}, bf16[512,256]{1,0:T(8,128)(2,1)S(1)}, u32[]{:S(2)}, u32[]{:S(2)}) collective-permute-start(bf16[512,256]{1,0:T(8,128)(2,1)S(1)} %relay.5.two_ref.refs_2_), channel_id=1, source_target_pairs={{0,8},{4,20},{8,0},{12,28},{16,24},{20,4},{24,16},{28,12},{1,9},{5... | collective-permute-start | bytes 786440 | tf_op jit(solution)/shard_map/ppermute | solution.py:403
  21.0 0.0 copy-done.4
  21.1 2.5 %collective-permute-start.5 = (bf16[512,256]{1,0:T(8,128)(2,1)S(1)}, bf16[512,256]{1,0:T(8,128)(2,1)S(1)}, u32[]{:S(2)}, u32[]{:S(2)}) collective-permute-start(bf16[512,256]{1,0:T(8,128)(2,1)S(1)} %relay.3), channel_id=1, source_target_pairs={{0,3},{1,2},{2,1},{3,0},{4,7},{5,6},{6,5},{7,4},{8,11},{9,10},{10,... | collective-permute-start | bytes 786440 | tf_op jit(solution)/shard_map/ppermute | solution.py:355
  23.5 0.0 collective-permute-done.2.refs_2_
  23.5 0.1 blend_states.3
  23.6 1.6 %collective-permute-start.3 = (f32[16,2048]{1,0:T(8,128)S(1)}, f32[16,2048]{1,0:T(8,128)S(1)}, u32[]{:S(2)}, u32[]{:S(2)}) collective-permute-start(f32[16,2048]{1,0:T(8,128)S(1)} %get-tuple-element.28.refs_0_), channel_id=1, source_target_pairs={{0,16},{4,20},{8,24},{12,28},{16,0},{20,4},{24,8},{28,12},{1,17},{... | collective-permute-start | bytes 393224 | tf_op jit(solution)/shard_map/ppermute | solution.py:340
  25.2 0.8 %stack_rows.2 = bf16[1024,256]{1,0:T(8,128)(2,1)} custom-call(bf16[512,256]{1,0:T(8,128)(2,1)S(1)} %collective-permute-done.4.refs_0_.one_ref, bf16[512,256]{1,0:T(8,128)(2,1)S(1)} %relay.5.two_ref.refs_2_), custom_call_target="tpu_custom_call" | custom-call | tf_op jit(solution)/shard_map/stack_rows/pallas_call | solution.py:251
  26.0 0.5 collective-permute-start.13
  26.5 2.8 %collective-permute-done.3.refs_8_ = f32[16,2048]{1,0:T(8,128)S(1)} collective-permute-done((f32[16,2048]{1,0:T(8,128)S(1)}, f32[16,2048]{1,0:T(8,128)S(1)}, u32[]{:S(2)}, u32[]{:S(2)}) %collective-permute-start.3) | collective-permute-done | bytes 131104 | tf_op jit(solution)/shard_map/ppermute | solution.py:340
  29.3 0.0 copy-done
  29.3 0.0 copy-done.5
  29.3 1.7 %gate.1.mine_ref.gated_ref = bf16[128,2048]{1,0:T(8,128)(2,1)S(1)} custom-call(s32[1]{0:T(128)} %bitcast.which_ref.refs_0_.index_ref.nums_ref, bf16[128,2048]{1,0:T(8,128)(2,1)S(1)} %bitcast.8, f32[8,2048]{1,0:T(8,128)S(1)} %collective-permute-done.refs_2_, f32[3,3,2048]{2,1,0:T(4,128)S(1)} %copy-done.3, bf16[128,2048]{1,0:T(8,128)(2,1)S(1)} %get-tuple-element.21.refs_4_, ...), custom_call_target="tpu_custom_call" | custom-call | tf_op jit(solution)/shard_map/gate/pallas_call | solution.py:373
  31.0 0.1 collective-permute-start.9
  31.1 0.0 collective-permute-done.10.one_ref.refs_1_
  31.1 0.0 collective-permute-done.12.two_ref.refs_3_
  31.1 0.8 %stack_rows.3 = bf16[1024,256]{1,0:T(8,128)(2,1)} custom-call(bf16[512,256]{1,0:T(8,128)(2,1)S(1)} %collective-permute-done.10.one_ref.refs_1_, bf16[512,256]{1,0:T(8,128)(2,1)S(1)} %collective-permute-done.12.two_ref.refs_3_), custom_call_target="tpu_custom_call" | custom-call | tf_op jit(solution)/shard_map/stack_rows/pallas_call | solution.py:251
  32.0 1.8 %collective-permute-start.14 = (bf16[1024,256]{1,0:T(8,128)(2,1)}, bf16[1024,256]{1,0:T(8,128)(2,1)}, u32[]{:S(2)}, u32[]{:S(2)}) collective-permute-start(bf16[1024,256]{1,0:T(8,128)(2,1)} %stack_rows.3), channel_id=1, source_target_pairs={{0,16},{4,12},{8,24},{12,4},{16,0},{20,28},{24,8},{28,20},{1,17},{... | collective-permute-start | bytes 1572872 | tf_op jit(solution)/shard_map/ppermute | solution.py:403
  33.8 0.0 collective-permute-done.5.in_ref
  33.8 1.5 %collective-permute-start.6 = (bf16[512,256]{1,0:T(8,128)(2,1)S(1)}, bf16[512,256]{1,0:T(8,128)(2,1)S(1)}, u32[]{:S(2)}, u32[]{:S(2)}) collective-permute-start(bf16[512,256]{1,0:T(8,128)(2,1)S(1)} %relay.4.refs_0_), channel_id=1, source_target_pairs={{0,8},{4,20},{8,0},{12,28},{16,24},{20,4},{24,16},{28,12},{1,9},{5... | collective-permute-start | bytes 786440 | tf_op jit(solution)/shard_map/ppermute | solution.py:403
  35.2 0.0 collective-permute-start.7
  35.2 7.8 %collective-permute-done.6.refs_1_ = bf16[512,256]{1,0:T(8,128)(2,1)S(1)} collective-permute-done((bf16[512,256]{1,0:T(8,128)(2,1)S(1)}, bf16[512,256]{1,0:T(8,128)(2,1)S(1)}, u32[]{:S(2)}, u32[]{:S(2)}) %collective-permute-start.6) | collective-permute-done | bytes 262176 | tf_op jit(solution)/shard_map/ppermute | solution.py:403
  43.0 0.1 collective-permute-start.8
  43.1 0.0 collective-permute-done.13.refs_4_
  43.1 0.0 collective-permute-done.9.other_ref.gated_ref
  43.2 1.1 %collective-permute-done.14.refs_5_ = bf16[1024,256]{1,0:T(8,128)(2,1)} collective-permute-done((bf16[1024,256]{1,0:T(8,128)(2,1)}, bf16[1024,256]{1,0:T(8,128)(2,1)}, u32[]{:S(2)}, u32[]{:S(2)}) %collective-permute-start.14) | collective-permute-done | bytes 524320 | tf_op jit(solution)/shard_map/ppermute | solution.py:403
  44.3 2.8 %project_near.1.refs_4_ = f32[256,1024]{1,0:T(8,128)S(1)} custom-call(s32[1]{0:T(128)} %bitcast.which_ref.refs_0_.index_ref.nums_ref, s32[1]{0:T(128)} %bitcast.1.place_ref, bf16[128,2048]{1,0:T(8,128)(2,1)S(1)} %gate.1.mine_ref.gated_ref, bf16[128,2048]{1,0:T(8,128)(2,1)S(1)} %collective-permute-done.9.other_ref.gated_ref, bf16[512,2048]{1,0:T(8,128)(2,1)} %weight_ref.3, ...), custom_call_target="tpu_custom_call" | custom-call | tf_op jit(solution)/shard_map/project_near/pallas_call | solution.py:467
  47.1 0.0 collective-permute-done.7.refs_2_
  47.1 2.7 %collective-permute-done.8.refs_3_ = bf16[512,256]{1,0:T(8,128)(2,1)S(1)} collective-permute-done((bf16[512,256]{1,0:T(8,128)(2,1)S(1)}, bf16[512,256]{1,0:T(8,128)(2,1)S(1)}, u32[]{:S(2)}, u32[]{:S(2)}) %collective-permute-start.8) | collective-permute-done | bytes 262176 | tf_op jit(solution)/shard_map/ppermute | solution.py:403
  49.8 0.3 project_theirs.1
  50.1 0.1 collective-permute-start.15
  50.2 0.3 project_mine.1.mine_ref
  50.5 1.2 %collective-permute-done.15.other_ref = bf16[128,1024]{1,0:T(8,128)(2,1)S(1)} collective-permute-done((bf16[128,1024]{1,0:T(8,128)(2,1)S(1)}, bf16[128,1024]{1,0:T(8,128)(2,1)S(1)}, u32[]{:S(2)}, u32[]{:S(2)}) %collective-permute-start.15) | collective-permute-done | bytes 262176 | tf_op jit(solution)/shard_map/ppermute | solution.py:487
  51.7 0.8 %join_columns.1 = bf16[128,2048]{1,0:T(8,128)(2,1)} custom-call(s32[1]{0:T(128)} %bitcast.which_ref.refs_0_.index_ref.nums_ref, bf16[128,1024]{1,0:T(8,128)(2,1)S(1)} %project_mine.1.mine_ref, bf16[128,1024]{1,0:T(8,128)(2,1)S(1)} %collective-permute-done.15.other_ref), custom_call_target="tpu_custom_call" | custom-call | tf_op jit(solution)/shard_map/join_columns/pallas_call | solution.py:467
  (4 shorter events, 0.0 us)
Async XLA Ops:
  0.0 10.2 %copy-start.2 = (bf16[1,128,2048]{2,1,0:T(8,128)(2,1)S(1)}, bf16[1,128,2048]{2,1,0:T(8,128)(2,1)}, u32[]{:S(2)}) copy-start(bf16[1,128,2048]{2,1,0:T(8,128)(2,1)} %param.10) | copy-start | bytes 1572868
  0.0 10.2 %copy-start.1 = (bf16[1,128,2048]{2,1,0:T(8,128)(2,1)S(1)}, bf16[1,128,2048]{2,1,0:T(8,128)(2,1)}, u32[]{:S(2)}) copy-start(bf16[1,128,2048]{2,1,0:T(8,128)(2,1)} %param.9) | copy-start | bytes 1572868
  0.0 8.9 %copy-start.6 = (f32[128,16]{0,1:T(8,128)S(1)}, f32[128,16]{0,1:T(8,128)}, u32[]{:S(2)}) copy-start(f32[128,16]{0,1:T(8,128)} %param.12) | copy-start | bytes 24580
  0.0 9.0 %copy-start.7 = (f32[128,16]{0,1:T(8,128)S(1)}, f32[128,16]{0,1:T(8,128)}, u32[]{:S(2)}) copy-start(f32[128,16]{0,1:T(8,128)} %param.13) | copy-start | bytes 24580
  0.0 10.2 %copy-start.3 = (f32[3,3,2048]{2,1,0:T(4,128)S(1)}, f32[3,3,2048]{2,1,0:T(4,128)}, u32[]{:S(2)}) copy-start(f32[3,3,2048]{2,1,0:T(4,128)} %refs_3_.3) | copy-start | bytes 221188
  1.9 19.2 %copy-start.4 = (bf16[512,256]{1,0:T(8,128)(2,1)S(1)}, bf16[512,256]{1,0:T(8,128)(2,1)}, u32[]{:S(2)}) copy-start(bf16[512,256]{1,0:T(8,128)(2,1)} %get-tuple-element.30.in_ref) | copy-start | bytes 786436
  1.9 16.5 %collective-permute-start.4 = (bf16[512,256]{1,0:T(8,128)(2,1)}, bf16[512,256]{1,0:T(8,128)(2,1)S(1)}, u32[]{:S(2)}, u32[]{:S(2)}) collective-permute-start(bf16[512,256]{1,0:T(8,128)(2,1)} %get-tuple-element.30.in_ref), channel_id=1, source_target_pairs={{0,1},{1,0},{2,3},{3,2},{4,5},{5,4},{6,7},{7,6},{8,9},{9,8},{10,11... | collective-permute-start | bytes 786440 | tf_op jit(solution)/shard_map/ppermute | solution.py:506
  5.0 14.6 %collective-permute-start.11 = (bf16[512,256]{1,0:T(8,128)(2,1)}, bf16[512,256]{1,0:T(8,128)(2,1)S(1)}, u32[]{:S(2)}, u32[]{:S(2)}) collective-permute-start(bf16[512,256]{1,0:T(8,128)(2,1)} %get-tuple-element.30.in_ref), channel_id=1, source_target_pairs={{0,2},{1,3},{2,0},{3,1},{4,6},{5,7},{6,4},{7,5},{8,10},{9,11},{10,... | collective-permute-start | bytes 786440 | tf_op jit(solution)/shard_map/ppermute | solution.py:505
  7.6 2.6 %collective-permute-start = (f32[8,2048]{1,0:T(8,128)}, f32[8,2048]{1,0:T(8,128)S(1)}, u32[]{:S(2)}, u32[]{:S(2)}) collective-permute-start(f32[8,2048]{1,0:T(8,128)} %get-tuple-element.18), channel_id=1, source_target_pairs={{0,4},{4,8},{8,12},{12,16},{16,20},{20,24},{24,28},{1,5},{5,9},{9,... | collective-permute-start | bytes 196616 | tf_op jit(solution)/shard_map/ppermute | solution.py:504
  12.1 17.1 %copy-start = (bf16[1,128,2048]{2,1,0:T(8,128)(2,1)S(1)}, bf16[1,128,2048]{2,1,0:T(8,128)(2,1)}, u32[]{:S(2)}) copy-start(bf16[1,128,2048]{2,1,0:T(8,128)(2,1)} %param.8) | copy-start | bytes 1572868
  12.2 17.1 %copy-start.5 = (f32[2048]{0:T(1024)S(1)}, f32[2048]{0:T(1024)}, u32[]{:S(2)}) copy-start(f32[2048]{0:T(1024)} %param.14) | copy-start | bytes 24580
  12.2 3.6 %collective-permute-start.1 = (f32[16,2048]{1,0:T(8,128)S(1)}, f32[16,2048]{1,0:T(8,128)S(1)}, u32[]{:S(2)}, u32[]{:S(2)}) collective-permute-start(f32[16,2048]{1,0:T(8,128)S(1)} %get-tuple-element.24.refs_1_), channel_id=1, source_target_pairs={{0,4},{4,0},{8,12},{12,8},{16,20},{20,16},{24,28},{28,24},{1,5},{5... | collective-permute-start | bytes 393224 | tf_op jit(solution)/shard_map/ppermute | solution.py:340
  15.8 7.7 %collective-permute-start.2 = (f32[16,2048]{1,0:T(8,128)S(1)}, f32[16,2048]{1,0:T(8,128)S(1)}, u32[]{:S(2)}, u32[]{:S(2)}) collective-permute-start(f32[16,2048]{1,0:T(8,128)S(1)} %get-tuple-element.25.refs_1_.refs_0_), channel_id=1, source_target_pairs={{0,8},{4,12},{8,0},{12,4},{16,24},{20,28},{24,16},{28,20},{1,9},{5... | collective-permute-start | bytes 393224 | tf_op jit(solution)/shard_map/ppermute | solution.py:340
  18.4 12.7 %collective-permute-start.10 = (bf16[512,256]{1,0:T(8,128)(2,1)S(1)}, bf16[512,256]{1,0:T(8,128)(2,1)S(1)}, u32[]{:S(2)}, u32[]{:S(2)}) collective-permute-start(bf16[512,256]{1,0:T(8,128)(2,1)S(1)} %collective-permute-done.4.refs_0_.one_ref), channel_id=1, source_target_pairs={{0,8},{4,20},{8,0},{12,28},{16,24},{20,4},{24,16},{28,12},{1,9},{5... | collective-permute-start | bytes 786440 | tf_op jit(solution)/shard_map/ppermute | solution.py:403
  19.6 11.6 %collective-permute-start.12 = (bf16[512,256]{1,0:T(8,128)(2,1)S(1)}, bf16[512,256]{1,0:T(8,128)(2,1)S(1)}, u32[]{:S(2)}, u32[]{:S(2)}) collective-permute-start(bf16[512,256]{1,0:T(8,128)(2,1)S(1)} %relay.5.two_ref.refs_2_), channel_id=1, source_target_pairs={{0,8},{4,20},{8,0},{12,28},{16,24},{20,4},{24,16},{28,12},{1,9},{5... | collective-permute-start | bytes 786440 | tf_op jit(solution)/shard_map/ppermute | solution.py:403
  21.1 12.7 %collective-permute-start.5 = (bf16[512,256]{1,0:T(8,128)(2,1)S(1)}, bf16[512,256]{1,0:T(8,128)(2,1)S(1)}, u32[]{:S(2)}, u32[]{:S(2)}) collective-permute-start(bf16[512,256]{1,0:T(8,128)(2,1)S(1)} %relay.3), channel_id=1, source_target_pairs={{0,3},{1,2},{2,1},{3,0},{4,7},{5,6},{6,5},{7,4},{8,11},{9,10},{10,... | collective-permute-start | bytes 786440 | tf_op jit(solution)/shard_map/ppermute | solution.py:355
  23.6 5.7 %collective-permute-start.3 = (f32[16,2048]{1,0:T(8,128)S(1)}, f32[16,2048]{1,0:T(8,128)S(1)}, u32[]{:S(2)}, u32[]{:S(2)}) collective-permute-start(f32[16,2048]{1,0:T(8,128)S(1)} %get-tuple-element.28.refs_0_), channel_id=1, source_target_pairs={{0,16},{4,20},{8,24},{12,28},{16,0},{20,4},{24,8},{28,12},{1,17},{... | collective-permute-start | bytes 393224 | tf_op jit(solution)/shard_map/ppermute | solution.py:340
  26.0 17.1 %collective-permute-start.13 = (bf16[1024,256]{1,0:T(8,128)(2,1)}, bf16[1024,256]{1,0:T(8,128)(2,1)}, u32[]{:S(2)}, u32[]{:S(2)}) collective-permute-start(bf16[1024,256]{1,0:T(8,128)(2,1)} %stack_rows.2), channel_id=1, source_target_pairs={{0,16},{4,12},{8,24},{12,4},{16,0},{20,28},{24,8},{28,20},{1,17},{... | collective-permute-start | bytes 1572872 | tf_op jit(solution)/shard_map/ppermute | solution.py:403
  31.0 12.1 %collective-permute-start.9 = (bf16[128,2048]{1,0:T(8,128)(2,1)S(1)}, bf16[128,2048]{1,0:T(8,128)(2,1)S(1)}, u32[]{:S(2)}, u32[]{:S(2)}) collective-permute-start(bf16[128,2048]{1,0:T(8,128)(2,1)S(1)} %gate.1.mine_ref.gated_ref), channel_id=1, source_target_pairs={{0,4},{4,0},{8,12},{12,8},{16,20},{20,16},{24,28},{28,24},{1,5},{5... | collective-permute-start | bytes 1572872 | tf_op jit(solution)/shard_map/ppermute | solution.py:462
  32.0 12.3 %collective-permute-start.14 = (bf16[1024,256]{1,0:T(8,128)(2,1)}, bf16[1024,256]{1,0:T(8,128)(2,1)}, u32[]{:S(2)}, u32[]{:S(2)}) collective-permute-start(bf16[1024,256]{1,0:T(8,128)(2,1)} %stack_rows.3), channel_id=1, source_target_pairs={{0,16},{4,12},{8,24},{12,4},{16,0},{20,28},{24,8},{28,20},{1,17},{... | collective-permute-start | bytes 1572872 | tf_op jit(solution)/shard_map/ppermute | solution.py:403
  33.8 9.2 %collective-permute-start.6 = (bf16[512,256]{1,0:T(8,128)(2,1)S(1)}, bf16[512,256]{1,0:T(8,128)(2,1)S(1)}, u32[]{:S(2)}, u32[]{:S(2)}) collective-permute-start(bf16[512,256]{1,0:T(8,128)(2,1)S(1)} %relay.4.refs_0_), channel_id=1, source_target_pairs={{0,8},{4,20},{8,0},{12,28},{16,24},{20,4},{24,16},{28,12},{1,9},{5... | collective-permute-start | bytes 786440 | tf_op jit(solution)/shard_map/ppermute | solution.py:403
  35.2 11.9 %collective-permute-start.7 = (bf16[512,256]{1,0:T(8,128)(2,1)S(1)}, bf16[512,256]{1,0:T(8,128)(2,1)S(1)}, u32[]{:S(2)}, u32[]{:S(2)}) collective-permute-start(bf16[512,256]{1,0:T(8,128)(2,1)S(1)} %relay.4.refs_0_), channel_id=1, source_target_pairs={{0,16},{4,12},{8,24},{12,4},{16,0},{20,28},{24,8},{28,20},{1,17},{... | collective-permute-start | bytes 786440 | tf_op jit(solution)/shard_map/ppermute | solution.py:403
  43.0 6.8 %collective-permute-start.8 = (bf16[512,256]{1,0:T(8,128)(2,1)S(1)}, bf16[512,256]{1,0:T(8,128)(2,1)S(1)}, u32[]{:S(2)}, u32[]{:S(2)}) collective-permute-start(bf16[512,256]{1,0:T(8,128)(2,1)S(1)} %collective-permute-done.6.refs_1_), channel_id=1, source_target_pairs={{0,16},{4,12},{8,24},{12,4},{16,0},{20,28},{24,8},{28,20},{1,17},{... | collective-permute-start | bytes 786440 | tf_op jit(solution)/shard_map/ppermute | solution.py:403
  50.1 1.6 %collective-permute-start.15 = (bf16[128,1024]{1,0:T(8,128)(2,1)S(1)}, bf16[128,1024]{1,0:T(8,128)(2,1)S(1)}, u32[]{:S(2)}, u32[]{:S(2)}) collective-permute-start(bf16[128,1024]{1,0:T(8,128)(2,1)S(1)} %project_theirs.1), channel_id=1, source_target_pairs={{0,4},{4,0},{8,12},{12,8},{16,20},{20,16},{24,28},{28,24},{1,5},{5... | collective-permute-start | bytes 786440 | tf_op jit(solution)/shard_map/ppermute | solution.py:487

commit v8 on v7

--- a/solution.py
+++ b/solution.py
@@ -11,7 +11,7 @@
 HOLD = [[], [], [], []]
 RELAY = {'z1': [], 'a1': [], 'mine': ['z1'], 'z2': ['s1'], 'z3': ['s2'], 'a3': []}
 FEAT = 3
-WIDE = 1024
+WIDE = 2048
 LANES = 128
 SUB = 32
 VMEM_LIMIT = 48 << 20

time: 52.7 us -> 52.4 us (level)
  Pallas kernels: 12.7 us -> 11.9 us
    ppermute x7, waiting for transfers between devices: 11.6 us -> 12.2 us  [hop(): lax.ppermute(x, 'ctx', [(i, i ^ (odd if i % 2 else even)) for i in range(...]
  transfers between devices with their start and end apart: 16 -> 16, of which waited for: 7 -> 7; matrix products, arithmetic and copies ran while one was open for 0% -> 0% of each run, Pallas kernels for 18% -> 17%
where the time goes in v8:
time: 52.4 us; the launch traced here: 52.2 us
  starting transfers between devices  22.2 us (42%)
  waiting for transfers between devices  17.6 us (34%)
  Pallas kernels  11.9 us (23%)
    ppermute x7, waiting for transfers between devices, hop(): lax.ppermute(x, 'ctx', [(i, i ^ (odd if i % 2 else even)) for i in range(...  12.2 us
    ppermute x3, starting transfers between devices, conv_path(): other = lax.ppermute(state, 'ctx', [(i, i ^ step) for i in range(count)])  6.73 us
    ppermute x7, starting transfers between devices, hop(): lax.ppermute(x, 'ctx', [(i, i ^ (odd if i % 2 else even)) for i in range(...  5.95 us
    pallas_call x4, Pallas kernels, call(): pl.pallas_call(kernel, in_specs=[smem] * len(scalars) + [vmem] * len(args...  4.29 us
    ppermute x3, waiting for transfers between devices, conv_path(): other = lax.ppermute(state, 'ctx', [(i, i ^ step) for i in range(count)])  3.31 us
    ppermute x1, starting transfers between devices, local(): near = lax.ppermute(mine, 'fsdp', [(i, i ^ 1) for i in range(4)])  3.1 us
    ppermute x1, starting transfers between devices, local(): two = lax.ppermute(mine, 'fsdp', [(i, i ^ 2) for i in range(4)])  2.59 us
    ppermute x1, starting transfers between devices, conv_path(): lax.ppermute(at(mine, 'mine'), 'fsdp', [(i, i ^ 3) for i in range(4)])  2.45 us
  transfers between devices with their start and end apart: 16, of which 7 were waited for; matrix products, arithmetic and copies ran while one was open for 0% of the time, Pallas kernels for 17%

profile of v8, /device:TPU:0, one launch (start us, length us, event | category | flops | bytes accessed | tf_op | source)
XLA Modules:
  0.0 52.2 jit_solution(6428131063415667525)
XLA Ops:
  0.0 0.0 copy-start.2
  0.0 0.0 copy-start.1
  0.0 0.0 copy-start.6
  0.0 0.0 copy-start.7
  0.0 0.0 copy-start.3
  0.0 1.9 %prepare.1 = (f32[8,2048]{1,0:T(8,128)}, bf16[512,256]{1,0:T(8,128)(2,1)}) custom-call(s32[1]{0:T(128)} %bitcast.which_ref.refs_0_.index_ref.nums_ref, bf16[128,2048]{1,0:T(8,128)(2,1)} %bitcast.7, bf16[128,2048]{1,0:T(8,128)(2,1)} %bitcast.9, bf16[128,2048]{1,0:T(8,128)(2,1)} %bitcast.11, bf16[512,2048]{1,0:T(8,128)(2,1)} %weight_ref.3), custom_call_target="tpu_custom_call" | custom-call | tf_op jit(solution)/shard_map/prepare/pallas_call | solution.py:228
  1.9 0.0 copy-start.4
  1.9 3.1 %collective-permute-start.4 = (bf16[512,256]{1,0:T(8,128)(2,1)}, bf16[512,256]{1,0:T(8,128)(2,1)S(1)}, u32[]{:S(2)}, u32[]{:S(2)}) collective-permute-start(bf16[512,256]{1,0:T(8,128)(2,1)} %get-tuple-element.30.in_ref), channel_id=1, source_target_pairs={{0,1},{1,0},{2,3},{3,2},{4,5},{5,4},{6,7},{7,6},{8,9},{9,8},{10,11... | collective-permute-start | bytes 786440 | tf_op jit(solution)/shard_map/ppermute | solution.py:506
  5.0 2.6 %collective-permute-start.11 = (bf16[512,256]{1,0:T(8,128)(2,1)}, bf16[512,256]{1,0:T(8,128)(2,1)S(1)}, u32[]{:S(2)}, u32[]{:S(2)}) collective-permute-start(bf16[512,256]{1,0:T(8,128)(2,1)} %get-tuple-element.30.in_ref), channel_id=1, source_target_pairs={{0,2},{1,3},{2,0},{3,1},{4,6},{5,7},{6,4},{7,5},{8,10},{9,11},{10,... | collective-permute-start | bytes 786440 | tf_op jit(solution)/shard_map/ppermute | solution.py:505
  7.6 1.3 %collective-permute-start = (f32[8,2048]{1,0:T(8,128)}, f32[8,2048]{1,0:T(8,128)S(1)}, u32[]{:S(2)}, u32[]{:S(2)}) collective-permute-start(f32[8,2048]{1,0:T(8,128)} %get-tuple-element.18), channel_id=1, source_target_pairs={{0,4},{4,8},{8,12},{12,16},{16,20},{20,24},{24,28},{1,5},{5,9},{9,... | collective-permute-start | bytes 196616 | tf_op jit(solution)/shard_map/ppermute | solution.py:504
  8.9 0.0 copy-done.6
  8.9 0.1 copy.12.rate_ref
  9.0 0.0 copy-done.7
  9.0 0.1 copy.13.residue_ref
  9.1 1.1 %tables.1 = (bf16[16,96,256]{2,1,0:T(8,128)(2,1)S(1)}, bf16[16,64,256]{2,1,0:T(8,128)(2,1)S(1)}, f32[16,2048]{1,0:T(8,128)S(1)}) custom-call(f32[128,16]{1,0:T(8,128)S(1)} %copy.12.rate_ref, f32[128,16]{1,0:T(8,128)S(1)} %copy.13.residue_ref), custom_call_target="tpu_custom_call" | custom-call | tf_op jit(solution)/shard_map/tables/pallas_call | solution.py:292
  10.2 0.0 collective-permute-done.refs_2_
  10.2 0.0 copy-done.2
  10.2 0.0 copy-done.1
  10.2 0.0 copy-done.3
  10.2 1.5 %kv_and_state.1 = (bf16[128,2048]{1,0:T(8,128)(2,1)S(1)}, f32[128,2048]{1,0:T(8,128)S(1)}, f32[64,2048]{1,0:T(8,128)S(1)}, f32[16,2048]{1,0:T(8,128)S(1)}) custom-call(bf16[128,2048]{1,0:T(8,128)(2,1)S(1)} %bitcast.10, bf16[128,2048]{1,0:T(8,128)(2,1)S(1)} %bitcast.12, f32[8,2048]{1,0:T(8,128)S(1)} %collective-permute-done.refs_2_, ...), custom_call_target="tpu_custom_call" | custom-call | tf_op jit(solution)/shard_map/kv_and_state/pallas_call | solution.py:317
  11.7 0.0 copy-start
  11.7 0.0 copy-start.5
  11.7 2.6 %collective-permute-start.1 = (f32[16,2048]{1,0:T(8,128)S(1)}, f32[16,2048]{1,0:T(8,128)S(1)}, u32[]{:S(2)}, u32[]{:S(2)}) collective-permute-start(f32[16,2048]{1,0:T(8,128)S(1)} %get-tuple-element.24.refs_1_), channel_id=1, source_target_pairs={{0,4},{4,0},{8,12},{12,8},{16,20},{20,16},{24,28},{28,24},{1,5},{5... | collective-permute-start | bytes 393224 | tf_op jit(solution)/shard_map/ppermute | solution.py:340
  14.3 1.0 %collective-permute-done.1.refs_2_ = f32[16,2048]{1,0:T(8,128)S(1)} collective-permute-done((f32[16,2048]{1,0:T(8,128)S(1)}, f32[16,2048]{1,0:T(8,128)S(1)}, u32[]{:S(2)}, u32[]{:S(2)}) %collective-permute-start.1) | collective-permute-done | bytes 131104 | tf_op jit(solution)/shard_map/ppermute | solution.py:340
  15.3 0.1 blend_states.2
  15.4 2.6 %collective-permute-start.2 = (f32[16,2048]{1,0:T(8,128)S(1)}, f32[16,2048]{1,0:T(8,128)S(1)}, u32[]{:S(2)}, u32[]{:S(2)}) collective-permute-start(f32[16,2048]{1,0:T(8,128)S(1)} %get-tuple-element.25.refs_1_.refs_0_), channel_id=1, source_target_pairs={{0,8},{4,12},{8,0},{12,4},{16,24},{20,28},{24,16},{28,20},{1,9},{5... | collective-permute-start | bytes 393224 | tf_op jit(solution)/shard_map/ppermute | solution.py:340
  17.9 0.0 collective-permute-done.4.refs_0_.one_ref
  17.9 0.7 %collective-permute-start.10 = (bf16[512,256]{1,0:T(8,128)(2,1)S(1)}, bf16[512,256]{1,0:T(8,128)(2,1)S(1)}, u32[]{:S(2)}, u32[]{:S(2)}) collective-permute-start(bf16[512,256]{1,0:T(8,128)(2,1)S(1)} %collective-permute-done.4.refs_0_.one_ref), channel_id=1, source_target_pairs={{0,8},{4,20},{8,0},{12,28},{16,24},{20,4},{24,16},{28,12},{1,9},{5... | collective-permute-start | bytes 786440 | tf_op jit(solution)/shard_map/ppermute | solution.py:403
  18.7 0.9 %collective-permute-done.11.in_ref = bf16[512,256]{1,0:T(8,128)(2,1)S(1)} collective-permute-done((bf16[512,256]{1,0:T(8,128)(2,1)}, bf16[512,256]{1,0:T(8,128)(2,1)S(1)}, u32[]{:S(2)}, u32[]{:S(2)}) %collective-permute-start.11) | collective-permute-done | bytes 262176 | tf_op jit(solution)/shard_map/ppermute | solution.py:505
  19.6 1.5 %collective-permute-start.12 = (bf16[512,256]{1,0:T(8,128)(2,1)S(1)}, bf16[512,256]{1,0:T(8,128)(2,1)S(1)}, u32[]{:S(2)}, u32[]{:S(2)}) collective-permute-start(bf16[512,256]{1,0:T(8,128)(2,1)S(1)} %relay.5.two_ref.refs_2_), channel_id=1, source_target_pairs={{0,8},{4,20},{8,0},{12,28},{16,24},{20,4},{24,16},{28,12},{1,9},{5... | collective-permute-start | bytes 786440 | tf_op jit(solution)/shard_map/ppermute | solution.py:403
  21.0 0.0 copy-done.4
  21.1 2.5 %collective-permute-start.5 = (bf16[512,256]{1,0:T(8,128)(2,1)S(1)}, bf16[512,256]{1,0:T(8,128)(2,1)S(1)}, u32[]{:S(2)}, u32[]{:S(2)}) collective-permute-start(bf16[512,256]{1,0:T(8,128)(2,1)S(1)} %relay.3), channel_id=1, source_target_pairs={{0,3},{1,2},{2,1},{3,0},{4,7},{5,6},{6,5},{7,4},{8,11},{9,10},{10,... | collective-permute-start | bytes 786440 | tf_op jit(solution)/shard_map/ppermute | solution.py:355
  23.5 0.0 collective-permute-done.2.refs_2_
  23.5 0.1 blend_states.3
  23.6 1.6 %collective-permute-start.3 = (f32[16,2048]{1,0:T(8,128)S(1)}, f32[16,2048]{1,0:T(8,128)S(1)}, u32[]{:S(2)}, u32[]{:S(2)}) collective-permute-start(f32[16,2048]{1,0:T(8,128)S(1)} %get-tuple-element.28.refs_0_), channel_id=1, source_target_pairs={{0,16},{4,20},{8,24},{12,28},{16,0},{20,4},{24,8},{28,12},{1,17},{... | collective-permute-start | bytes 393224 | tf_op jit(solution)/shard_map/ppermute | solution.py:340
  25.2 0.8 %stack_rows.2 = bf16[1024,256]{1,0:T(8,128)(2,1)} custom-call(bf16[512,256]{1,0:T(8,128)(2,1)S(1)} %collective-permute-done.4.refs_0_.one_ref, bf16[512,256]{1,0:T(8,128)(2,1)S(1)} %relay.5.two_ref.refs_2_), custom_call_target="tpu_custom_call" | custom-call | tf_op jit(solution)/shard_map/stack_rows/pallas_call | solution.py:251
  26.0 0.5 collective-permute-start.13
  26.5 2.3 %collective-permute-done.3.refs_8_ = f32[16,2048]{1,0:T(8,128)S(1)} collective-permute-done((f32[16,2048]{1,0:T(8,128)S(1)}, f32[16,2048]{1,0:T(8,128)S(1)}, u32[]{:S(2)}, u32[]{:S(2)}) %collective-permute-start.3) | collective-permute-done | bytes 131104 | tf_op jit(solution)/shard_map/ppermute | solution.py:340
  28.8 0.0 copy-done
  28.8 0.0 copy-done.5
  28.8 1.4 %gate.1.mine_ref.gated_ref = bf16[128,2048]{1,0:T(8,128)(2,1)S(1)} custom-call(s32[1]{0:T(128)} %bitcast.which_ref.refs_0_.index_ref.nums_ref, bf16[128,2048]{1,0:T(8,128)(2,1)S(1)} %bitcast.8, f32[8,2048]{1,0:T(8,128)S(1)} %collective-permute-done.refs_2_, f32[3,3,2048]{2,1,0:T(4,128)S(1)} %copy-done.3, bf16[128,2048]{1,0:T(8,128)(2,1)S(1)} %get-tuple-element.21.refs_4_, ...), custom_call_target="tpu_custom_call" | custom-call | tf_op jit(solution)/shard_map/gate/pallas_call | solution.py:373
  30.3 0.1 collective-permute-start.9
  30.3 0.0 collective-permute-done.10.one_ref.refs_1_
  30.4 0.0 collective-permute-done.12.two_ref.refs_3_
  30.4 0.8 %stack_rows.3 = bf16[1024,256]{1,0:T(8,128)(2,1)} custom-call(bf16[512,256]{1,0:T(8,128)(2,1)S(1)} %collective-permute-done.10.one_ref.refs_1_, bf16[512,256]{1,0:T(8,128)(2,1)S(1)} %collective-permute-done.12.two_ref.refs_3_), custom_call_target="tpu_custom_call" | custom-call | tf_op jit(solution)/shard_map/stack_rows/pallas_call | solution.py:251
  31.2 2.1 %collective-permute-start.14 = (bf16[1024,256]{1,0:T(8,128)(2,1)}, bf16[1024,256]{1,0:T(8,128)(2,1)}, u32[]{:S(2)}, u32[]{:S(2)}) collective-permute-start(bf16[1024,256]{1,0:T(8,128)(2,1)} %stack_rows.3), channel_id=1, source_target_pairs={{0,16},{4,12},{8,24},{12,4},{16,0},{20,28},{24,8},{28,20},{1,17},{... | collective-permute-start | bytes 1572872 | tf_op jit(solution)/shard_map/ppermute | solution.py:403
  33.3 0.0 collective-permute-done.5.in_ref
  33.3 0.8 %collective-permute-start.6 = (bf16[512,256]{1,0:T(8,128)(2,1)S(1)}, bf16[512,256]{1,0:T(8,128)(2,1)S(1)}, u32[]{:S(2)}, u32[]{:S(2)}) collective-permute-start(bf16[512,256]{1,0:T(8,128)(2,1)S(1)} %relay.4.refs_0_), channel_id=1, source_target_pairs={{0,8},{4,20},{8,0},{12,28},{16,24},{20,4},{24,16},{28,12},{1,9},{5... | collective-permute-start | bytes 786440 | tf_op jit(solution)/shard_map/ppermute | solution.py:403
  34.2 0.3 collective-permute-start.7
  34.4 8.1 %collective-permute-done.6.refs_1_ = bf16[512,256]{1,0:T(8,128)(2,1)S(1)} collective-permute-done((bf16[512,256]{1,0:T(8,128)(2,1)S(1)}, bf16[512,256]{1,0:T(8,128)(2,1)S(1)}, u32[]{:S(2)}, u32[]{:S(2)}) %collective-permute-start.6) | collective-permute-done | bytes 262176 | tf_op jit(solution)/shard_map/ppermute | solution.py:403
  42.6 0.0 collective-permute-start.8
  42.6 0.0 collective-permute-done.13.refs_4_
  42.6 0.0 collective-permute-done.9.other_ref.gated_ref
  42.6 1.4 %collective-permute-done.14.refs_5_ = bf16[1024,256]{1,0:T(8,128)(2,1)} collective-permute-done((bf16[1024,256]{1,0:T(8,128)(2,1)}, bf16[1024,256]{1,0:T(8,128)(2,1)}, u32[]{:S(2)}, u32[]{:S(2)}) %collective-permute-start.14) | collective-permute-done | bytes 524320 | tf_op jit(solution)/shard_map/ppermute | solution.py:403
  43.9 2.8 %project_near.1.refs_4_ = f32[256,1024]{1,0:T(8,128)S(1)} custom-call(s32[1]{0:T(128)} %bitcast.which_ref.refs_0_.index_ref.nums_ref, s32[1]{0:T(128)} %bitcast.1.place_ref, bf16[128,2048]{1,0:T(8,128)(2,1)S(1)} %gate.1.mine_ref.gated_ref, bf16[128,2048]{1,0:T(8,128)(2,1)S(1)} %collective-permute-done.9.other_ref.gated_ref, bf16[512,2048]{1,0:T(8,128)(2,1)} %weight_ref.3, ...), custom_call_target="tpu_custom_call" | custom-call | tf_op jit(solution)/shard_map/project_near/pallas_call | solution.py:467
  46.7 0.0 collective-permute-done.7.refs_2_
  46.8 2.7 %collective-permute-done.8.refs_3_ = bf16[512,256]{1,0:T(8,128)(2,1)S(1)} collective-permute-done((bf16[512,256]{1,0:T(8,128)(2,1)S(1)}, bf16[512,256]{1,0:T(8,128)(2,1)S(1)}, u32[]{:S(2)}, u32[]{:S(2)}) %collective-permute-start.8) | collective-permute-done | bytes 262176 | tf_op jit(solution)/shard_map/ppermute | solution.py:403
  49.4 0.3 project_theirs.1
  49.8 0.1 collective-permute-start.15
  49.8 0.3 project_mine.1.mine_ref
  50.2 1.2 %collective-permute-done.15.other_ref = bf16[128,1024]{1,0:T(8,128)(2,1)S(1)} collective-permute-done((bf16[128,1024]{1,0:T(8,128)(2,1)S(1)}, bf16[128,1024]{1,0:T(8,128)(2,1)S(1)}, u32[]{:S(2)}, u32[]{:S(2)}) %collective-permute-start.15) | collective-permute-done | bytes 262176 | tf_op jit(solution)/shard_map/ppermute | solution.py:487
  51.4 0.8 %join_columns.1 = bf16[128,2048]{1,0:T(8,128)(2,1)} custom-call(s32[1]{0:T(128)} %bitcast.which_ref.refs_0_.index_ref.nums_ref, bf16[128,1024]{1,0:T(8,128)(2,1)S(1)} %project_mine.1.mine_ref, bf16[128,1024]{1,0:T(8,128)(2,1)S(1)} %collective-permute-done.15.other_ref), custom_call_target="tpu_custom_call" | custom-call | tf_op jit(solution)/shard_map/join_columns/pallas_call | solution.py:467
  (4 shorter events, 0.0 us)
Async XLA Ops:
  0.0 10.2 %copy-start.2 = (bf16[1,128,2048]{2,1,0:T(8,128)(2,1)S(1)}, bf16[1,128,2048]{2,1,0:T(8,128)(2,1)}, u32[]{:S(2)}) copy-start(bf16[1,128,2048]{2,1,0:T(8,128)(2,1)} %param.10) | copy-start | bytes 1572868
  0.0 10.2 %copy-start.1 = (bf16[1,128,2048]{2,1,0:T(8,128)(2,1)S(1)}, bf16[1,128,2048]{2,1,0:T(8,128)(2,1)}, u32[]{:S(2)}) copy-start(bf16[1,128,2048]{2,1,0:T(8,128)(2,1)} %param.9) | copy-start | bytes 1572868
  0.0 8.9 %copy-start.6 = (f32[128,16]{0,1:T(8,128)S(1)}, f32[128,16]{0,1:T(8,128)}, u32[]{:S(2)}) copy-start(f32[128,16]{0,1:T(8,128)} %param.12) | copy-start | bytes 24580
  0.0 9.0 %copy-start.7 = (f32[128,16]{0,1:T(8,128)S(1)}, f32[128,16]{0,1:T(8,128)}, u32[]{:S(2)}) copy-start(f32[128,16]{0,1:T(8,128)} %param.13) | copy-start | bytes 24580
  0.0 10.2 %copy-start.3 = (f32[3,3,2048]{2,1,0:T(4,128)S(1)}, f32[3,3,2048]{2,1,0:T(4,128)}, u32[]{:S(2)}) copy-start(f32[3,3,2048]{2,1,0:T(4,128)} %refs_3_.3) | copy-start | bytes 221188
  1.9 19.2 %copy-start.4 = (bf16[512,256]{1,0:T(8,128)(2,1)S(1)}, bf16[512,256]{1,0:T(8,128)(2,1)}, u32[]{:S(2)}) copy-start(bf16[512,256]{1,0:T(8,128)(2,1)} %get-tuple-element.30.in_ref) | copy-start | bytes 786436
  1.9 16.1 %collective-permute-start.4 = (bf16[512,256]{1,0:T(8,128)(2,1)}, bf16[512,256]{1,0:T(8,128)(2,1)S(1)}, u32[]{:S(2)}, u32[]{:S(2)}) collective-permute-start(bf16[512,256]{1,0:T(8,128)(2,1)} %get-tuple-element.30.in_ref), channel_id=1, source_target_pairs={{0,1},{1,0},{2,3},{3,2},{4,5},{5,4},{6,7},{7,6},{8,9},{9,8},{10,11... | collective-permute-start | bytes 786440 | tf_op jit(solution)/shard_map/ppermute | solution.py:506
  5.0 14.6 %collective-permute-start.11 = (bf16[512,256]{1,0:T(8,128)(2,1)}, bf16[512,256]{1,0:T(8,128)(2,1)S(1)}, u32[]{:S(2)}, u32[]{:S(2)}) collective-permute-start(bf16[512,256]{1,0:T(8,128)(2,1)} %get-tuple-element.30.in_ref), channel_id=1, source_target_pairs={{0,2},{1,3},{2,0},{3,1},{4,6},{5,7},{6,4},{7,5},{8,10},{9,11},{10,... | collective-permute-start | bytes 786440 | tf_op jit(solution)/shard_map/ppermute | solution.py:505
  7.6 2.6 %collective-permute-start = (f32[8,2048]{1,0:T(8,128)}, f32[8,2048]{1,0:T(8,128)S(1)}, u32[]{:S(2)}, u32[]{:S(2)}) collective-permute-start(f32[8,2048]{1,0:T(8,128)} %get-tuple-element.18), channel_id=1, source_target_pairs={{0,4},{4,8},{8,12},{12,16},{16,20},{20,24},{24,28},{1,5},{5,9},{9,... | collective-permute-start | bytes 196616 | tf_op jit(solution)/shard_map/ppermute | solution.py:504
  11.7 17.1 %copy-start = (bf16[1,128,2048]{2,1,0:T(8,128)(2,1)S(1)}, bf16[1,128,2048]{2,1,0:T(8,128)(2,1)}, u32[]{:S(2)}) copy-start(bf16[1,128,2048]{2,1,0:T(8,128)(2,1)} %param.8) | copy-start | bytes 1572868
  11.7 17.1 %copy-start.5 = (f32[2048]{0:T(1024)S(1)}, f32[2048]{0:T(1024)}, u32[]{:S(2)}) copy-start(f32[2048]{0:T(1024)} %param.14) | copy-start | bytes 24580
  11.7 3.6 %collective-permute-start.1 = (f32[16,2048]{1,0:T(8,128)S(1)}, f32[16,2048]{1,0:T(8,128)S(1)}, u32[]{:S(2)}, u32[]{:S(2)}) collective-permute-start(f32[16,2048]{1,0:T(8,128)S(1)} %get-tuple-element.24.refs_1_), channel_id=1, source_target_pairs={{0,4},{4,0},{8,12},{12,8},{16,20},{20,16},{24,28},{28,24},{1,5},{5... | collective-permute-start | bytes 393224 | tf_op jit(solution)/shard_map/ppermute | solution.py:340
  15.4 8.1 %collective-permute-start.2 = (f32[16,2048]{1,0:T(8,128)S(1)}, f32[16,2048]{1,0:T(8,128)S(1)}, u32[]{:S(2)}, u32[]{:S(2)}) collective-permute-start(f32[16,2048]{1,0:T(8,128)S(1)} %get-tuple-element.25.refs_1_.refs_0_), channel_id=1, source_target_pairs={{0,8},{4,12},{8,0},{12,4},{16,24},{20,28},{24,16},{28,20},{1,9},{5... | collective-permute-start | bytes 393224 | tf_op jit(solution)/shard_map/ppermute | solution.py:340
  17.9 12.4 %collective-permute-start.10 = (bf16[512,256]{1,0:T(8,128)(2,1)S(1)}, bf16[512,256]{1,0:T(8,128)(2,1)S(1)}, u32[]{:S(2)}, u32[]{:S(2)}) collective-permute-start(bf16[512,256]{1,0:T(8,128)(2,1)S(1)} %collective-permute-done.4.refs_0_.one_ref), channel_id=1, source_target_pairs={{0,8},{4,20},{8,0},{12,28},{16,24},{20,4},{24,16},{28,12},{1,9},{5... | collective-permute-start | bytes 786440 | tf_op jit(solution)/shard_map/ppermute | solution.py:403
  19.6 10.8 %collective-permute-start.12 = (bf16[512,256]{1,0:T(8,128)(2,1)S(1)}, bf16[512,256]{1,0:T(8,128)(2,1)S(1)}, u32[]{:S(2)}, u32[]{:S(2)}) collective-permute-start(bf16[512,256]{1,0:T(8,128)(2,1)S(1)} %relay.5.two_ref.refs_2_), channel_id=1, source_target_pairs={{0,8},{4,20},{8,0},{12,28},{16,24},{20,4},{24,16},{28,12},{1,9},{5... | collective-permute-start | bytes 786440 | tf_op jit(solution)/shard_map/ppermute | solution.py:403
  21.1 12.3 %collective-permute-start.5 = (bf16[512,256]{1,0:T(8,128)(2,1)S(1)}, bf16[512,256]{1,0:T(8,128)(2,1)S(1)}, u32[]{:S(2)}, u32[]{:S(2)}) collective-permute-start(bf16[512,256]{1,0:T(8,128)(2,1)S(1)} %relay.3), channel_id=1, source_target_pairs={{0,3},{1,2},{2,1},{3,0},{4,7},{5,6},{6,5},{7,4},{8,11},{9,10},{10,... | collective-permute-start | bytes 786440 | tf_op jit(solution)/shard_map/ppermute | solution.py:355
  23.6 5.2 %collective-permute-start.3 = (f32[16,2048]{1,0:T(8,128)S(1)}, f32[16,2048]{1,0:T(8,128)S(1)}, u32[]{:S(2)}, u32[]{:S(2)}) collective-permute-start(f32[16,2048]{1,0:T(8,128)S(1)} %get-tuple-element.28.refs_0_), channel_id=1, source_target_pairs={{0,16},{4,20},{8,24},{12,28},{16,0},{20,4},{24,8},{28,12},{1,17},{... | collective-permute-start | bytes 393224 | tf_op jit(solution)/shard_map/ppermute | solution.py:340
  26.0 16.6 %collective-permute-start.13 = (bf16[1024,256]{1,0:T(8,128)(2,1)}, bf16[1024,256]{1,0:T(8,128)(2,1)}, u32[]{:S(2)}, u32[]{:S(2)}) collective-permute-start(bf16[1024,256]{1,0:T(8,128)(2,1)} %stack_rows.2), channel_id=1, source_target_pairs={{0,16},{4,12},{8,24},{12,4},{16,0},{20,28},{24,8},{28,20},{1,17},{... | collective-permute-start | bytes 1572872 | tf_op jit(solution)/shard_map/ppermute | solution.py:403
  30.3 12.3 %collective-permute-start.9 = (bf16[128,2048]{1,0:T(8,128)(2,1)S(1)}, bf16[128,2048]{1,0:T(8,128)(2,1)S(1)}, u32[]{:S(2)}, u32[]{:S(2)}) collective-permute-start(bf16[128,2048]{1,0:T(8,128)(2,1)S(1)} %gate.1.mine_ref.gated_ref), channel_id=1, source_target_pairs={{0,4},{4,0},{8,12},{12,8},{16,20},{20,16},{24,28},{28,24},{1,5},{5... | collective-permute-start | bytes 1572872 | tf_op jit(solution)/shard_map/ppermute | solution.py:462
  31.2 12.7 %collective-permute-start.14 = (bf16[1024,256]{1,0:T(8,128)(2,1)}, bf16[1024,256]{1,0:T(8,128)(2,1)}, u32[]{:S(2)}, u32[]{:S(2)}) collective-permute-start(bf16[1024,256]{1,0:T(8,128)(2,1)} %stack_rows.3), channel_id=1, source_target_pairs={{0,16},{4,12},{8,24},{12,4},{16,0},{20,28},{24,8},{28,20},{1,17},{... | collective-permute-start | bytes 1572872 | tf_op jit(solution)/shard_map/ppermute | solution.py:403
  33.3 9.2 %collective-permute-start.6 = (bf16[512,256]{1,0:T(8,128)(2,1)S(1)}, bf16[512,256]{1,0:T(8,128)(2,1)S(1)}, u32[]{:S(2)}, u32[]{:S(2)}) collective-permute-start(bf16[512,256]{1,0:T(8,128)(2,1)S(1)} %relay.4.refs_0_), channel_id=1, source_target_pairs={{0,8},{4,20},{8,0},{12,28},{16,24},{20,4},{24,16},{28,12},{1,9},{5... | collective-permute-start | bytes 786440 | tf_op jit(solution)/shard_map/ppermute | solution.py:403
  34.2 12.6 %collective-permute-start.7 = (bf16[512,256]{1,0:T(8,128)(2,1)S(1)}, bf16[512,256]{1,0:T(8,128)(2,1)S(1)}, u32[]{:S(2)}, u32[]{:S(2)}) collective-permute-start(bf16[512,256]{1,0:T(8,128)(2,1)S(1)} %relay.4.refs_0_), channel_id=1, source_target_pairs={{0,16},{4,12},{8,24},{12,4},{16,0},{20,28},{24,8},{28,20},{1,17},{... | collective-permute-start | bytes 786440 | tf_op jit(solution)/shard_map/ppermute | solution.py:403
  42.6 6.9 %collective-permute-start.8 = (bf16[512,256]{1,0:T(8,128)(2,1)S(1)}, bf16[512,256]{1,0:T(8,128)(2,1)S(1)}, u32[]{:S(2)}, u32[]{:S(2)}) collective-permute-start(bf16[512,256]{1,0:T(8,128)(2,1)S(1)} %collective-permute-done.6.refs_1_), channel_id=1, source_target_pairs={{0,16},{4,12},{8,24},{12,4},{16,0},{20,28},{24,8},{28,20},{1,17},{... | collective-permute-start | bytes 786440 | tf_op jit(solution)/shard_map/ppermute | solution.py:403
  49.8 1.6 %collective-permute-start.15 = (bf16[128,1024]{1,0:T(8,128)(2,1)S(1)}, bf16[128,1024]{1,0:T(8,128)(2,1)S(1)}, u32[]{:S(2)}, u32[]{:S(2)}) collective-permute-start(bf16[128,1024]{1,0:T(8,128)(2,1)S(1)} %project_theirs.1), channel_id=1, source_target_pairs={{0,4},{4,0},{8,12},{12,8},{16,20},{20,16},{24,28},{28,24},{1,5},{5... | collective-permute-start | bytes 786440 | tf_op jit(solution)/shard_map/ppermute | solution.py:487
